TPU v7x, 256 devices: a whole 4x4x8 slice. The times are simulated.
256 devices in a mesh: cluster: 64 (over z, y, core), sub: 4 (over x).
Axes of the slice: x: 4, y: 4, z: 8, core: 2. Of those that a mesh axis runs over, the one named last changes fastest.
Arguments:
- adjoint_input: bfloat16 [1024, 2, 4, 128], P('cluster'), may hold values from -6 to 6
- efie_left: bfloat16 [1024, 8, 2, 64, 128], P('cluster', None, None, 'sub'), may hold values from -0.375 to 0.375
- efie_right: bfloat16 [1024, 8, 2, 64, 128], P('cluster', None, None, 'sub'), may hold values from -0.1875 to 0.1875
- dual_left: bfloat16 [1024, 8, 2, 64, 128], P('cluster', None, None, 'sub'), may hold values from -0.375 to 0.375
- dual_right: bfloat16 [1024, 8, 2, 64, 128], P('cluster', None, None, 'sub'), may hold values from -0.1875 to 0.1875
- block_ranks: int32 [1024, 8], P('cluster'), may hold values from 16 to 64
- far_cols: int32 [1024, 8], P('cluster'), may hold values from 0 to 1023, as said below
- efie_near: bfloat16 [1024, 8, 2, 128, 128], P('cluster', 'sub'), may hold values from -0.125 to 0.125
- dual_near: bfloat16 [1024, 8, 2, 128, 128], P('cluster', 'sub'), may hold values from -0.125 to 0.125
- near_cols: int32 [1024, 8], P('cluster', 'sub'), may hold values from 0 to 1023, as said below
Outputs:
- adjoint_efie: bfloat16 [1024, 2, 4, 128], P('cluster', None, 'sub')
- adjoint_dual: bfloat16 [1024, 2, 4, 128], P('cluster', None, 'sub')
Inputs may be any that keep to these rules, and one draw needn't show every extreme that they name: `far_cols`: the clusters e * 16 to e * 16 + 15 belong to index e of cluster; among the far blocks of the 16 block rows of one index, at most 4 have column clusters of any one index. `near_cols`: entry k of row i lies within 16 of i, and entry 0 of each row is i itself.
All inputs are finite; a program needn't handle non-finite values.
Results may differ from a plain program's by a relative error of at most 0.0035.
Values sent between devices are 32-bit elements; how exact they have to be, the bound alone decides.
No kernel may reach another device: no remote copies, remote signals or barrier semaphores. Data moves between devices by JAX's collectives and lax.ppermute only.
A program may use at most 64 MiB of HBM per device.

v0:
```python
import jax
import jax.numpy as jnp
from jax import lax
from jax.sharding import PartitionSpec as P


def padded(block, sides, width):
    for axis, dim in sides:
        count = lax.axis_size(axis)
        forward = [(i, i + 1) for i in range(count - 1)]
        backward = [(target, source) for source, target in forward]
        low = lax.ppermute(
            lax.slice_in_dim(block, block.shape[dim] - width, None, axis=dim), axis, forward
        )
        high = lax.ppermute(lax.slice_in_dim(block, 0, width, axis=dim), axis, backward)
        block = jnp.concatenate([low, block, high], axis=dim)
    return block


def conj_apply(mat_real, mat_imag, vec_real, vec_imag, pattern):

    def product(matrix, vector):
        return jnp.einsum(pattern, matrix, vector, preferred_element_type=jnp.float32)

    return (
        product(mat_real, vec_real) + product(mat_imag, vec_imag),
        product(mat_real, vec_imag) - product(mat_imag, vec_real),
    )


def plain_apply(mat_real, mat_imag, vec_real, vec_imag, pattern):

    def product(matrix, vector):
        return jnp.einsum(pattern, matrix, vector, preferred_element_type=jnp.float32)

    return (
        product(mat_real, vec_real) - product(mat_imag, vec_imag),
        product(mat_real, vec_imag) + product(mat_imag, vec_real),
    )


def per_device(
    adjoint_input,
    efie_left,
    efie_right,
    dual_left,
    dual_right,
    block_ranks,
    far_cols,
    efie_near,
    dual_near,
    near_cols,
):
    per_dev = adjoint_input.shape[0]
    far_count = far_cols.shape[1]
    slices = efie_left.shape[3]
    position = lax.axis_index("cluster")
    rank_index = lax.axis_index("sub") * slices + jnp.arange(slices, dtype=jnp.int32)
    keep_mask = rank_index[None, None, None, :] < block_ranks[:, :, None, None]
    vec_real = adjoint_input[:, 0]
    vec_imag = adjoint_input[:, 1]

    def far_terms(left_factor, right_factor):
        coef_real, coef_imag = conj_apply(
            left_factor[:, :, 0], left_factor[:, :, 1], vec_real, vec_imag, "cfrs,cns->cfnr"
        )
        coef_real = jnp.where(keep_mask, coef_real, 0.0).astype(jnp.bfloat16)
        coef_imag = jnp.where(keep_mask, coef_imag, 0.0).astype(jnp.bfloat16)
        out_real, out_imag = plain_apply(
            right_factor[:, :, 0], right_factor[:, :, 1], coef_real, coef_imag, "cfrt,cfnr->cfnt"
        )
        return jnp.stack([out_real, out_imag], 2)

    def near_terms(blocks):
        out_real, out_imag = conj_apply(
            blocks[:, :, 0], blocks[:, :, 1], vec_real, vec_imag, "ckst,cns->cknt"
        )
        return jnp.stack([out_real, out_imag], 2)

    far_part = jnp.stack([far_terms(efie_left, efie_right), far_terms(dual_left, dual_right)], 2)
    far_part = far_part.reshape((per_dev * far_count,) + far_part.shape[2:])
    near_part = jnp.stack([near_terms(efie_near), near_terms(dual_near)], 2)
    near_flat = near_part.reshape(near_part.shape[0] * near_part.shape[1], -1)
    window_rows = 3 * per_dev
    target = (near_cols - (position * per_dev - per_dev)).reshape(-1)
    select = (jnp.arange(window_rows, dtype=jnp.int32)[:, None] == target[None, :]).astype(
        jnp.float32
    )
    window = jnp.dot(select, near_flat, precision=lax.Precision.HIGHEST).reshape(
        (window_rows,) + near_part.shape[2:]
    )
    tail_shape = far_part.shape[1:]
    block_count = per_dev * far_count
    far_flat = far_part.reshape(block_count, -1)
    targets = far_cols.reshape(-1)
    offset = targets
    inside = (offset >= 0) & (offset < lax.axis_size("cluster") * per_dev)
    offset = jnp.where(inside, offset, lax.axis_size("cluster") * per_dev)
    gathered = lax.psum_scatter(
        jnp.zeros((lax.axis_size("cluster") * per_dev, far_flat.shape[1]), jnp.float32)
        .at[offset]
        .add(far_flat, mode="drop"),
        "cluster",
        scatter_dimension=0,
        tiled=True,
    )
    summed = gathered.reshape((per_dev,) + tail_shape)
    extended = padded(window, (("cluster", 0),), per_dev)
    summed = (
        summed + extended[:per_dev] + extended[2 * per_dev : 3 * per_dev] + extended[4 * per_dev :]
    )
    summed = lax.psum_scatter(summed, "sub", scatter_dimension=3, tiled=True)
    result = summed.astype(jnp.bfloat16)
    return (result[:, 0], result[:, 1])


def solution(mesh):
    return jax.shard_map(
        per_device,
        mesh=mesh,
        in_specs=(
            P("cluster", None, None, None),
            P("cluster", None, None, "sub", None),
            P("cluster", None, None, "sub", None),
            P("cluster", None, None, "sub", None),
            P("cluster", None, None, "sub", None),
            P("cluster", None),
            P("cluster", None),
            P("cluster", "sub", None, None, None),
            P("cluster", "sub", None, None, None),
            P("cluster", "sub"),
        ),
        out_specs=(P("cluster", None, "sub", None), P("cluster", None, "sub", None)),
        check_vma=False,
    )
```

profile of v0, /device:TPU:1, one launch (start us, length us, event | category | flops | bytes accessed | tf_op | source)
XLA Modules:
  0.0 220.5 jit_solution(6943516664873159008)
XLA Ops:
  7.3 3.2 %fusion.50 = f32[16,4,8,16]{3,1,2,0:T(4,128)} fusion(bf16[16,8,2,16,128]{4,3,2,1,0:T(8,128)(2,1)} %param.13, bf16[16,2,4,128]{3,2,1,0:T(4,128)(2,1)} %param.10), kind=kOutput, calls=%fused_computation.66 | convolution fusion | flops 2097152 | bytes 573440 | tf_op jit(solution)/shard_map/cfrs,cns->cfnr/dot_general | solution.py:23
  10.5 3.2 %fusion.52 = f32[16,4,8,16]{3,1,2,0:T(4,128)} fusion(bf16[16,8,2,16,128]{4,3,2,1,0:T(8,128)(2,1)} %param.13, bf16[16,2,4,128]{3,2,1,0:T(4,128)(2,1)} %param.10), kind=kOutput, calls=%fused_computation.68 | convolution fusion | flops 2097152 | bytes 573440 | tf_op jit(solution)/shard_map/cfrs,cns->cfnr/dot_general | solution.py:23
  13.7 3.1 %fusion.62 = f32[16,4,8,16]{3,1,2,0:T(4,128)} fusion(bf16[16,8,2,16,128]{4,3,2,1,0:T(8,128)(2,1)} %param.11, bf16[16,2,4,128]{3,2,1,0:T(4,128)(2,1)} %param.10), kind=kOutput, calls=%fused_computation.78 | convolution fusion | flops 2097152 | bytes 573440 | tf_op jit(solution)/shard_map/cfrs,cns->cfnr/dot_general | solution.py:23
  16.8 1.3 fusion.64
  18.3 2.3 %fusion.14 = bf16[16,8,4,16]{3,2,1,0:T(4,128)(2,1)S(1)} fusion(f32[16,4,8,16]{3,1,2,0:T(4,128)} %fusion.50, bf16[16,8,2,16,128]{4,3,2,1,0:T(8,128)(2,1)S(1)} %copy-done.5, pred[16,8,16]{2,1,0:T(8,128)(4,1)S(1)} %broadcast_compare_fusion, bf16[16,2,4,128]{3,2,1,0:T(4,128)(2,1)S(1)} %copy-done.4), kind=kOutput, calls=%fused_computation.23 | convolution fusion | flops 2121728 | bytes 606208 | tf_op jit(solution)/shard_map/cfrs,cns->cfnr/dot_general | solution.py:23
  20.6 2.3 %fusion.15 = bf16[16,8,4,16]{3,2,1,0:T(4,128)(2,1)S(1)} fusion(f32[16,4,8,16]{3,1,2,0:T(4,128)} %fusion.52, bf16[16,8,2,16,128]{4,3,2,1,0:T(8,128)(2,1)S(1)} %copy-done.5, pred[16,8,16]{2,1,0:T(8,128)(4,1)S(1)} %broadcast_compare_fusion, bf16[16,2,4,128]{3,2,1,0:T(4,128)(2,1)S(1)} %copy-done.4), kind=kOutput, calls=%fused_computation.24 | convolution fusion | flops 2121728 | bytes 606208 | tf_op jit(solution)/shard_map/cfrs,cns->cfnr/dot_general | solution.py:23
  24.0 1.3 fusion.16
  25.3 1.3 fusion.17
  26.7 0.3 fusion.56
  27.2 0.3 fusion.6
  28.5 0.3 copy-done.9
  29.0 5.8 %scatter_custom_fusion = f32[1024,2048]{1,0:T(8,128)} fusion(s32[128]{0:T(128)S(1)} %fusion.100, f32[128,2048]{1,0:T(8,128)S(1)} %bitcast.191, f32[]{:T(128)} %constant.8.clone.1), kind=kCustom, calls=%fused_computation.1 | custom fusion | flops 262144 | bytes 8388612 | tf_op jit(solution)/shard_map/scatter-add | solution.py:102
  34.9 1.5 copy-done
  37.4 0.6 copy-done.1
  39.5 0.3 fusion.82
  40.0 5.2 %collective-permute-start.1 = (f32[16,2,2,4,128]{4,3,2,1,0:T(4,128)S(1)}, f32[16,2,2,4,128]{4,3,2,1,0:T(4,128)S(1)}, u32[]{:S(2)}, u32[]{:S(2)}) collective-permute-start(f32[16,2,2,4,128]{4,3,2,1,0:T(4,128)S(1)} %slice.85), channel_id=1, source_target_pairs={{4,0},{8,4},{12,8},{16,12},{20,16},{24,20},{28,24},{32,28},{36,32}... | collective-permute-start | bytes 393224 | tf_op jit(solution)/shard_map/ppermute | solution.py:15
  45.3 1.9 collective-permute-start
  47.3 138.1 %reduce-scatter.3.cloned.1.call-done = f32[16,2048]{1,0:T(8,128)} async-done(((f32[1024,2048]{1,0:T(8,128)}), f32[16,2048]{1,0:T(8,128)}) %reduce-scatter.3.cloned.1.call-update) | async-done | bytes 131088 | tf_op jit(solution)/shard_map/reduce_scatter | solution.py:99
  185.4 1.0 reshape.70
  186.4 0.7 copy.95
  187.2 24.5 %reduce-scatter.5.cloned.1.call-done = f32[16,2,2,1,128]{4,0,2,1,3:T(8,128)} async-done(((f32[16,2,2,4,128]{4,0,2,1,3:T(8,128)}), f32[16,2,2,1,128]{4,0,2,1,3:T(8,128)}) %reduce-scatter.5.cloned.1.call-update) | async-done | bytes 32784 | tf_op jit(solution)/shard_map/reduce_scatter | solution.py:112
  211.6 0.8 bitcast_convert_fusion
  212.4 0.6 copy.97
  213.0 0.6 copy.98
  (61 shorter events, 5.6 us)
Async XLA Ops:
  7.2 9.6 %copy-start.4 = (bf16[16,2,4,128]{3,2,1,0:T(4,128)(2,1)S(1)}, bf16[16,2,4,128]{3,2,1,0:T(4,128)(2,1)}, u32[]{:S(2)}) copy-start(bf16[16,2,4,128]{3,2,1,0:T(4,128)(2,1)} %param.10) | copy-start | bytes 98308
  7.2 11.1 %copy-start.5 = (bf16[16,8,2,16,128]{4,3,2,1,0:T(8,128)(2,1)S(1)}, bf16[16,8,2,16,128]{4,3,2,1,0:T(8,128)(2,1)}, u32[]{:S(2)}) copy-start(bf16[16,8,2,16,128]{4,3,2,1,0:T(8,128)(2,1)} %param.13) | copy-start | bytes 3145732
  7.2 9.6 %copy-start.6 = (bf16[16,8,2,16,128]{4,3,2,1,0:T(8,128)(2,1)S(1)}, bf16[16,8,2,16,128]{4,3,2,1,0:T(8,128)(2,1)}, u32[]{:S(2)}) copy-start(bf16[16,8,2,16,128]{4,3,2,1,0:T(8,128)(2,1)} %param.11) | copy-start | bytes 3145732
  7.2 10.9 %copy-start.8 = (s32[16,8]{0,1:T(8,128)S(1)}, s32[16,8]{0,1:T(8,128)}, u32[]{:S(2)}) copy-start(s32[16,8]{0,1:T(8,128)} %param.15) | copy-start | bytes 1540
  7.2 178.2 %reduce-scatter.3.cloned.1.call-start = ((), (), s32[]{:S(2)}) async-start(), calls=%async_computation.2 | async-start | bytes 8519680 | tf_op jit(solution)/shard_map/reduce_scatter | solution.py:99
  10.5 12.4 %copy-start.2 = (bf16[16,8,2,16,128]{4,3,2,1,0:T(8,128)(2,1)S(1)}, bf16[16,8,2,16,128]{4,3,2,1,0:T(8,128)(2,1)}, u32[]{:S(2)}) copy-start(bf16[16,8,2,16,128]{4,3,2,1,0:T(8,128)(2,1)} %param.14) | copy-start | bytes 3145732
  22.8 1.2 copy-start.7
  23.4 3.3 %copy-start.3 = (bf16[16,8,2,16,128]{4,3,2,1,0:T(8,128)(2,1)S(1)}, bf16[16,8,2,16,128]{4,3,2,1,0:T(8,128)(2,1)}, u32[]{:S(2)}) copy-start(bf16[16,8,2,16,128]{4,3,2,1,0:T(8,128)(2,1)} %param.12) | copy-start | bytes 3145732
  28.1 0.7 copy-start.9
  34.8 1.6 copy-start
  34.8 176.8 %reduce-scatter.5.cloned.1.call-start = ((), (), s32[]{:S(2)}) async-start(), calls=%async_computation.3 | async-start | bytes 163840 | tf_op jit(solution)/shard_map/reduce_scatter | solution.py:112
  36.4 1.6 copy-start.1
  38.5 0.8 copy-start.10
  40.0 146.4 %collective-permute-start.1 = (f32[16,2,2,4,128]{4,3,2,1,0:T(4,128)S(1)}, f32[16,2,2,4,128]{4,3,2,1,0:T(4,128)S(1)}, u32[]{:S(2)}, u32[]{:S(2)}) collective-permute-start(f32[16,2,2,4,128]{4,3,2,1,0:T(4,128)S(1)} %slice.85), channel_id=1, source_target_pairs={{4,0},{8,4},{12,8},{16,12},{20,16},{24,20},{28,24},{32,28},{36,32}... | collective-permute-start | bytes 393224 | tf_op jit(solution)/shard_map/ppermute | solution.py:15
  45.3 141.1 %collective-permute-start = (f32[16,2,2,4,128]{4,3,2,1,0:T(4,128)S(1)}, f32[16,2,2,4,128]{4,3,2,1,0:T(4,128)S(1)}, u32[]{:S(2)}, u32[]{:S(2)}) collective-permute-start(f32[16,2,2,4,128]{4,3,2,1,0:T(4,128)S(1)} %slice.81), channel_id=1, source_target_pairs={{0,4},{4,8},{8,12},{12,16},{16,20},{20,24},{24,28},{28,32},{32,36}... | collective-permute-start | bytes 393224 | tf_op jit(solution)/shard_map/ppermute | solution.py:12
Sparse Core Ops, SparseCore 0:
  35.0 150.3 reduce-scatter.2
  188.0 23.5 reduce-scatter.4
where the time goes:
time: 222 us; the launch traced here: 220 us
  waiting for transfers between devices  163 us (73%)
  matrix products  22.6 us (10%)
  between operations  14.4 us (6%)
  other arithmetic  7.42 us (3%)
  starting transfers between devices  7.15 us (3%)
  local copies, waits for them, and re-layouts  6.35 us (3%)
    reduce_scatter x1, waiting for transfers between devices, per_device(): lax.psum_scatter(jnp.zeros((lax.axis_size('cluster') * per_dev, far_flat....  138 us
    reduce_scatter x1, waiting for transfers between devices, per_device(): summed = lax.psum_scatter(summed, 'sub', scatter_dimension=3, tiled=True)  24.5 us
    dot_general x24, matrix products, product(): jnp.einsum(pattern, matrix, vector, preferred_element_type=jnp.float32)  22.3 us
    scatter-add x1, other arithmetic, per_device(): gathered = lax.psum_scatter(jnp.zeros((lax.axis_size('cluster') * per_dev...  5.85 us
    ppermute x1, starting transfers between devices, padded(): lax.ppermute(lax.slice_in_dim(block, 0, width, axis=dim), axis, backward)  5.15 us
  transfers between devices with their start and end apart: 4, of which 2 were waited for; matrix products, arithmetic and copies ran while one was open for 2% of the time, Pallas kernels for 0%

commit v1 on v0

v1 whole, which is shorter than its diff:
```python
import jax
import jax.numpy as jnp
from jax import lax
from jax.experimental import pallas as pl
from jax.experimental.pallas import tpu as pltpu
from jax.sharding import PartitionSpec as P

F32 = jnp.float32
BF16 = jnp.bfloat16
LIMIT = 48 * 1024 * 1024


def iota(shape, dim):
    return lax.broadcasted_iota(jnp.int32, shape, dim)


def dot(left, right, dims=((1,), (0,))):
    return lax.dot_general(left, right, (dims, ((), ())), preferred_element_type=F32)


def vectors(x, me, cluster, copies):
    rows = 8 * copies
    shape = (2 * rows, x.shape[0])
    row, col = iota(shape, 0), iota(shape, 1)
    half = row // rows
    part = (row // copies) % 2
    vec = (me + (row % rows) // (2 * copies)) & 3
    wanted = cluster * 8 + jnp.where(half == part, 0, 1) * 4 + vec
    sign = jnp.where((half == 1) & (part == 1), -1.0, 1.0)
    both = dot(jnp.where(col == wanted, sign, 0.0).astype(BF16), x)
    return jnp.concatenate([both[:rows], both[rows:]], axis=1).astype(BF16)


def far_kernel(me_ref, rank_ref, x_ref, le, re, ld, rd, *outs):
    per_step = le.shape[0]
    step = pl.program_id(0)
    me = me_ref[0]
    x = x_ref[...]
    lane, sublane = iota((8, 128), 1), iota((8, 128), 0)
    for at in range(per_step):
        cluster = step * per_step + at
        lhs = vectors(x, me, cluster, 8)
        ranks = jnp.zeros((8, 128), jnp.int32)
        for f in range(8):
            ranks = jnp.where(lane // 16 == f, rank_ref[cluster, f], ranks)
        keep = (lane // 16 == sublane) & (me * 16 + lane % 16 < ranks)
        for op, (left, right) in enumerate(((le, re), (ld, rd))):
            u = jnp.concatenate([left[at, :, q].reshape(128, 128) for q in (0, 1)], axis=1)
            coef = dot(lhs, u, ((1,), (1,)))
            real = [jnp.where(keep, coef[k * 16 : k * 16 + 8], 0.0) for k in range(4)]
            imag = [jnp.where(keep, coef[k * 16 + 8 : k * 16 + 16], 0.0) for k in range(4)]
            first = jnp.concatenate([v for k in range(4) for v in (real[k], imag[k])], axis=0)
            second = jnp.concatenate([v for k in range(4) for v in (-imag[k], real[k])], axis=0)
            spread = jnp.concatenate([first, second], axis=1).astype(BF16)
            v = jnp.concatenate([right[at, :, q].reshape(128, 128) for q in (0, 1)], axis=0)
            far = dot(spread, v)
            for k in range(4):
                for q in range(2):
                    start = k * 16 + q * 8
                    outs[k][op * 2 + q, at * 8 : at * 8 + 8, :] = far[start : start + 8]


def near_kernel(me_ref, col_ref, x_ref, de, dd, low, mid, high, window):
    per_step = de.shape[0]
    step = pl.program_id(0)
    me, base = me_ref[0], me_ref[1]
    x = x_ref[...]

    @pl.when(step == 0)
    def _():
        window[...] = jnp.zeros_like(window)

    for at in range(per_step):
        cluster = step * per_step + at
        lhs = vectors(x, me, cluster, 1)
        for slot in range(2):
            d = jnp.concatenate([r[at, slot].reshape(256, 128) for r in (de, dd)], axis=1)
            out = dot(lhs, d)
            target = col_ref[cluster, slot] - base
            window[target, 0] += out[:, :128]
            window[target, 1] += out[:, 128:]

    @pl.when(step == pl.num_programs(0) - 1)
    def _():
        low[...] = window[0:16]
        mid[...] = window[16:32]
        high[...] = window[32:48]


def merge_kernel(mid, left, right, *outs):
    for k in range(4):
        for j in range(4):
            rows = pl.ds((j // 2) * 8 + k * 2 + j % 2, 16, stride=16)
            outs[k][j] = mid[rows, :] + left[rows, :] + right[rows, :]


def halves(value):
    high = value.astype(BF16)
    return high, (value - high.astype(F32)).astype(BF16)


def send_kernel(slot_ref, cols_ref, a, b, c, d, out):
    slot = jnp.broadcast_to(slot_ref[0:1, :], (64, 128))
    target = iota((64, 128), 0)
    picks = [jnp.where(slot == target * 4 + k, 1.0, 0.0).astype(BF16) for k in range(4)]
    pick = jnp.concatenate(picks, axis=0)
    pick = jnp.concatenate([pick, pick], axis=1)
    for pair in range(2):
        parts = []
        for j in (pair * 2, pair * 2 + 1):
            high, low = halves(a[j] + b[j] + c[j] + d[j])
            parts.append(jnp.concatenate([high, low], axis=0))
        moved = dot(pick, jnp.concatenate(parts, axis=1))
        for q in range(2):
            for k in range(4):
                rows = pl.ds(k * 4 + pair * 2 + q, 64, stride=17)
                out[rows, :] = moved[k * 64 : k * 64 + 64, q * 128 : q * 128 + 128]
    here = jnp.where(slot // 4 == target, 1.0, 0.0).astype(BF16)
    place = jnp.where(cols_ref[...] == iota((128, 128), 1), 1.0, 0.0).astype(BF16)
    out[pl.ds(16, 64, stride=17), :] = dot(here, place)


def sum_kernel(got, na, nb, nc, nd, efie, dual):
    marks = got[pl.ds(16, 64, stride=17), :].T
    pick = jnp.concatenate([marks[k * 16 : k * 16 + 16, :] for k in range(4)], axis=1).astype(BF16)
    pick = jnp.concatenate([pick, pick], axis=1)
    sums = []
    for j in range(4):
        value = jnp.concatenate([got[pl.ds(k * 4 + j, 64, stride=17), :] for k in range(4)], axis=0)
        high, low = halves(value)
        far = dot(pick, jnp.concatenate([high, low], axis=0))
        sums.append(far + na[j] + nb[j] + nc[j] + nd[j])
    efie[...] = jnp.stack([sums[0], sums[1]], axis=1).astype(BF16)
    dual[...] = jnp.stack([sums[2], sums[3]], axis=1).astype(BF16)


def whole(shape):
    return pl.BlockSpec(shape, lambda *_: (0,) * len(shape))


SMEM = pl.BlockSpec(memory_space=pltpu.SMEM)
VMEM = pl.BlockSpec(memory_space=pltpu.VMEM)


def per_device(
    adjoint_input,
    efie_left,
    efie_right,
    dual_left,
    dual_right,
    block_ranks,
    far_cols,
    efie_near,
    dual_near,
    near_cols,
):
    per_dev = adjoint_input.shape[0]
    subs = lax.axis_size("sub")
    position = lax.axis_index("cluster")
    me = lax.axis_index("sub")
    scalars = jnp.stack([me, position * per_dev - per_dev]).astype(jnp.int32)
    x = adjoint_input.reshape(per_dev * 8, 128)
    params = pltpu.CompilerParams(vmem_limit_bytes=LIMIT)

    def struct(shape, dtype=F32):
        return jax.ShapeDtypeStruct(shape, dtype)

    step = 4
    far_block = pl.BlockSpec((step, 8, 2, 16, 128), lambda i: (i, 0, 0, 0, 0))
    far = pl.pallas_call(
        far_kernel,
        grid=(per_dev // step,),
        in_specs=[SMEM, SMEM, whole((128, 128))] + [far_block] * 4,
        out_specs=[pl.BlockSpec((4, step * 8, 128), lambda i: (0, i, 0))] * 4,
        out_shape=[struct((4, 128, 128))] * 4,
        compiler_params=params,
        cost_estimate=pl.CostEstimate(flops=200_000_000, bytes_accessed=5_300_000, transcendentals=0),
        name="far",
    )(scalars, block_ranks, x, efie_left, efie_right, dual_left, dual_right)

    def shift(k):
        return [(i, (i + k) % subs) for i in range(subs)]

    far_got = [far[0]] + [lax.ppermute(far[k], "sub", shift(k)) for k in (1, 2, 3)]

    near_block = pl.BlockSpec((step, 2, 2, 128, 128), lambda i: (i, 0, 0, 0, 0))
    low, mid, high = pl.pallas_call(
        near_kernel,
        grid=(per_dev // step,),
        in_specs=[SMEM, SMEM, whole((128, 128)), near_block, near_block],
        out_specs=[whole((per_dev, 2, 8, 128))] * 3,
        out_shape=[struct((per_dev, 2, 8, 128))] * 3,
        scratch_shapes=[pltpu.VMEM((3 * per_dev, 2, 8, 128), F32)],
        compiler_params=params,
        cost_estimate=pl.CostEstimate(flops=200_000_000, bytes_accessed=4_600_000, transcendentals=0),
        name="near",
    )(scalars, near_cols, x, efie_near, dual_near)
    count = lax.axis_size("cluster")
    forward = [(i, i + 1) for i in range(count - 1)]
    backward = [(i + 1, i) for i in range(count - 1)]
    from_left = lax.ppermute(high, "cluster", forward)
    from_right = lax.ppermute(low, "cluster", backward)
    near = pl.pallas_call(
        merge_kernel,
        in_specs=[VMEM] * 3,
        out_specs=[VMEM] * 4,
        out_shape=[struct((4, per_dev, 128))] * 4,
        compiler_params=params,
        name="merge",
    )(*(v.reshape(per_dev * 16, 128) for v in (mid, from_left, from_right)))
    near_got = [near[0]] + [lax.ppermute(near[k], "sub", shift(k)) for k in (1, 2, 3)]

    cols = far_cols.reshape(-1)
    owner = cols // per_dev
    earlier = (owner[:, None] == owner[None, :]) & (jnp.arange(128)[None, :] < jnp.arange(128)[:, None])
    order = jnp.sum(earlier.astype(jnp.int32), axis=1)
    slot = jnp.broadcast_to((owner * 4 + order)[None, :], (8, 128))
    place = jnp.broadcast_to((order * 16 + cols % per_dev)[:, None], (128, 128))
    sent = pl.pallas_call(
        send_kernel,
        in_specs=[VMEM] * 6,
        out_specs=VMEM,
        out_shape=struct((count * 17, 128)),
        compiler_params=params,
        name="send",
    )(slot, place, *far_got)
    got = lax.all_to_all(sent.reshape(count * 17, 1, 128), "cluster", 0, 0, tiled=True)
    efie, dual = pl.pallas_call(
        sum_kernel,
        in_specs=[VMEM] * 5,
        out_specs=[VMEM] * 2,
        out_shape=[struct((per_dev, 2, 128), BF16)] * 2,
        compiler_params=params,
        name="total",
    )(got.reshape(count * 17, 128), *near_got)
    shape = (per_dev, 2, 1, 128)
    return efie.reshape(shape), dual.reshape(shape)


def solution(mesh):
    return jax.shard_map(
        per_device,
        mesh=mesh,
        in_specs=(
            P("cluster", None, None, None),
            P("cluster", None, None, "sub", None),
            P("cluster", None, None, "sub", None),
            P("cluster", None, None, "sub", None),
            P("cluster", None, None, "sub", None),
            P("cluster", None),
            P("cluster", None),
            P("cluster", "sub", None, None, None),
            P("cluster", "sub", None, None, None),
            P("cluster", "sub"),
        ),
        out_specs=(P("cluster", None, "sub", None), P("cluster", None, "sub", None)),
        check_vma=False,
    )
```

time: 222 us -> 70.9 us (0.32)
  the two profiles are of different devices: /device:TPU:1 before, /device:TPU:127 now
where the time goes in v1:
time: 70.9 us; the launch traced here: 70.4 us
  waiting for transfers between devices  24.7 us (35%)
  starting transfers between devices  22.2 us (31%)
  Pallas kernels  14.2 us (20%)
  local copies, waits for them, and re-layouts  8.34 us (12%)
  between operations  0.73 us (1%)
    ppermute x3, waiting for transfers between devices, per_device(): lax.ppermute(far[k], 'sub', shift(k))  13 us
    all_to_all x1, starting transfers between devices, per_device(): lax.all_to_all(sent.reshape(count * 17, 1, 128), 'cluster', 0, 0, tiled=T...  10.7 us
    pallas_call x1, Pallas kernels, per_device(): pl.pallas_call(far_kernel, grid=(per_dev // step,), in_specs=[SMEM, SMEM,...  8.61 us
    unnamed x23, local copies, waits for them, and re-layouts  8.17 us
    ppermute x1, waiting for transfers between devices, per_device(): from_right = lax.ppermute(low, 'cluster', backward)  5.57 us
    ppermute x1, starting transfers between devices, per_device(): from_left = lax.ppermute(high, 'cluster', forward)  4.56 us
    ppermute x3, waiting for transfers between devices, per_device(): lax.ppermute(near[k], 'sub', shift(k))  3.97 us
    pallas_call x1, Pallas kernels, per_device(): pl.pallas_call(near_kernel, grid=(per_dev // step,), in_specs=[SMEM, SMEM...  3.39 us
  transfers between devices with their start and end apart: 9, of which 8 were waited for; matrix products, arithmetic and copies ran while one was open for 1% of the time, Pallas kernels for 5%

profile of v1, /device:TPU:127, one launch (start us, length us, event | category | flops | bytes accessed | tf_op | source)
XLA Modules:
  0.0 70.4 jit_solution(5139314287040304171)
XLA Ops:
  0.6 0.8 %copy.29.rank_ref = s32[16,8]{1,0:T(8,128)S(1)} copy(s32[16,8]{0,1:T(8,128)} %param.15) | data formatting | bytes 1024 | tf_op args[5]
  1.5 1.2 %copy-done.2 = bf16[16,8,2,16,128]{4,3,2,1,0:T(8,128)(2,1)S(1)} copy-done((bf16[16,8,2,16,128]{4,3,2,1,0:T(8,128)(2,1)S(1)}, bf16[16,8,2,16,128]{4,3,2,1,0:T(8,128)(2,1)}, u32[]{:S(2)}) %copy-start.2) | copy-done | bytes 1048600
  2.7 1.2 %copy-done.3 = bf16[16,8,2,16,128]{4,3,2,1,0:T(8,128)(2,1)S(1)} copy-done((bf16[16,8,2,16,128]{4,3,2,1,0:T(8,128)(2,1)S(1)}, bf16[16,8,2,16,128]{4,3,2,1,0:T(8,128)(2,1)}, u32[]{:S(2)}) %copy-start.3) | copy-done | bytes 1048600
  3.9 1.2 %copy-done.4 = bf16[16,8,2,16,128]{4,3,2,1,0:T(8,128)(2,1)S(1)} copy-done((bf16[16,8,2,16,128]{4,3,2,1,0:T(8,128)(2,1)S(1)}, bf16[16,8,2,16,128]{4,3,2,1,0:T(8,128)(2,1)}, u32[]{:S(2)}) %copy-start.4) | copy-done | bytes 1048600
  5.1 1.2 %copy-done.5 = bf16[16,8,2,16,128]{4,3,2,1,0:T(8,128)(2,1)S(1)} copy-done((bf16[16,8,2,16,128]{4,3,2,1,0:T(8,128)(2,1)S(1)}, bf16[16,8,2,16,128]{4,3,2,1,0:T(8,128)(2,1)}, u32[]{:S(2)}) %copy-start.5) | copy-done | bytes 1048600
  6.4 0.8 %copy-done.6 = bf16[16,2,4,128]{3,2,1,0:T(4,128)(2,1)S(1)} copy-done((bf16[16,2,4,128]{3,2,1,0:T(4,128)(2,1)S(1)}, bf16[16,2,4,128]{3,2,1,0:T(4,128)(2,1)}, u32[]{:S(2)}) %copy-start.6) | copy-done | bytes 32792
  7.1 8.6 %far.1 = (f32[4,128,128]{2,1,0:T(8,128)S(1)}, f32[4,128,128]{2,1,0:T(8,128)}, f32[4,128,128]{2,1,0:T(8,128)}, f32[4,128,128]{2,1,0:T(8,128)S(1)}) custom-call(s32[2]{0:T(128)S(1)} %pad_add_fusion.me_ref, s32[16,8]{1,0:T(8,128)S(1)} %copy.29.rank_ref, bf16[128,128]{1,0:T(8,128)(2,1)S(1)} %bitcast.17, bf16[16,8,2,16,128]{4,3,2,1,0:T(8,128)(2,1)S(1)} %copy-done.2, ...), custom_call_target="tpu_custom_call" | custom-call | flops 200000000 | bytes 5300000 | tf_op jit(solution)/shard_map/far/pallas_call | solution.py:170
  16.0 2.1 %collective-permute-start.1 = (f32[4,128,128]{2,1,0:T(8,128)}, f32[4,128,128]{2,1,0:T(8,128)S(1)}, u32[]{:S(2)}, u32[]{:S(2)}) collective-permute-start(f32[4,128,128]{2,1,0:T(8,128)} %get-tuple-element.17), channel_id=1, source_target_pairs={{0,2},{1,3},{2,0},{3,1},{4,6},{5,7},{6,4},{7,5},{8,10},{9,11},{10,... | collective-permute-start | bytes 786440 | tf_op jit(solution)/shard_map/ppermute | solution.py:184
  18.5 4.7 %collective-permute-done.b = f32[4,128,128]{2,1,0:T(8,128)S(1)} collective-permute-done((f32[4,128,128]{2,1,0:T(8,128)}, f32[4,128,128]{2,1,0:T(8,128)S(1)}, u32[]{:S(2)}, u32[]{:S(2)}) %collective-permute-start) | collective-permute-done | bytes 262176 | tf_op jit(solution)/shard_map/ppermute | solution.py:184
  23.2 1.4 %collective-permute-done.1.c = f32[4,128,128]{2,1,0:T(8,128)S(1)} collective-permute-done((f32[4,128,128]{2,1,0:T(8,128)}, f32[4,128,128]{2,1,0:T(8,128)S(1)}, u32[]{:S(2)}, u32[]{:S(2)}) %collective-permute-start.1) | collective-permute-done | bytes 262176 | tf_op jit(solution)/shard_map/ppermute | solution.py:184
  24.6 6.9 %collective-permute-done.2.d = f32[4,128,128]{2,1,0:T(8,128)S(1)} collective-permute-done((f32[4,128,128]{2,1,0:T(8,128)S(1)}, f32[4,128,128]{2,1,0:T(8,128)S(1)}, u32[]{:S(2)}, u32[]{:S(2)}) %collective-permute-start.2) | collective-permute-done | bytes 262176 | tf_op jit(solution)/shard_map/ppermute | solution.py:184
  31.7 1.1 %send.1 = f32[1088,128]{1,0:T(8,128)} custom-call(s32[8,128]{1,0:T(8,128)S(1)} %broadcast_in_dim.4.slot_ref, s32[128,128]{1,0:T(8,128)S(1)} %broadcast_in_dim.5.cols_ref, f32[4,128,128]{2,1,0:T(8,128)S(1)} %get-tuple-element.15.a, f32[4,128,128]{2,1,0:T(8,128)S(1)} %collective-permute-done.b, f32[4,128,128]{2,1,0:T(8,128)S(1)} %collective-permute-done.1.c, ...), custom_call_target="tpu_custom_call" | custom-call | tf_op jit(solution)/shard_map/send/pallas_call | solution.py:219
  32.8 10.7 %all-to-all-start = ((f32[1088,1,128]{2,1,0:T(1,128)}), f32[1088,1,128]{2,1,0:T(1,128)S(1)}, u32[]{:S(2)}, u32[]{:S(2)}) async-start(f32[1088,1,128]{2,1,0:T(1,128)} %bitcast.4), calls=%async_computation | async-start | bytes 1114112 | tf_op jit(solution)/shard_map/all_to_all | solution.py:227
  43.6 1.6 %copy-done.1 = bf16[16,2,2,128,128]{4,3,2,1,0:T(8,128)(2,1)S(1)} copy-done((bf16[16,2,2,128,128]{4,3,2,1,0:T(8,128)(2,1)S(1)}, bf16[16,2,2,128,128]{4,3,2,1,0:T(8,128)(2,1)}, u32[]{:S(2)}) %copy-start.1) | copy-done | bytes 2097176
  45.2 3.4 %near.1 = (f32[16,2,8,128]{3,2,1,0:T(8,128)S(1)}, f32[16,2,8,128]{3,2,1,0:T(8,128)S(1)}, f32[16,2,8,128]{3,2,1,0:T(8,128)S(1)}) custom-call(s32[2]{0:T(128)S(1)} %pad_add_fusion.me_ref, s32[16,2]{1,0:T(8,128)S(1)} %copy.31.col_ref, bf16[128,128]{1,0:T(8,128)(2,1)S(1)} %bitcast.18, bf16[16,2,2,128,128]{4,3,2,1,0:T(8,128)(2,1)S(1)} %copy-done, ...), custom_call_target="tpu_custom_call" | custom-call | flops 200000000 | bytes 4600000 | tf_op jit(solution)/shard_map/near/pallas_call | solution.py:187
  48.6 4.6 %collective-permute-start.3 = (f32[16,2,8,128]{3,2,1,0:T(8,128)S(1)}, f32[16,2,8,128]{3,2,1,0:T(8,128)S(1)}, u32[]{:S(2)}, u32[]{:S(2)}) collective-permute-start(f32[16,2,8,128]{3,2,1,0:T(8,128)S(1)} %get-tuple-element.20), channel_id=1, source_target_pairs={{0,4},{4,8},{8,12},{12,16},{16,20},{20,24},{24,28},{28,32},{32,36}... | collective-permute-start | bytes 393224 | tf_op jit(solution)/shard_map/ppermute | solution.py:201
  53.2 1.9 %collective-permute-start.4 = (f32[16,2,8,128]{3,2,1,0:T(8,128)S(1)}, f32[16,2,8,128]{3,2,1,0:T(8,128)S(1)}, u32[]{:S(2)}, u32[]{:S(2)}) collective-permute-start(f32[16,2,8,128]{3,2,1,0:T(8,128)S(1)} %get-tuple-element.21), channel_id=1, source_target_pairs={{4,0},{8,4},{12,8},{16,12},{20,16},{24,20},{28,24},{32,28},{36,32}... | collective-permute-start | bytes 393224 | tf_op jit(solution)/shard_map/ppermute | solution.py:202
  55.1 2.1 %collective-permute-done.3 = f32[16,2,8,128]{3,2,1,0:T(8,128)S(1)} collective-permute-done((f32[16,2,8,128]{3,2,1,0:T(8,128)S(1)}, f32[16,2,8,128]{3,2,1,0:T(8,128)S(1)}, u32[]{:S(2)}, u32[]{:S(2)}) %collective-permute-start.3) | collective-permute-done | bytes 131104 | tf_op jit(solution)/shard_map/ppermute | solution.py:201
  57.2 5.6 %collective-permute-done.4 = f32[16,2,8,128]{3,2,1,0:T(8,128)S(1)} collective-permute-done((f32[16,2,8,128]{3,2,1,0:T(8,128)S(1)}, f32[16,2,8,128]{3,2,1,0:T(8,128)S(1)}, u32[]{:S(2)}, u32[]{:S(2)}) %collective-permute-start.4) | collective-permute-done | bytes 131104 | tf_op jit(solution)/shard_map/ppermute | solution.py:202
  62.9 0.8 %collective-permute-start.5 = (f32[4,16,128]{2,1,0:T(8,128)S(1)}, f32[4,16,128]{2,1,0:T(8,128)S(1)}, u32[]{:S(2)}, u32[]{:S(2)}) collective-permute-start(f32[4,16,128]{2,1,0:T(8,128)S(1)} %get-tuple-element.23), channel_id=1, source_target_pairs={{0,1},{1,2},{2,3},{3,0},{4,5},{5,6},{6,7},{7,4},{8,9},{9,10},{10,1... | collective-permute-start | bytes 98312 | tf_op jit(solution)/shard_map/ppermute | solution.py:211
  63.7 1.8 %collective-permute-start.6 = (f32[4,16,128]{2,1,0:T(8,128)S(1)}, f32[4,16,128]{2,1,0:T(8,128)S(1)}, u32[]{:S(2)}, u32[]{:S(2)}) collective-permute-start(f32[4,16,128]{2,1,0:T(8,128)S(1)} %get-tuple-element.24), channel_id=1, source_target_pairs={{0,2},{1,3},{2,0},{3,1},{4,6},{5,7},{6,4},{7,5},{8,10},{9,11},{10,... | collective-permute-start | bytes 98312 | tf_op jit(solution)/shard_map/ppermute | solution.py:211
  65.7 2.2 %collective-permute-done.6.nc = f32[4,16,128]{2,1,0:T(8,128)S(1)} collective-permute-done((f32[4,16,128]{2,1,0:T(8,128)S(1)}, f32[4,16,128]{2,1,0:T(8,128)S(1)}, u32[]{:S(2)}, u32[]{:S(2)}) %collective-permute-start.6) | collective-permute-done | bytes 32800 | tf_op jit(solution)/shard_map/ppermute | solution.py:211
  67.9 1.5 %collective-permute-done.7.nd = f32[4,16,128]{2,1,0:T(8,128)S(1)} collective-permute-done((f32[4,16,128]{2,1,0:T(8,128)S(1)}, f32[4,16,128]{2,1,0:T(8,128)S(1)}, u32[]{:S(2)}, u32[]{:S(2)}) %collective-permute-start.7) | collective-permute-done | bytes 32800 | tf_op jit(solution)/shard_map/ppermute | solution.py:211
  69.4 0.9 %total.1 = (bf16[16,2,128]{2,1,0:T(2,128)(2,1)}, bf16[16,2,128]{2,1,0:T(2,128)(2,1)}) custom-call(f32[1088,128]{1,0:T(8,128)S(1)} %bitcast.16, f32[4,16,128]{2,1,0:T(8,128)S(1)} %get-tuple-element.22.na, f32[4,16,128]{2,1,0:T(8,128)S(1)} %collective-permute-done.5.nb, f32[4,16,128]{2,1,0:T(8,128)S(1)} %collective-permute-done.6.nc, ...), custom_call_target="tpu_custom_call" | custom-call | tf_op jit(solution)/shard_map/total/pallas_call | solution.py:228
  (29 shorter events, 1.3 us)
Async XLA Ops:
  1.5 1.2 %copy-start.2 = (bf16[16,8,2,16,128]{4,3,2,1,0:T(8,128)(2,1)S(1)}, bf16[16,8,2,16,128]{4,3,2,1,0:T(8,128)(2,1)}, u32[]{:S(2)}) copy-start(bf16[16,8,2,16,128]{4,3,2,1,0:T(8,128)(2,1)} %le.1) | copy-start | bytes 3145732
  2.7 1.2 %copy-start.3 = (bf16[16,8,2,16,128]{4,3,2,1,0:T(8,128)(2,1)S(1)}, bf16[16,8,2,16,128]{4,3,2,1,0:T(8,128)(2,1)}, u32[]{:S(2)}) copy-start(bf16[16,8,2,16,128]{4,3,2,1,0:T(8,128)(2,1)} %re.1) | copy-start | bytes 3145732
  3.9 1.2 %copy-start.4 = (bf16[16,8,2,16,128]{4,3,2,1,0:T(8,128)(2,1)S(1)}, bf16[16,8,2,16,128]{4,3,2,1,0:T(8,128)(2,1)}, u32[]{:S(2)}) copy-start(bf16[16,8,2,16,128]{4,3,2,1,0:T(8,128)(2,1)} %ld.1) | copy-start | bytes 3145732
  5.1 1.2 %copy-start.5 = (bf16[16,8,2,16,128]{4,3,2,1,0:T(8,128)(2,1)S(1)}, bf16[16,8,2,16,128]{4,3,2,1,0:T(8,128)(2,1)}, u32[]{:S(2)}) copy-start(bf16[16,8,2,16,128]{4,3,2,1,0:T(8,128)(2,1)} %rd.1) | copy-start | bytes 3145732
  6.4 0.8 %copy-start.6 = (bf16[16,2,4,128]{3,2,1,0:T(4,128)(2,1)S(1)}, bf16[16,2,4,128]{3,2,1,0:T(4,128)(2,1)}, u32[]{:S(2)}) copy-start(bf16[16,2,4,128]{3,2,1,0:T(4,128)(2,1)} %param.10) | copy-start | bytes 98308
  7.1 11.0 %copy-start.8 = (s32[16,8]{0,1:T(8,128)S(1)}, s32[16,8]{0,1:T(8,128)}, u32[]{:S(2)}) copy-start(s32[16,8]{0,1:T(8,128)} %param.16) | copy-start | bytes 1540
  15.7 27.8 %copy-start.9 = (s32[16,2]{0,1:T(2,128)S(1)}, s32[16,2]{0,1:T(2,128)}, u32[]{:S(2)}) copy-start(s32[16,2]{0,1:T(2,128)} %param.19) | copy-start | bytes 388
  15.7 27.9 %copy-start = (bf16[16,2,2,128,128]{4,3,2,1,0:T(8,128)(2,1)S(1)}, bf16[16,2,2,128,128]{4,3,2,1,0:T(8,128)(2,1)}, u32[]{:S(2)}) copy-start(bf16[16,2,2,128,128]{4,3,2,1,0:T(8,128)(2,1)} %de.1) | copy-start | bytes 6291460
  15.7 27.9 %copy-start.7 = (bf16[16,2,4,128]{3,2,1,0:T(4,128)(2,1)S(1)}, bf16[16,2,4,128]{3,2,1,0:T(4,128)(2,1)}, u32[]{:S(2)}) copy-start(bf16[16,2,4,128]{3,2,1,0:T(4,128)(2,1)} %param.10) | copy-start | bytes 98308
  15.8 7.5 %collective-permute-start = (f32[4,128,128]{2,1,0:T(8,128)}, f32[4,128,128]{2,1,0:T(8,128)S(1)}, u32[]{:S(2)}, u32[]{:S(2)}) collective-permute-start(f32[4,128,128]{2,1,0:T(8,128)} %get-tuple-element.16), channel_id=1, source_target_pairs={{0,1},{1,2},{2,3},{3,0},{4,5},{5,6},{6,7},{7,4},{8,9},{9,10},{10,1... | collective-permute-start | bytes 786440 | tf_op jit(solution)/shard_map/ppermute | solution.py:184
  16.0 8.6 %collective-permute-start.1 = (f32[4,128,128]{2,1,0:T(8,128)}, f32[4,128,128]{2,1,0:T(8,128)S(1)}, u32[]{:S(2)}, u32[]{:S(2)}) collective-permute-start(f32[4,128,128]{2,1,0:T(8,128)} %get-tuple-element.17), channel_id=1, source_target_pairs={{0,2},{1,3},{2,0},{3,1},{4,6},{5,7},{6,4},{7,5},{8,10},{9,11},{10,... | collective-permute-start | bytes 786440 | tf_op jit(solution)/shard_map/ppermute | solution.py:184
  18.2 13.4 %collective-permute-start.2 = (f32[4,128,128]{2,1,0:T(8,128)S(1)}, f32[4,128,128]{2,1,0:T(8,128)S(1)}, u32[]{:S(2)}, u32[]{:S(2)}) collective-permute-start(f32[4,128,128]{2,1,0:T(8,128)S(1)} %get-tuple-element.18), channel_id=1, source_target_pairs={{0,3},{1,0},{2,1},{3,2},{4,7},{5,4},{6,5},{7,6},{8,11},{9,8},{10,9... | collective-permute-start | bytes 786440 | tf_op jit(solution)/shard_map/ppermute | solution.py:184
  32.8 36.6 %all-to-all-start = ((f32[1088,1,128]{2,1,0:T(1,128)}), f32[1088,1,128]{2,1,0:T(1,128)S(1)}, u32[]{:S(2)}, u32[]{:S(2)}) async-start(f32[1088,1,128]{2,1,0:T(1,128)} %bitcast.4), calls=%async_computation | async-start | bytes 1114112 | tf_op jit(solution)/shard_map/all_to_all | solution.py:227
  43.6 1.6 %copy-start.1 = (bf16[16,2,2,128,128]{4,3,2,1,0:T(8,128)(2,1)S(1)}, bf16[16,2,2,128,128]{4,3,2,1,0:T(8,128)(2,1)}, u32[]{:S(2)}) copy-start(bf16[16,2,2,128,128]{4,3,2,1,0:T(8,128)(2,1)} %dd.1) | copy-start | bytes 6291460
  48.6 8.6 %collective-permute-start.3 = (f32[16,2,8,128]{3,2,1,0:T(8,128)S(1)}, f32[16,2,8,128]{3,2,1,0:T(8,128)S(1)}, u32[]{:S(2)}, u32[]{:S(2)}) collective-permute-start(f32[16,2,8,128]{3,2,1,0:T(8,128)S(1)} %get-tuple-element.20), channel_id=1, source_target_pairs={{0,4},{4,8},{8,12},{12,16},{16,20},{20,24},{24,28},{28,32},{32,36}... | collective-permute-start | bytes 393224 | tf_op jit(solution)/shard_map/ppermute | solution.py:201
  53.2 9.6 %collective-permute-start.4 = (f32[16,2,8,128]{3,2,1,0:T(8,128)S(1)}, f32[16,2,8,128]{3,2,1,0:T(8,128)S(1)}, u32[]{:S(2)}, u32[]{:S(2)}) collective-permute-start(f32[16,2,8,128]{3,2,1,0:T(8,128)S(1)} %get-tuple-element.21), channel_id=1, source_target_pairs={{4,0},{8,4},{12,8},{16,12},{20,16},{24,20},{28,24},{32,28},{36,32}... | collective-permute-start | bytes 393224 | tf_op jit(solution)/shard_map/ppermute | solution.py:202
  62.9 2.8 %collective-permute-start.5 = (f32[4,16,128]{2,1,0:T(8,128)S(1)}, f32[4,16,128]{2,1,0:T(8,128)S(1)}, u32[]{:S(2)}, u32[]{:S(2)}) collective-permute-start(f32[4,16,128]{2,1,0:T(8,128)S(1)} %get-tuple-element.23), channel_id=1, source_target_pairs={{0,1},{1,2},{2,3},{3,0},{4,5},{5,6},{6,7},{7,4},{8,9},{9,10},{10,1... | collective-permute-start | bytes 98312 | tf_op jit(solution)/shard_map/ppermute | solution.py:211
  63.7 4.3 %collective-permute-start.6 = (f32[4,16,128]{2,1,0:T(8,128)S(1)}, f32[4,16,128]{2,1,0:T(8,128)S(1)}, u32[]{:S(2)}, u32[]{:S(2)}) collective-permute-start(f32[4,16,128]{2,1,0:T(8,128)S(1)} %get-tuple-element.24), channel_id=1, source_target_pairs={{0,2},{1,3},{2,0},{3,1},{4,6},{5,7},{6,4},{7,5},{8,10},{9,11},{10,... | collective-permute-start | bytes 98312 | tf_op jit(solution)/shard_map/ppermute | solution.py:211
  65.4 4.0 %collective-permute-start.7 = (f32[4,16,128]{2,1,0:T(8,128)S(1)}, f32[4,16,128]{2,1,0:T(8,128)S(1)}, u32[]{:S(2)}, u32[]{:S(2)}) collective-permute-start(f32[4,16,128]{2,1,0:T(8,128)S(1)} %get-tuple-element.25), channel_id=1, source_target_pairs={{0,3},{1,0},{2,1},{3,2},{4,7},{5,4},{6,5},{7,6},{8,11},{9,8},{10,9... | collective-permute-start | bytes 98312 | tf_op jit(solution)/shard_map/ppermute | solution.py:211

commit v2 on v1

v2 whole, which is shorter than its diff:
```python
import functools

import jax
import jax.numpy as jnp
from jax import lax
from jax.experimental import pallas as pl
from jax.experimental.pallas import tpu as pltpu
from jax.sharding import PartitionSpec as P

F32 = jnp.float32
BF16 = jnp.bfloat16
MIB = 1024 * 1024


def iota(shape, dim):
    return lax.broadcasted_iota(jnp.int32, shape, dim)


def dot(left, right, dims=((1,), (0,))):
    return lax.dot_general(left, right, (dims, ((), ())), preferred_element_type=F32)


def vectors(x, me, cluster, copies):
    rows = 8 * copies
    shape = (2 * rows, x.shape[0])
    row, col = iota(shape, 0), iota(shape, 1)
    half = row // rows
    part = (row // copies) % 2
    vec = (me + (row % rows) // (2 * copies)) & 3
    wanted = cluster * 8 + jnp.where(half == part, 0, 1) * 4 + vec
    sign = jnp.where((half == 1) & (part == 1), -1.0, 1.0)
    both = dot(jnp.where(col == wanted, sign, 0.0).astype(BF16), x)
    return jnp.concatenate([both[:rows], both[rows:]], axis=1).astype(BF16)


def planes(ref, at, axis):
    return jnp.concatenate([ref[at, :, q].reshape(128, 128) for q in (0, 1)], axis=axis)


def far_kernel(chunk, me_ref, rank_ref, x_ref, le, re, ld, rd, o0, o1, o2, o3, ble, bre, bld, brd, made, lhs, sems, out_sems):
    outs = (o0, o1, o2, o3)
    clusters = ble.shape[0]
    steps = clusters // chunk

    def loads(i):
        part = pl.ds(i * chunk, chunk)
        pairs = ((le, ble), (ld, bld), (re, bre), (rd, brd))
        return [pltpu.make_async_copy(a.at[part], b.at[part], sems.at[j, i]) for j, (a, b) in enumerate(pairs)]

    def stores(i):
        part = pl.ds(i * chunk * 8, chunk * 8)
        return [pltpu.make_async_copy(made.at[k, :, part], outs[k].at[:, part], out_sems.at[k, i]) for k in (2, 1, 3, 0)]

    for i in range(steps):
        for copy in loads(i):
            copy.start()
    me = me_ref[0]
    x = x_ref[...]
    lane, sublane = iota((8, 128), 1), iota((8, 128), 0)
    for cluster in range(clusters):
        lhs[cluster] = vectors(x, me, cluster, 8)

    def spread(coef, keep):
        rows = [jnp.where(keep, coef[k * 8 : k * 8 + 8], 0.0) for k in range(8)]
        turned = [v for k in range(4) for v in (-rows[2 * k + 1], rows[2 * k])]
        both = [jnp.concatenate(rows, axis=0), jnp.concatenate(turned, axis=0)]
        return jnp.concatenate(both, axis=1).astype(BF16)

    for i in range(steps):
        for copy in loads(i):
            copy.wait()
        for cluster in range(i * chunk, i * chunk + chunk):
            ranks = jnp.zeros((8, 128), jnp.int32)
            for f in range(8):
                ranks = jnp.where(lane // 16 == f, rank_ref[f, cluster], ranks)
            keep = (lane // 16 == sublane) & (me * 16 + lane % 16 < ranks)
            u = jnp.concatenate([planes(ble, cluster, 1), planes(bld, cluster, 1)], axis=0)
            coef = dot(lhs[cluster], u, ((1,), (1,)))
            mixed = jnp.concatenate([spread(coef[:, :128], keep), spread(coef[:, 128:], keep)], axis=0)
            v = jnp.concatenate([planes(bre, cluster, 0), planes(brd, cluster, 0)], axis=1)
            far = dot(mixed, v)
            for op in range(2):
                for k in range(4):
                    for q in range(2):
                        start = op * 64 + k * 16 + q * 8
                        made[k, op * 2 + q, cluster * 8 : cluster * 8 + 8, :] = far[
                            start : start + 8, op * 128 : op * 128 + 128
                        ]
        for copy in stores(i):
            copy.start()
    for i in range(steps):
        for copy in stores(i):
            copy.wait()


def near_kernel(chunk, me_ref, base_ref, col_ref, x_ref, de, dd, after, mid, pair, other, bde, bdd, window, sems):
    clusters = bde.shape[0]
    steps = clusters // chunk

    def loads(i):
        part = pl.ds(i * chunk, chunk)
        pairs = ((de, bde), (dd, bdd))
        return [pltpu.make_async_copy(a.at[part], b.at[part], sems.at[j, i]) for j, (a, b) in enumerate(pairs)]

    for i in range(steps):
        for copy in loads(i):
            copy.start()
    me, base = me_ref[0], base_ref[0]
    x = x_ref[...]
    window[...] = jnp.zeros_like(window)
    lhs = [vectors(x, me, cluster, 1) for cluster in range(clusters)]
    for i in range(steps):
        for copy in loads(i):
            copy.wait()
        for cluster in range(i * chunk, i * chunk + chunk):
            for slot in range(2):
                d = jnp.concatenate([r[cluster, slot].reshape(256, 128) for r in (bde, bdd)], axis=1)
                out = dot(lhs[cluster], d)
                target = col_ref[slot, cluster] - base
                window[target, 0] += out[:, :128]
                window[target, 1] += out[:, 128:]
    odd = (base // 16) & 1 == 0
    mid[...] = window[16:32]
    pair[...] = window[pl.ds(jnp.where(odd, 0, 32), 16)]
    other[...] = window[pl.ds(jnp.where(odd, 32, 0), 16)]


def halves(value):
    high = value.astype(BF16)
    return high, (value - high.astype(F32)).astype(BF16)


def send_kernel(slot_ref, cols_ref, a, b, c, d, mid, pair, other, out, *near):
    slot = jnp.broadcast_to(slot_ref[0:1, :], (64, 128))
    target = iota((64, 128), 0)
    picks = [jnp.where(slot == target * 4 + k, 1.0, 0.0).astype(BF16) for k in range(4)]
    pick = jnp.concatenate(picks, axis=0)
    pick = jnp.concatenate([pick, pick], axis=1)
    for half in range(2):
        parts = []
        for j in (half * 2, half * 2 + 1):
            high, low = halves(a[j] + b[j] + c[j] + d[j])
            parts.append(jnp.concatenate([high, low], axis=0))
        moved = dot(pick, jnp.concatenate(parts, axis=1))
        for q in range(2):
            for k in range(4):
                rows = pl.ds(k * 4 + half * 2 + q, 64, stride=17)
                out[rows, :] = moved[k * 64 : k * 64 + 64, q * 128 : q * 128 + 128]
    here = jnp.where(slot // 4 == target, 1.0, 0.0).astype(BF16)
    place = jnp.where(cols_ref[...] == iota((128, 128), 1), 1.0, 0.0).astype(BF16)
    out[pl.ds(16, 64, stride=17), :] = dot(here, place)
    for k in range(4):
        for j in range(4):
            rows = pl.ds((j // 2) * 8 + k * 2 + j % 2, 16, stride=16)
            near[k][j] = mid[rows, :] + pair[rows, :] + other[rows, :]


def sum_kernel(got, na, nb, nc, nd, efie, dual):
    marks = got[pl.ds(16, 64, stride=17), :].T
    pick = jnp.concatenate([marks[k * 16 : k * 16 + 16, :] for k in range(4)], axis=1).astype(BF16)
    pick = jnp.concatenate([pick, pick], axis=1)
    sums = []
    for j in range(4):
        value = jnp.concatenate([got[pl.ds(k * 4 + j, 64, stride=17), :] for k in range(4)], axis=0)
        high, low = halves(value)
        far = dot(pick, jnp.concatenate([high, low], axis=0))
        sums.append(far + na[j] + nb[j] + nc[j] + nd[j])
    efie[...] = jnp.stack([sums[0], sums[1]], axis=1).astype(BF16)
    dual[...] = jnp.stack([sums[2], sums[3]], axis=1).astype(BF16)


SMEM = pl.BlockSpec(memory_space=pltpu.SMEM)
VMEM = pl.BlockSpec(memory_space=pltpu.VMEM)
ANY = pl.BlockSpec(memory_space=pl.ANY)


def per_device(
    adjoint_input,
    efie_left,
    efie_right,
    dual_left,
    dual_right,
    block_ranks,
    far_cols,
    efie_near,
    dual_near,
    near_cols,
):
    per_dev = adjoint_input.shape[0]
    subs = lax.axis_size("sub")
    position = lax.axis_index("cluster")
    me = lax.axis_index("sub")
    me_ref = me.astype(jnp.int32).reshape(1)
    base = (position * per_dev - per_dev).astype(jnp.int32).reshape(1)
    x = adjoint_input.reshape(per_dev * 8, 128)
    params = pltpu.CompilerParams(vmem_limit_bytes=62 * MIB)
    small = pltpu.CompilerParams(vmem_limit_bytes=12 * MIB)

    def struct(shape, dtype=F32):
        return jax.ShapeDtypeStruct(shape, dtype)

    chunk = 4
    steps = per_dev // chunk
    far = pl.pallas_call(
        functools.partial(far_kernel, chunk),
        in_specs=[SMEM, SMEM, VMEM] + [ANY] * 4,
        out_specs=[ANY] * 4,
        out_shape=[struct((4, 128, 128))] * 4,
        scratch_shapes=[pltpu.VMEM(efie_left.shape, BF16)] * 4
        + [
            pltpu.VMEM((4, 4, 128, 128), F32),
            pltpu.VMEM((per_dev, 64, 256), BF16),
            pltpu.SemaphoreType.DMA((4, steps)),
            pltpu.SemaphoreType.DMA((4, steps)),
        ],
        compiler_params=params,
        cost_estimate=pl.CostEstimate(flops=200_000_000, bytes_accessed=5_300_000, transcendentals=0),
        name="far",
    )(me_ref, block_ranks.T, x, efie_left, efie_right, dual_left, dual_right)

    def shift(k):
        return [(i, (i + k) % subs) for i in range(subs)]

    far_got = [far[0]] + [lax.ppermute(far[k], "sub", shift(k)) for k in (1, 2, 3)]

    mid, pair, other = pl.pallas_call(
        functools.partial(near_kernel, chunk),
        in_specs=[SMEM, SMEM, SMEM, VMEM] + [ANY] * 3,
        out_specs=[VMEM] * 3,
        out_shape=[struct((per_dev, 2, 8, 128))] * 3,
        scratch_shapes=[pltpu.VMEM(efie_near.shape, BF16)] * 2
        + [pltpu.VMEM((3 * per_dev, 2, 8, 128), F32), pltpu.SemaphoreType.DMA((2, steps))],
        compiler_params=params,
        cost_estimate=pl.CostEstimate(flops=200_000_000, bytes_accessed=4_600_000, transcendentals=0),
        name="near",
    )(me_ref, base, near_cols.T, x, efie_near, dual_near, far[0])
    count = lax.axis_size("cluster")
    within = [(i, i ^ 1) for i in range(count)]
    between = [(i, i + 1) for i in range(1, count - 1, 2)] + [(i + 1, i) for i in range(1, count - 1, 2)]
    got_pair = lax.ppermute(pair, "cluster", within)
    got_other = lax.ppermute(other, "cluster", between)

    cols = far_cols.reshape(-1)
    owner = cols // per_dev
    earlier = (owner[:, None] == owner[None, :]) & (jnp.arange(128)[None, :] < jnp.arange(128)[:, None])
    order = jnp.sum(earlier.astype(jnp.int32), axis=1)
    slot = jnp.broadcast_to((owner * 4 + order)[None, :], (8, 128))
    place = jnp.broadcast_to((order * 16 + cols % per_dev)[:, None], (128, 128))
    sent, *near = pl.pallas_call(
        send_kernel,
        in_specs=[VMEM] * 9,
        out_specs=[VMEM] * 5,
        out_shape=[struct((count * 17, 128))] + [struct((4, per_dev, 128))] * 4,
        compiler_params=small,
        name="send",
    )(slot, place, *far_got, *(v.reshape(per_dev * 16, 128) for v in (mid, got_pair, got_other)))
    near_got = [near[0]] + [lax.ppermute(near[k], "sub", shift(k)) for k in (1, 2, 3)]
    got = lax.all_to_all(sent.reshape(count * 17, 1, 128), "cluster", 0, 0, tiled=True)
    efie, dual = pl.pallas_call(
        sum_kernel,
        in_specs=[VMEM] * 5,
        out_specs=[VMEM] * 2,
        out_shape=[struct((per_dev, 2, 128), BF16)] * 2,
        compiler_params=small,
        name="total",
    )(got.reshape(count * 17, 128), *near_got)
    shape = (per_dev, 2, 1, 128)
    return efie.reshape(shape), dual.reshape(shape)


def solution(mesh):
    return jax.shard_map(
        per_device,
        mesh=mesh,
        in_specs=(
            P("cluster", None, None, None),
            P("cluster", None, None, "sub", None),
            P("cluster", None, None, "sub", None),
            P("cluster", None, None, "sub", None),
            P("cluster", None, None, "sub", None),
            P("cluster", None),
            P("cluster", None),
            P("cluster", "sub", None, None, None),
            P("cluster", "sub", None, None, None),
            P("cluster", "sub"),
        ),
        out_specs=(P("cluster", None, "sub", None), P("cluster", None, "sub", None)),
        check_vma=False,
    )
```

time: 70.9 us -> 60.5 us (0.85)
  the two profiles are of different devices: /device:TPU:127 before, /device:TPU:1 now
where the time goes in v2:
time: 60.5 us; the launch traced here: 60.2 us
  starting transfers between devices  27 us (45%)
  waiting for transfers between devices  18.5 us (31%)
  Pallas kernels  12.7 us (21%)
  local copies, waits for them, and re-layouts  1.14 us (2%)
  between operations  0.74 us (1%)
    all_to_all x1, starting transfers between devices, per_device(): lax.all_to_all(sent.reshape(count * 17, 1, 128), 'cluster', 0, 0, tiled=T...  13.7 us
    all_to_all x1, waiting for transfers between devices, per_device(): lax.all_to_all(sent.reshape(count * 17, 1, 128), 'cluster', 0, 0, tiled=T...  13.1 us
    pallas_call x1, Pallas kernels, per_device(): pl.pallas_call(functools.partial(far_kernel, chunk), in_specs=[SMEM, SMEM...  6.54 us
    ppermute x3, starting transfers between devices, per_device(): lax.ppermute(far[k], 'sub', shift(k))  5.72 us
    pallas_call x1, Pallas kernels, per_device(): pl.pallas_call(functools.partial(near_kernel, chunk), in_specs=[SMEM, SME...  4.05 us
    ppermute x1, starting transfers between devices, per_device(): got_other = lax.ppermute(other, 'cluster', between)  3.11 us
    ppermute x1, waiting for transfers between devices, per_device(): got_other = lax.ppermute(other, 'cluster', between)  2.97 us
    ppermute x3, starting transfers between devices, per_device(): lax.ppermute(near[k], 'sub', shift(k))  2.88 us
  transfers between devices with their start and end apart: 9, of which 5 were waited for; matrix products, arithmetic and copies ran while one was open for 1% of the time, Pallas kernels for 7%

profile of v2, /device:TPU:1, one launch (start us, length us, event | category | flops | bytes accessed | tf_op | source)
XLA Modules:
  0.0 60.2 jit_solution(18258379413025331744)
XLA Ops:
  0.6 6.5 %far.1 = (f32[4,128,128]{2,1,0:T(8,128)}, f32[4,128,128]{2,1,0:T(8,128)}, f32[4,128,128]{2,1,0:T(8,128)}, f32[4,128,128]{2,1,0:T(8,128)}) custom-call(s32[1]{0:T(128)} %bitcast.me_ref, s32[8,16]{1,0:T(8,128)} %bitcast.24, bf16[128,128]{1,0:T(8,128)(2,1)} %bitcast.22, bf16[16,8,2,16,128]{4,3,2,1,0:T(8,128)(2,1)} %le.1, bf16[16,8,2,16,128]{4,3,2,1,0:T(8,128)(2,1)} %re.1, ...), custom_call_target="tpu_custom_call" | custom-call | flops 200000000 | bytes 5300000 | tf_op jit(solution)/shard_map/far/pallas_call | solution.py:204
  7.2 2.1 %collective-permute-start = (f32[4,128,128]{2,1,0:T(8,128)}, f32[4,128,128]{2,1,0:T(8,128)S(1)}, u32[]{:S(2)}, u32[]{:S(2)}) collective-permute-start(f32[4,128,128]{2,1,0:T(8,128)} %get-tuple-element.17), channel_id=1, source_target_pairs={{0,1},{1,2},{2,3},{3,0},{4,5},{5,6},{6,7},{7,4},{8,9},{9,10},{10,1... | collective-permute-start | bytes 786440 | tf_op jit(solution)/shard_map/ppermute | solution.py:224
  9.3 2.4 %collective-permute-start.1 = (f32[4,128,128]{2,1,0:T(8,128)}, f32[4,128,128]{2,1,0:T(8,128)S(1)}, u32[]{:S(2)}, u32[]{:S(2)}) collective-permute-start(f32[4,128,128]{2,1,0:T(8,128)} %get-tuple-element.18), channel_id=1, source_target_pairs={{0,2},{1,3},{2,0},{3,1},{4,6},{5,7},{6,4},{7,5},{8,10},{9,11},{10,... | collective-permute-start | bytes 786440 | tf_op jit(solution)/shard_map/ppermute | solution.py:224
  11.8 1.2 %collective-permute-start.2 = (f32[4,128,128]{2,1,0:T(8,128)}, f32[4,128,128]{2,1,0:T(8,128)S(1)}, u32[]{:S(2)}, u32[]{:S(2)}) collective-permute-start(f32[4,128,128]{2,1,0:T(8,128)} %get-tuple-element.19), channel_id=1, source_target_pairs={{0,3},{1,0},{2,1},{3,2},{4,7},{5,4},{6,5},{7,6},{8,11},{9,8},{10,9... | collective-permute-start | bytes 786440 | tf_op jit(solution)/shard_map/ppermute | solution.py:224
  12.9 4.0 %near.1 = (f32[16,2,8,128]{3,2,1,0:T(8,128)}, f32[16,2,8,128]{3,2,1,0:T(8,128)}, f32[16,2,8,128]{3,2,1,0:T(8,128)}) custom-call(s32[1]{0:T(128)} %bitcast.me_ref, s32[1]{0:T(128)} %bitcast.3.base_ref, s32[2,16]{1,0:T(2,128)} %bitcast.25, bf16[128,128]{1,0:T(8,128)(2,1)} %bitcast.23, bf16[16,2,2,128,128]{4,3,2,1,0:T(8,128)(2,1)} %de.1, ...), custom_call_target="tpu_custom_call" | custom-call | flops 200000000 | bytes 4600000 | tf_op jit(solution)/shard_map/near/pallas_call | solution.py:226
  17.0 1.6 %collective-permute-start.3 = (f32[16,2,8,128]{3,2,1,0:T(8,128)}, f32[16,2,8,128]{3,2,1,0:T(8,128)S(1)}, u32[]{:S(2)}, u32[]{:S(2)}) collective-permute-start(f32[16,2,8,128]{3,2,1,0:T(8,128)} %get-tuple-element.21), channel_id=1, source_target_pairs={{0,4},{4,0},{8,12},{12,8},{16,20},{20,16},{24,28},{28,24},{32,36},... | collective-permute-start | bytes 393224 | tf_op jit(solution)/shard_map/ppermute | solution.py:240
  18.6 3.1 %collective-permute-start.4 = (f32[16,2,8,128]{3,2,1,0:T(8,128)}, f32[16,2,8,128]{3,2,1,0:T(8,128)S(1)}, u32[]{:S(2)}, u32[]{:S(2)}) collective-permute-start(f32[16,2,8,128]{3,2,1,0:T(8,128)} %get-tuple-element.22), channel_id=1, source_target_pairs={{4,8},{12,16},{20,24},{28,32},{36,40},{44,48},{52,56},{60,64},{68,... | collective-permute-start | bytes 393224 | tf_op jit(solution)/shard_map/ppermute | solution.py:241
  21.7 0.1 copy.22
  21.8 0.1 reshape.131
  21.9 0.2 convert_reduce_fusion
  22.1 3.0 %collective-permute-done.4 = f32[16,2,8,128]{3,2,1,0:T(8,128)S(1)} collective-permute-done((f32[16,2,8,128]{3,2,1,0:T(8,128)}, f32[16,2,8,128]{3,2,1,0:T(8,128)S(1)}, u32[]{:S(2)}, u32[]{:S(2)}) %collective-permute-start.4) | collective-permute-done | bytes 131104 | tf_op jit(solution)/shard_map/ppermute | solution.py:241
  25.1 0.0 collective-permute-done.b
  25.1 0.1 broadcast_in_dim.5.cols_ref
  25.2 0.9 %copy-done.1 = f32[16,2,8,128]{3,2,1,0:T(8,128)S(1)} copy-done((f32[16,2,8,128]{3,2,1,0:T(8,128)S(1)}, f32[16,2,8,128]{3,2,1,0:T(8,128)}, u32[]{:S(2)}) %copy-start.1) | copy-done | bytes 131096
  26.1 1.1 %send.1 = (f32[1088,128]{1,0:T(8,128)}, f32[4,16,128]{2,1,0:T(8,128)S(1)}, f32[4,16,128]{2,1,0:T(8,128)S(1)}, f32[4,16,128]{2,1,0:T(8,128)S(1)}, f32[4,16,128]{2,1,0:T(8,128)S(1)}) custom-call(s32[8,128]{1,0:T(8,128)S(1)} %broadcast_in_dim.4.slot_ref, s32[128,128]{1,0:T(8,128)S(1)} %broadcast_in_dim.5.cols_ref, f32[4,128,128]{2,1,0:T(8,128)S(1)} %copy-done, ...), custom_call_target="tpu_custom_call" | custom-call | tf_op jit(solution)/shard_map/send/pallas_call | solution.py:249
  27.2 13.7 %all-to-all-start = ((f32[1088,1,128]{2,1,0:T(1,128)}), f32[1088,1,128]{2,1,0:T(1,128)S(1)}, u32[]{:S(2)}, u32[]{:S(2)}) async-start(f32[1088,1,128]{2,1,0:T(1,128)} %bitcast.9), calls=%async_computation | async-start | bytes 1114112 | tf_op jit(solution)/shard_map/all_to_all | solution.py:258
  40.9 0.4 collective-permute-start.5
  41.3 0.6 collective-permute-start.6
  41.9 1.9 %collective-permute-start.7 = (f32[4,16,128]{2,1,0:T(8,128)S(1)}, f32[4,16,128]{2,1,0:T(8,128)S(1)}, u32[]{:S(2)}, u32[]{:S(2)}) collective-permute-start(f32[4,16,128]{2,1,0:T(8,128)S(1)} %get-tuple-element.27), channel_id=1, source_target_pairs={{0,3},{1,0},{2,1},{3,2},{4,7},{5,4},{6,5},{7,6},{8,11},{9,8},{10,9... | collective-permute-start | bytes 98312 | tf_op jit(solution)/shard_map/ppermute | solution.py:257
  43.8 1.5 %collective-permute-done.5.nb = f32[4,16,128]{2,1,0:T(8,128)S(1)} collective-permute-done((f32[4,16,128]{2,1,0:T(8,128)S(1)}, f32[4,16,128]{2,1,0:T(8,128)S(1)}, u32[]{:S(2)}, u32[]{:S(2)}) %collective-permute-start.5) | collective-permute-done | bytes 32800 | tf_op jit(solution)/shard_map/ppermute | solution.py:257
  45.3 0.3 collective-permute-done.6.nc
  45.6 0.6 %collective-permute-done.7.nd = f32[4,16,128]{2,1,0:T(8,128)S(1)} collective-permute-done((f32[4,16,128]{2,1,0:T(8,128)S(1)}, f32[4,16,128]{2,1,0:T(8,128)S(1)}, u32[]{:S(2)}, u32[]{:S(2)}) %collective-permute-start.7) | collective-permute-done | bytes 32800 | tf_op jit(solution)/shard_map/ppermute | solution.py:257
  46.2 13.1 %all-to-all-done = f32[1088,1,128]{2,1,0:T(1,128)S(1)} async-done(((f32[1088,1,128]{2,1,0:T(1,128)}), f32[1088,1,128]{2,1,0:T(1,128)S(1)}, u32[]{:S(2)}, u32[]{:S(2)}) %all-to-all-start) | async-done | bytes 557088 | tf_op jit(solution)/shard_map/all_to_all | solution.py:258
  59.3 0.9 %total.1 = (bf16[16,2,128]{2,1,0:T(2,128)(2,1)}, bf16[16,2,128]{2,1,0:T(2,128)(2,1)}) custom-call(f32[1088,128]{1,0:T(8,128)S(1)} %bitcast.18, f32[4,16,128]{2,1,0:T(8,128)S(1)} %get-tuple-element.24.na, f32[4,16,128]{2,1,0:T(8,128)S(1)} %collective-permute-done.5.nb, f32[4,16,128]{2,1,0:T(8,128)S(1)} %collective-permute-done.6.nc, ...), custom_call_target="tpu_custom_call" | custom-call | tf_op jit(solution)/shard_map/total/pallas_call | solution.py:259
  (11 shorter events, 0.0 us)
Async XLA Ops:
  7.2 17.9 %collective-permute-start = (f32[4,128,128]{2,1,0:T(8,128)}, f32[4,128,128]{2,1,0:T(8,128)S(1)}, u32[]{:S(2)}, u32[]{:S(2)}) collective-permute-start(f32[4,128,128]{2,1,0:T(8,128)} %get-tuple-element.17), channel_id=1, source_target_pairs={{0,1},{1,2},{2,3},{3,0},{4,5},{5,6},{6,7},{7,4},{8,9},{9,10},{10,1... | collective-permute-start | bytes 786440 | tf_op jit(solution)/shard_map/ppermute | solution.py:224
  9.3 15.8 %collective-permute-start.1 = (f32[4,128,128]{2,1,0:T(8,128)}, f32[4,128,128]{2,1,0:T(8,128)S(1)}, u32[]{:S(2)}, u32[]{:S(2)}) collective-permute-start(f32[4,128,128]{2,1,0:T(8,128)} %get-tuple-element.18), channel_id=1, source_target_pairs={{0,2},{1,3},{2,0},{3,1},{4,6},{5,7},{6,4},{7,5},{8,10},{9,11},{10,... | collective-permute-start | bytes 786440 | tf_op jit(solution)/shard_map/ppermute | solution.py:224
  11.8 13.3 %collective-permute-start.2 = (f32[4,128,128]{2,1,0:T(8,128)}, f32[4,128,128]{2,1,0:T(8,128)S(1)}, u32[]{:S(2)}, u32[]{:S(2)}) collective-permute-start(f32[4,128,128]{2,1,0:T(8,128)} %get-tuple-element.19), channel_id=1, source_target_pairs={{0,3},{1,0},{2,1},{3,2},{4,7},{5,4},{6,5},{7,6},{8,11},{9,8},{10,9... | collective-permute-start | bytes 786440 | tf_op jit(solution)/shard_map/ppermute | solution.py:224
  12.9 8.8 %copy-start.2 = (s32[16,8]{0,1:T(8,128)S(1)}, s32[16,8]{0,1:T(8,128)}, u32[]{:S(2)}) copy-start(s32[16,8]{0,1:T(8,128)} %param.16) | copy-start | bytes 1540
  12.9 12.2 %copy-start = (f32[4,128,128]{2,1,0:T(8,128)S(1)}, f32[4,128,128]{2,1,0:T(8,128)}, u32[]{:S(2)}) copy-start(f32[4,128,128]{2,1,0:T(8,128)} %get-tuple-element.16.after.a) | copy-start | bytes 786436
  17.0 5.1 %collective-permute-start.3 = (f32[16,2,8,128]{3,2,1,0:T(8,128)}, f32[16,2,8,128]{3,2,1,0:T(8,128)S(1)}, u32[]{:S(2)}, u32[]{:S(2)}) collective-permute-start(f32[16,2,8,128]{3,2,1,0:T(8,128)} %get-tuple-element.21), channel_id=1, source_target_pairs={{0,4},{4,0},{8,12},{12,8},{16,20},{20,16},{24,28},{28,24},{32,36},... | collective-permute-start | bytes 393224 | tf_op jit(solution)/shard_map/ppermute | solution.py:240
  18.6 6.5 %collective-permute-start.4 = (f32[16,2,8,128]{3,2,1,0:T(8,128)}, f32[16,2,8,128]{3,2,1,0:T(8,128)S(1)}, u32[]{:S(2)}, u32[]{:S(2)}) collective-permute-start(f32[16,2,8,128]{3,2,1,0:T(8,128)} %get-tuple-element.22), channel_id=1, source_target_pairs={{4,8},{12,16},{20,24},{28,32},{36,40},{44,48},{52,56},{60,64},{68,... | collective-permute-start | bytes 393224 | tf_op jit(solution)/shard_map/ppermute | solution.py:241
  25.2 0.9 %copy-start.1 = (f32[16,2,8,128]{3,2,1,0:T(8,128)S(1)}, f32[16,2,8,128]{3,2,1,0:T(8,128)}, u32[]{:S(2)}) copy-start(f32[16,2,8,128]{3,2,1,0:T(8,128)} %get-tuple-element.20) | copy-start | bytes 393220
  27.2 32.1 %all-to-all-start = ((f32[1088,1,128]{2,1,0:T(1,128)}), f32[1088,1,128]{2,1,0:T(1,128)S(1)}, u32[]{:S(2)}, u32[]{:S(2)}) async-start(f32[1088,1,128]{2,1,0:T(1,128)} %bitcast.9), calls=%async_computation | async-start | bytes 1114112 | tf_op jit(solution)/shard_map/all_to_all | solution.py:258
  40.9 4.3 %collective-permute-start.5 = (f32[4,16,128]{2,1,0:T(8,128)S(1)}, f32[4,16,128]{2,1,0:T(8,128)S(1)}, u32[]{:S(2)}, u32[]{:S(2)}) collective-permute-start(f32[4,16,128]{2,1,0:T(8,128)S(1)} %get-tuple-element.25), channel_id=1, source_target_pairs={{0,1},{1,2},{2,3},{3,0},{4,5},{5,6},{6,7},{7,4},{8,9},{9,10},{10,1... | collective-permute-start | bytes 98312 | tf_op jit(solution)/shard_map/ppermute | solution.py:257
  41.3 4.3 %collective-permute-start.6 = (f32[4,16,128]{2,1,0:T(8,128)S(1)}, f32[4,16,128]{2,1,0:T(8,128)S(1)}, u32[]{:S(2)}, u32[]{:S(2)}) collective-permute-start(f32[4,16,128]{2,1,0:T(8,128)S(1)} %get-tuple-element.26), channel_id=1, source_target_pairs={{0,2},{1,3},{2,0},{3,1},{4,6},{5,7},{6,4},{7,5},{8,10},{9,11},{10,... | collective-permute-start | bytes 98312 | tf_op jit(solution)/shard_map/ppermute | solution.py:257
  41.9 4.3 %collective-permute-start.7 = (f32[4,16,128]{2,1,0:T(8,128)S(1)}, f32[4,16,128]{2,1,0:T(8,128)S(1)}, u32[]{:S(2)}, u32[]{:S(2)}) collective-permute-start(f32[4,16,128]{2,1,0:T(8,128)S(1)} %get-tuple-element.27), channel_id=1, source_target_pairs={{0,3},{1,0},{2,1},{3,2},{4,7},{5,4},{6,5},{7,6},{8,11},{9,8},{10,9... | collective-permute-start | bytes 98312 | tf_op jit(solution)/shard_map/ppermute | solution.py:257

commit v3 on v2

--- a/solution.py
+++ b/solution.py
@@ -66,26 +66,39 @@
         both = [jnp.concatenate(rows, axis=0), jnp.concatenate(turned, axis=0)]
         return jnp.concatenate(both, axis=1).astype(BF16)
 
-    for i in range(steps):
-        for copy in loads(i):
+    def coefs(cluster):
+        u = jnp.concatenate([planes(ble, cluster, 1), planes(bld, cluster, 1)], axis=0)
+        return dot(lhs[cluster], u, ((1,), (1,)))
+
+    def mixed(cluster, coef):
+        ranks = jnp.zeros((8, 128), jnp.int32)
+        for f in range(8):
+            ranks = jnp.where(lane // 16 == f, rank_ref[f, cluster], ranks)
+        keep = (lane // 16 == sublane) & (me * 16 + lane % 16 < ranks)
+        return jnp.concatenate([spread(coef[:, :128], keep), spread(coef[:, 128:], keep)], axis=0)
+
+    def results(cluster, mix):
+        v = jnp.concatenate([planes(bre, cluster, 0), planes(brd, cluster, 0)], axis=1)
+        far = dot(mix, v)
+        for op in range(2):
+            for k in range(4):
+                for q in range(2):
+                    start = op * 64 + k * 16 + q * 8
+                    made[k, op * 2 + q, cluster * 8 : cluster * 8 + 8, :] = far[
+                        start : start + 8, op * 128 : op * 128 + 128
+                    ]
+
+    for i in range(steps):
+        copies = loads(i)
+        these = range(i * chunk, i * chunk + chunk)
+        for copy in copies[:2]:
             copy.wait()
-        for cluster in range(i * chunk, i * chunk + chunk):
-            ranks = jnp.zeros((8, 128), jnp.int32)
-            for f in range(8):
-                ranks = jnp.where(lane // 16 == f, rank_ref[f, cluster], ranks)
-            keep = (lane // 16 == sublane) & (me * 16 + lane % 16 < ranks)
-            u = jnp.concatenate([planes(ble, cluster, 1), planes(bld, cluster, 1)], axis=0)
-            coef = dot(lhs[cluster], u, ((1,), (1,)))
-            mixed = jnp.concatenate([spread(coef[:, :128], keep), spread(coef[:, 128:], keep)], axis=0)
-            v = jnp.concatenate([planes(bre, cluster, 0), planes(brd, cluster, 0)], axis=1)
-            far = dot(mixed, v)
-            for op in range(2):
-                for k in range(4):
-                    for q in range(2):
-                        start = op * 64 + k * 16 + q * 8
-                        made[k, op * 2 + q, cluster * 8 : cluster * 8 + 8, :] = far[
-                            start : start + 8, op * 128 : op * 128 + 128
-                        ]
+        coef = [coefs(cluster) for cluster in these]
+        mix = [mixed(cluster, c) for cluster, c in zip(these, coef)]
+        for copy in copies[2:]:
+            copy.wait()
+        for cluster, m in zip(these, mix):
+            results(cluster, m)
         for copy in stores(i):
             copy.start()
     for i in range(steps):
@@ -112,13 +125,15 @@
     for i in range(steps):
         for copy in loads(i):
             copy.wait()
-        for cluster in range(i * chunk, i * chunk + chunk):
-            for slot in range(2):
-                d = jnp.concatenate([r[cluster, slot].reshape(256, 128) for r in (bde, bdd)], axis=1)
-                out = dot(lhs[cluster], d)
-                target = col_ref[slot, cluster] - base
-                window[target, 0] += out[:, :128]
-                window[target, 1] += out[:, 128:]
+        these = [(cluster, slot) for cluster in range(i * chunk, i * chunk + chunk) for slot in range(2)]
+        outs = []
+        for cluster, slot in these:
+            d = jnp.concatenate([r[cluster, slot].reshape(256, 128) for r in (bde, bdd)], axis=1)
+            outs.append(dot(lhs[cluster], d))
+        for (cluster, slot), out in zip(these, outs):
+            target = col_ref[slot, cluster] - base
+            window[target, 0] += out[:, :128]
+            window[target, 1] += out[:, 128:]
     odd = (base // 16) & 1 == 0
     mid[...] = window[16:32]
     pair[...] = window[pl.ds(jnp.where(odd, 0, 32), 16)]
@@ -130,7 +145,7 @@
     return high, (value - high.astype(F32)).astype(BF16)
 
 
-def send_kernel(slot_ref, cols_ref, a, b, c, d, mid, pair, other, out, *near):
+def send_kernel(slot_ref, cols_ref, a, b, c, d, after, passed, out, passed_out):
     slot = jnp.broadcast_to(slot_ref[0:1, :], (64, 128))
     target = iota((64, 128), 0)
     picks = [jnp.where(slot == target * 4 + k, 1.0, 0.0).astype(BF16) for k in range(4)]
@@ -149,6 +164,9 @@
     here = jnp.where(slot // 4 == target, 1.0, 0.0).astype(BF16)
     place = jnp.where(cols_ref[...] == iota((128, 128), 1), 1.0, 0.0).astype(BF16)
     out[pl.ds(16, 64, stride=17), :] = dot(here, place)
+
+
+def merge_kernel(mid, pair, other, *near):
     for k in range(4):
         for j in range(4):
             rows = pl.ds((j // 2) * 8 + k * 2 + j % 2, 16, stride=16)
@@ -221,7 +239,11 @@
     def shift(k):
         return [(i, (i + k) % subs) for i in range(subs)]
 
-    far_got = [far[0]] + [lax.ppermute(far[k], "sub", shift(k)) for k in (1, 2, 3)]
+    def over_sub(parts):
+        one, three, two = (lax.ppermute(parts[k], "sub", shift(k)) for k in (1, 3, 2))
+        return [parts[0], one, two, three]
+
+    far_got = over_sub(far)
 
     mid, pair, other = pl.pallas_call(
         functools.partial(near_kernel, chunk),
@@ -246,15 +268,24 @@
     order = jnp.sum(earlier.astype(jnp.int32), axis=1)
     slot = jnp.broadcast_to((owner * 4 + order)[None, :], (8, 128))
     place = jnp.broadcast_to((order * 16 + cols % per_dev)[:, None], (128, 128))
-    sent, *near = pl.pallas_call(
+    sent, got_pair = pl.pallas_call(
         send_kernel,
-        in_specs=[VMEM] * 9,
-        out_specs=[VMEM] * 5,
-        out_shape=[struct((count * 17, 128))] + [struct((4, per_dev, 128))] * 4,
+        in_specs=[VMEM] * 6 + [ANY] * 2,
+        out_specs=[VMEM, ANY],
+        out_shape=[struct((count * 17, 128)), struct(pair.shape)],
+        input_output_aliases={7: 1},
         compiler_params=small,
         name="send",
-    )(slot, place, *far_got, *(v.reshape(per_dev * 16, 128) for v in (mid, got_pair, got_other)))
-    near_got = [near[0]] + [lax.ppermute(near[k], "sub", shift(k)) for k in (1, 2, 3)]
+    )(slot, place, *far_got, got_other, got_pair)
+    near = pl.pallas_call(
+        merge_kernel,
+        in_specs=[VMEM] * 3,
+        out_specs=[VMEM] * 4,
+        out_shape=[struct((4, per_dev, 128))] * 4,
+        compiler_params=small,
+        name="merge",
+    )(*(v.reshape(per_dev * 16, 128) for v in (mid, got_pair, got_other)))
+    near_got = over_sub(near)
     got = lax.all_to_all(sent.reshape(count * 17, 1, 128), "cluster", 0, 0, tiled=True)
     efie, dual = pl.pallas_call(
         sum_kernel,

time: 60.5 us -> 56.7 us (0.937)
  Pallas kernels: 12.7 us -> 11.1 us
  waiting for transfers between devices: 18.5 us -> 17.1 us
  local copies, waits for them, and re-layouts: 1.14 us -> 0.25 us
    ppermute x1, starting transfers between devices: 3.11 us -> 4.74 us  [per_device(): got_other = lax.ppermute(other, 'cluster', between)]
    pallas_call x1, Pallas kernels: 6.54 us -> 4.92 us  [per_device(): pl.pallas_call(functools.partial(far_kernel, chunk), in_specs=[SMEM, SMEM...]
    ppermute x1, starting transfers between devices: 1.6 us -> 0.09 us  [per_device(): got_pair = lax.ppermute(pair, 'cluster', within)]
    unnamed x7, local copies, waits for them, and re-layouts: 0.98 us -> 0.08 us
    all_to_all x1, starting transfers between devices: 13.7 us -> 12.9 us  [per_device(): lax.all_to_all(sent.reshape(count * 17, 1, 128), 'cluster', 0, 0, tiled=T...]
    ppermute x6, starting transfers between devices: 8.6 us -> 9.24 us  [over_sub(): lax.ppermute(parts[k], 'sub', shift(k))]
    ppermute x6, waiting for transfers between devices: 2.4 us -> 1.77 us  [over_sub(): lax.ppermute(parts[k], 'sub', shift(k))]
    ppermute x1, waiting for transfers between devices: 2.97 us -> 2.36 us  [per_device(): got_other = lax.ppermute(other, 'cluster', between)]
where the time goes in v3:
time: 56.7 us; the launch traced here: 56.4 us
  starting transfers between devices  27 us (48%)
  waiting for transfers between devices  17.1 us (30%)
  Pallas kernels  11.1 us (20%)
  between operations  0.76 us (1%)
    all_to_all x1, waiting for transfers between devices, per_device(): lax.all_to_all(sent.reshape(count * 17, 1, 128), 'cluster', 0, 0, tiled=T...  13 us
    all_to_all x1, starting transfers between devices, per_device(): lax.all_to_all(sent.reshape(count * 17, 1, 128), 'cluster', 0, 0, tiled=T...  12.9 us
    ppermute x6, starting transfers between devices, over_sub(): lax.ppermute(parts[k], 'sub', shift(k))  9.24 us
    pallas_call x1, Pallas kernels, per_device(): pl.pallas_call(functools.partial(far_kernel, chunk), in_specs=[SMEM, SMEM...  4.92 us
    ppermute x1, starting transfers between devices, per_device(): got_other = lax.ppermute(other, 'cluster', between)  4.74 us
    pallas_call x1, Pallas kernels, per_device(): pl.pallas_call(functools.partial(near_kernel, chunk), in_specs=[SMEM, SME...  4.06 us
    ppermute x1, waiting for transfers between devices, per_device(): got_other = lax.ppermute(other, 'cluster', between)  2.36 us
    ppermute x6, waiting for transfers between devices, over_sub(): lax.ppermute(parts[k], 'sub', shift(k))  1.77 us
  transfers between devices with their start and end apart: 9, of which 5 were waited for; matrix products, arithmetic and copies ran while one was open for 1% of the time, Pallas kernels for 7%

profile of v3, /device:TPU:1, one launch (start us, length us, event | category | flops | bytes accessed | tf_op | source)
XLA Modules:
  0.0 56.4 jit_solution(186000977001735115)
XLA Ops:
  0.6 4.9 %far.1 = (f32[4,128,128]{2,1,0:T(8,128)}, f32[4,128,128]{2,1,0:T(8,128)}, f32[4,128,128]{2,1,0:T(8,128)}, f32[4,128,128]{2,1,0:T(8,128)}) custom-call(s32[1]{0:T(128)} %bitcast.me_ref, s32[8,16]{1,0:T(8,128)} %bitcast.24, bf16[128,128]{1,0:T(8,128)(2,1)} %bitcast.22, bf16[16,8,2,16,128]{4,3,2,1,0:T(8,128)(2,1)} %le.1, bf16[16,8,2,16,128]{4,3,2,1,0:T(8,128)(2,1)} %re.1, ...), custom_call_target="tpu_custom_call" | custom-call | flops 200000000 | bytes 5300000 | tf_op jit(solution)/shard_map/far/pallas_call | solution.py:222
  5.6 2.1 %collective-permute-start = (f32[4,128,128]{2,1,0:T(8,128)}, f32[4,128,128]{2,1,0:T(8,128)S(1)}, u32[]{:S(2)}, u32[]{:S(2)}) collective-permute-start(f32[4,128,128]{2,1,0:T(8,128)} %get-tuple-element.18), channel_id=1, source_target_pairs={{0,1},{1,2},{2,3},{3,0},{4,5},{5,6},{6,7},{7,4},{8,9},{9,10},{10,1... | collective-permute-start | bytes 786440 | tf_op jit(solution)/shard_map/ppermute | solution.py:243
  7.7 2.4 %collective-permute-start.1 = (f32[4,128,128]{2,1,0:T(8,128)}, f32[4,128,128]{2,1,0:T(8,128)S(1)}, u32[]{:S(2)}, u32[]{:S(2)}) collective-permute-start(f32[4,128,128]{2,1,0:T(8,128)} %get-tuple-element.19), channel_id=1, source_target_pairs={{0,2},{1,3},{2,0},{3,1},{4,6},{5,7},{6,4},{7,5},{8,10},{9,11},{10,... | collective-permute-start | bytes 786440 | tf_op jit(solution)/shard_map/ppermute | solution.py:243
  10.1 1.2 %collective-permute-start.2 = (f32[4,128,128]{2,1,0:T(8,128)}, f32[4,128,128]{2,1,0:T(8,128)S(1)}, u32[]{:S(2)}, u32[]{:S(2)}) collective-permute-start(f32[4,128,128]{2,1,0:T(8,128)} %get-tuple-element.20), channel_id=1, source_target_pairs={{0,3},{1,0},{2,1},{3,2},{4,7},{5,4},{6,5},{7,6},{8,11},{9,8},{10,9... | collective-permute-start | bytes 786440 | tf_op jit(solution)/shard_map/ppermute | solution.py:243
  11.3 4.1 %near.1 = (f32[16,2,8,128]{3,2,1,0:T(8,128)}, f32[16,2,8,128]{3,2,1,0:T(8,128)}, f32[16,2,8,128]{3,2,1,0:T(8,128)}) custom-call(s32[1]{0:T(128)} %bitcast.me_ref, s32[1]{0:T(128)} %bitcast.3.base_ref, s32[2,16]{1,0:T(2,128)} %bitcast.25, bf16[128,128]{1,0:T(8,128)(2,1)} %bitcast.23, bf16[16,2,2,128,128]{4,3,2,1,0:T(8,128)(2,1)} %de.1, ...), custom_call_target="tpu_custom_call" | custom-call | flops 200000000 | bytes 4600000 | tf_op jit(solution)/shard_map/near/pallas_call | solution.py:248
  15.4 4.7 %collective-permute-start.3 = (f32[16,2,8,128]{3,2,1,0:T(8,128)}, f32[16,2,8,128]{3,2,1,0:T(8,128)S(1)}, u32[]{:S(2)}, u32[]{:S(2)}) collective-permute-start(f32[16,2,8,128]{3,2,1,0:T(8,128)} %get-tuple-element.21), channel_id=1, source_target_pairs={{4,8},{12,16},{20,24},{28,32},{36,40},{44,48},{52,56},{60,64},{68,... | collective-permute-start | bytes 393224 | tf_op jit(solution)/shard_map/ppermute | solution.py:263
  20.1 0.1 collective-permute-start.4
  20.2 0.1 copy.23
  20.3 0.1 reshape.131
  20.4 0.2 convert_reduce_fusion
  20.6 2.4 %collective-permute-done.3.after = f32[16,2,8,128]{3,2,1,0:T(8,128)S(1)} collective-permute-done((f32[16,2,8,128]{3,2,1,0:T(8,128)}, f32[16,2,8,128]{3,2,1,0:T(8,128)S(1)}, u32[]{:S(2)}, u32[]{:S(2)}) %collective-permute-start.3) | collective-permute-done | bytes 131104 | tf_op jit(solution)/shard_map/ppermute | solution.py:263
  23.0 0.0 collective-permute-done.4.passed
  23.0 0.1 broadcast_in_dim.5.cols_ref
  23.1 1.1 %send.1 = (f32[1088,128]{1,0:T(8,128)}, f32[16,2,8,128]{3,2,1,0:T(8,128)S(1)}) custom-call(s32[8,128]{1,0:T(8,128)S(1)} %broadcast_in_dim.4.slot_ref, s32[128,128]{1,0:T(8,128)S(1)} %broadcast_in_dim.5.cols_ref, f32[4,128,128]{2,1,0:T(8,128)S(1)} %copy-done, f32[4,128,128]{2,1,0:T(8,128)S(1)} %collective-permute-done.b, ...), custom_call_target="tpu_custom_call", output_to_operand_aliasing={{1}: (7, {})} | custom-call | tf_op jit(solution)/shard_map/send/pallas_call | solution.py:271
  24.2 12.9 %all-to-all-start = ((f32[1088,1,128]{2,1,0:T(1,128)}), f32[1088,1,128]{2,1,0:T(1,128)S(1)}, u32[]{:S(2)}, u32[]{:S(2)}) async-start(f32[1088,1,128]{2,1,0:T(1,128)} %bitcast.6), calls=%async_computation | async-start | bytes 1114112 | tf_op jit(solution)/shard_map/all_to_all | solution.py:289
  37.1 0.1 merge.1
  37.2 0.4 collective-permute-start.5
  37.6 1.8 %collective-permute-start.6 = (f32[4,16,128]{2,1,0:T(8,128)S(1)}, f32[4,16,128]{2,1,0:T(8,128)S(1)}, u32[]{:S(2)}, u32[]{:S(2)}) collective-permute-start(f32[4,16,128]{2,1,0:T(8,128)S(1)} %get-tuple-element.28), channel_id=1, source_target_pairs={{0,2},{1,3},{2,0},{3,1},{4,6},{5,7},{6,4},{7,5},{8,10},{9,11},{10,... | collective-permute-start | bytes 98312 | tf_op jit(solution)/shard_map/ppermute | solution.py:243
  39.4 1.3 %collective-permute-start.7 = (f32[4,16,128]{2,1,0:T(8,128)S(1)}, f32[4,16,128]{2,1,0:T(8,128)S(1)}, u32[]{:S(2)}, u32[]{:S(2)}) collective-permute-start(f32[4,16,128]{2,1,0:T(8,128)S(1)} %get-tuple-element.29), channel_id=1, source_target_pairs={{0,3},{1,0},{2,1},{3,2},{4,7},{5,4},{6,5},{7,6},{8,11},{9,8},{10,9... | collective-permute-start | bytes 98312 | tf_op jit(solution)/shard_map/ppermute | solution.py:243
  40.7 0.8 %collective-permute-done.5.nb = f32[4,16,128]{2,1,0:T(8,128)S(1)} collective-permute-done((f32[4,16,128]{2,1,0:T(8,128)S(1)}, f32[4,16,128]{2,1,0:T(8,128)S(1)}, u32[]{:S(2)}, u32[]{:S(2)}) %collective-permute-start.5) | collective-permute-done | bytes 32800 | tf_op jit(solution)/shard_map/ppermute | solution.py:243
  41.5 0.5 collective-permute-done.6.nc
  42.0 0.5 collective-permute-done.7.nd
  42.5 13.0 %all-to-all-done = f32[1088,1,128]{2,1,0:T(1,128)S(1)} async-done(((f32[1088,1,128]{2,1,0:T(1,128)}), f32[1088,1,128]{2,1,0:T(1,128)S(1)}, u32[]{:S(2)}, u32[]{:S(2)}) %all-to-all-start) | async-done | bytes 557088 | tf_op jit(solution)/shard_map/all_to_all | solution.py:289
  55.4 0.9 %total.1 = (bf16[16,2,128]{2,1,0:T(2,128)(2,1)}, bf16[16,2,128]{2,1,0:T(2,128)(2,1)}) custom-call(f32[1088,128]{1,0:T(8,128)S(1)} %bitcast.18, f32[4,16,128]{2,1,0:T(8,128)S(1)} %get-tuple-element.26.na, f32[4,16,128]{2,1,0:T(8,128)S(1)} %collective-permute-done.5.nb, f32[4,16,128]{2,1,0:T(8,128)S(1)} %collective-permute-done.6.nc, ...), custom_call_target="tpu_custom_call" | custom-call | tf_op jit(solution)/shard_map/total/pallas_call | solution.py:290
  (12 shorter events, 0.0 us)
Async XLA Ops:
  5.6 17.4 %collective-permute-start = (f32[4,128,128]{2,1,0:T(8,128)}, f32[4,128,128]{2,1,0:T(8,128)S(1)}, u32[]{:S(2)}, u32[]{:S(2)}) collective-permute-start(f32[4,128,128]{2,1,0:T(8,128)} %get-tuple-element.18), channel_id=1, source_target_pairs={{0,1},{1,2},{2,3},{3,0},{4,5},{5,6},{6,7},{7,4},{8,9},{9,10},{10,1... | collective-permute-start | bytes 786440 | tf_op jit(solution)/shard_map/ppermute | solution.py:243
  7.7 15.3 %collective-permute-start.1 = (f32[4,128,128]{2,1,0:T(8,128)}, f32[4,128,128]{2,1,0:T(8,128)S(1)}, u32[]{:S(2)}, u32[]{:S(2)}) collective-permute-start(f32[4,128,128]{2,1,0:T(8,128)} %get-tuple-element.19), channel_id=1, source_target_pairs={{0,2},{1,3},{2,0},{3,1},{4,6},{5,7},{6,4},{7,5},{8,10},{9,11},{10,... | collective-permute-start | bytes 786440 | tf_op jit(solution)/shard_map/ppermute | solution.py:243
  10.1 12.8 %collective-permute-start.2 = (f32[4,128,128]{2,1,0:T(8,128)}, f32[4,128,128]{2,1,0:T(8,128)S(1)}, u32[]{:S(2)}, u32[]{:S(2)}) collective-permute-start(f32[4,128,128]{2,1,0:T(8,128)} %get-tuple-element.20), channel_id=1, source_target_pairs={{0,3},{1,0},{2,1},{3,2},{4,7},{5,4},{6,5},{7,6},{8,11},{9,8},{10,9... | collective-permute-start | bytes 786440 | tf_op jit(solution)/shard_map/ppermute | solution.py:243
  11.3 8.9 %copy-start.2 = (s32[16,8]{0,1:T(8,128)S(1)}, s32[16,8]{0,1:T(8,128)}, u32[]{:S(2)}) copy-start(s32[16,8]{0,1:T(8,128)} %param.16) | copy-start | bytes 1540
  11.3 11.8 %copy-start = (f32[4,128,128]{2,1,0:T(8,128)S(1)}, f32[4,128,128]{2,1,0:T(8,128)}, u32[]{:S(2)}) copy-start(f32[4,128,128]{2,1,0:T(8,128)} %get-tuple-element.17.after.a) | copy-start | bytes 786436
  15.4 21.7 %copy-start.1 = (f32[16,2,8,128]{3,2,1,0:T(8,128)S(1)}, f32[16,2,8,128]{3,2,1,0:T(8,128)}, u32[]{:S(2)}) copy-start(f32[16,2,8,128]{3,2,1,0:T(8,128)} %get-tuple-element.24) | copy-start | bytes 393220
  15.4 7.6 %collective-permute-start.3 = (f32[16,2,8,128]{3,2,1,0:T(8,128)}, f32[16,2,8,128]{3,2,1,0:T(8,128)S(1)}, u32[]{:S(2)}, u32[]{:S(2)}) collective-permute-start(f32[16,2,8,128]{3,2,1,0:T(8,128)} %get-tuple-element.21), channel_id=1, source_target_pairs={{4,8},{12,16},{20,24},{28,32},{36,40},{44,48},{52,56},{60,64},{68,... | collective-permute-start | bytes 393224 | tf_op jit(solution)/shard_map/ppermute | solution.py:263
  20.1 2.9 %collective-permute-start.4 = (f32[16,2,8,128]{3,2,1,0:T(8,128)}, f32[16,2,8,128]{3,2,1,0:T(8,128)S(1)}, u32[]{:S(2)}, u32[]{:S(2)}) collective-permute-start(f32[16,2,8,128]{3,2,1,0:T(8,128)} %get-tuple-element.22), channel_id=1, source_target_pairs={{0,4},{4,0},{8,12},{12,8},{16,20},{20,16},{24,28},{28,24},{32,36},... | collective-permute-start | bytes 393224 | tf_op jit(solution)/shard_map/ppermute | solution.py:262
  24.2 31.3 %all-to-all-start = ((f32[1088,1,128]{2,1,0:T(1,128)}), f32[1088,1,128]{2,1,0:T(1,128)S(1)}, u32[]{:S(2)}, u32[]{:S(2)}) async-start(f32[1088,1,128]{2,1,0:T(1,128)} %bitcast.6), calls=%async_computation | async-start | bytes 1114112 | tf_op jit(solution)/shard_map/all_to_all | solution.py:289
  37.2 4.3 %collective-permute-start.5 = (f32[4,16,128]{2,1,0:T(8,128)S(1)}, f32[4,16,128]{2,1,0:T(8,128)S(1)}, u32[]{:S(2)}, u32[]{:S(2)}) collective-permute-start(f32[4,16,128]{2,1,0:T(8,128)S(1)} %get-tuple-element.27), channel_id=1, source_target_pairs={{0,1},{1,2},{2,3},{3,0},{4,5},{5,6},{6,7},{7,4},{8,9},{9,10},{10,1... | collective-permute-start | bytes 98312 | tf_op jit(solution)/shard_map/ppermute | solution.py:243
  37.6 4.4 %collective-permute-start.6 = (f32[4,16,128]{2,1,0:T(8,128)S(1)}, f32[4,16,128]{2,1,0:T(8,128)S(1)}, u32[]{:S(2)}, u32[]{:S(2)}) collective-permute-start(f32[4,16,128]{2,1,0:T(8,128)S(1)} %get-tuple-element.28), channel_id=1, source_target_pairs={{0,2},{1,3},{2,0},{3,1},{4,6},{5,7},{6,4},{7,5},{8,10},{9,11},{10,... | collective-permute-start | bytes 98312 | tf_op jit(solution)/shard_map/ppermute | solution.py:243
  39.4 3.1 %collective-permute-start.7 = (f32[4,16,128]{2,1,0:T(8,128)S(1)}, f32[4,16,128]{2,1,0:T(8,128)S(1)}, u32[]{:S(2)}, u32[]{:S(2)}) collective-permute-start(f32[4,16,128]{2,1,0:T(8,128)S(1)} %get-tuple-element.29), channel_id=1, source_target_pairs={{0,3},{1,0},{2,1},{3,2},{4,7},{5,4},{6,5},{7,6},{8,11},{9,8},{10,9... | collective-permute-start | bytes 98312 | tf_op jit(solution)/shard_map/ppermute | solution.py:243

commit v4 on v3

--- a/solution.py
+++ b/solution.py
@@ -37,8 +37,8 @@
     return jnp.concatenate([ref[at, :, q].reshape(128, 128) for q in (0, 1)], axis=axis)
 
 
-def far_kernel(chunk, me_ref, rank_ref, x_ref, le, re, ld, rd, o0, o1, o2, o3, ble, bre, bld, brd, made, lhs, sems, out_sems):
-    outs = (o0, o1, o2, o3)
+def far_kernel(chunk, me_ref, rank_ref, x_ref, le, re, ld, rd, *rest):
+    *outs, ble, bre, bld, brd, lhs, sems = rest
     clusters = ble.shape[0]
     steps = clusters // chunk
 
@@ -46,10 +46,6 @@
         part = pl.ds(i * chunk, chunk)
         pairs = ((le, ble), (ld, bld), (re, bre), (rd, brd))
         return [pltpu.make_async_copy(a.at[part], b.at[part], sems.at[j, i]) for j, (a, b) in enumerate(pairs)]
-
-    def stores(i):
-        part = pl.ds(i * chunk * 8, chunk * 8)
-        return [pltpu.make_async_copy(made.at[k, :, part], outs[k].at[:, part], out_sems.at[k, i]) for k in (2, 1, 3, 0)]
 
     for i in range(steps):
         for copy in loads(i):
@@ -84,7 +80,7 @@
             for k in range(4):
                 for q in range(2):
                     start = op * 64 + k * 16 + q * 8
-                    made[k, op * 2 + q, cluster * 8 : cluster * 8 + 8, :] = far[
+                    outs[k][op * 2 + q, cluster * 8 : cluster * 8 + 8, :] = far[
                         start : start + 8, op * 128 : op * 128 + 128
                     ]
 
@@ -99,12 +95,6 @@
             copy.wait()
         for cluster, m in zip(these, mix):
             results(cluster, m)
-        for copy in stores(i):
-            copy.start()
-    for i in range(steps):
-        for copy in stores(i):
-            copy.wait()
-
 
 def near_kernel(chunk, me_ref, base_ref, col_ref, x_ref, de, dd, after, mid, pair, other, bde, bdd, window, sems):
     clusters = bde.shape[0]
@@ -145,7 +135,7 @@
     return high, (value - high.astype(F32)).astype(BF16)
 
 
-def send_kernel(slot_ref, cols_ref, a, b, c, d, after, passed, out, passed_out):
+def send_kernel(slot_ref, cols_ref, a, b, c, d, out):
     slot = jnp.broadcast_to(slot_ref[0:1, :], (64, 128))
     target = iota((64, 128), 0)
     picks = [jnp.where(slot == target * 4 + k, 1.0, 0.0).astype(BF16) for k in range(4)]
@@ -211,30 +201,28 @@
     me_ref = me.astype(jnp.int32).reshape(1)
     base = (position * per_dev - per_dev).astype(jnp.int32).reshape(1)
     x = adjoint_input.reshape(per_dev * 8, 128)
-    params = pltpu.CompilerParams(vmem_limit_bytes=62 * MIB)
+    params = pltpu.CompilerParams(vmem_limit_bytes=24 * MIB)
     small = pltpu.CompilerParams(vmem_limit_bytes=12 * MIB)
 
     def struct(shape, dtype=F32):
         return jax.ShapeDtypeStruct(shape, dtype)
+
+    def in_hbm(*values):
+        return [pltpu.with_memory_space_constraint(v, pltpu.HBM) for v in values]
 
     chunk = 4
     steps = per_dev // chunk
     far = pl.pallas_call(
         functools.partial(far_kernel, chunk),
         in_specs=[SMEM, SMEM, VMEM] + [ANY] * 4,
-        out_specs=[ANY] * 4,
-        out_shape=[struct((4, 128, 128))] * 4,
+        out_specs=[VMEM] * 4,
+        out_shape=[struct((4, 128, 128), F32)] * 4,
         scratch_shapes=[pltpu.VMEM(efie_left.shape, BF16)] * 4
-        + [
-            pltpu.VMEM((4, 4, 128, 128), F32),
-            pltpu.VMEM((per_dev, 64, 256), BF16),
-            pltpu.SemaphoreType.DMA((4, steps)),
-            pltpu.SemaphoreType.DMA((4, steps)),
-        ],
+        + [pltpu.VMEM((per_dev, 64, 256), BF16), pltpu.SemaphoreType.DMA((4, steps))],
         compiler_params=params,
         cost_estimate=pl.CostEstimate(flops=200_000_000, bytes_accessed=5_300_000, transcendentals=0),
         name="far",
-    )(me_ref, block_ranks.T, x, efie_left, efie_right, dual_left, dual_right)
+    )(me_ref, *in_hbm(block_ranks.T, x, efie_left, efie_right, dual_left, dual_right))
 
     def shift(k):
         return [(i, (i + k) % subs) for i in range(subs)]
@@ -255,7 +243,7 @@
         compiler_params=params,
         cost_estimate=pl.CostEstimate(flops=200_000_000, bytes_accessed=4_600_000, transcendentals=0),
         name="near",
-    )(me_ref, base, near_cols.T, x, efie_near, dual_near, far[0])
+    )(me_ref, base, *in_hbm(near_cols.T, x, efie_near, dual_near), far[0])
     count = lax.axis_size("cluster")
     within = [(i, i ^ 1) for i in range(count)]
     between = [(i, i + 1) for i in range(1, count - 1, 2)] + [(i + 1, i) for i in range(1, count - 1, 2)]
@@ -268,15 +256,23 @@
     order = jnp.sum(earlier.astype(jnp.int32), axis=1)
     slot = jnp.broadcast_to((owner * 4 + order)[None, :], (8, 128))
     place = jnp.broadcast_to((order * 16 + cols % per_dev)[:, None], (128, 128))
-    sent, got_pair = pl.pallas_call(
+    sent = pl.pallas_call(
         send_kernel,
-        in_specs=[VMEM] * 6 + [ANY] * 2,
-        out_specs=[VMEM, ANY],
-        out_shape=[struct((count * 17, 128)), struct(pair.shape)],
-        input_output_aliases={7: 1},
+        in_specs=[VMEM] * 6,
+        out_specs=VMEM,
+        out_shape=struct((count * 17, 128)),
         compiler_params=small,
         name="send",
-    )(slot, place, *far_got, got_other, got_pair)
+    )(slot, place, *far_got)
+    sent, got_pair, got_other = pl.pallas_call(
+        lambda *refs: None,
+        in_specs=[ANY] * 3,
+        out_specs=[ANY] * 3,
+        out_shape=[struct((count * 17, 128)), struct(pair.shape), struct(pair.shape)],
+        input_output_aliases={0: 0, 1: 1, 2: 2},
+        compiler_params=small,
+        name="join",
+    )(sent, got_pair, got_other)
     near = pl.pallas_call(
         merge_kernel,
         in_specs=[VMEM] * 3,

time: 56.7 us -> 55 us (0.970)
  Pallas kernels: 11.1 us -> 9.53 us
  waiting for transfers between devices: 17.1 us -> 15.8 us
  starting transfers between devices: 27 us -> 28.2 us
    ppermute x1, waiting for transfers between devices: 2.36 us -> 0.01 us  [per_device(): got_other = lax.ppermute(other, 'cluster', between)]
    ppermute x6, waiting for transfers between devices: 1.77 us -> 3.68 us  [over_sub(): lax.ppermute(parts[k], 'sub', shift(k))]
    ppermute x1, starting transfers between devices: 4.74 us -> 3.1 us  [per_device(): got_other = lax.ppermute(other, 'cluster', between)]
    ppermute x1, starting transfers between devices: 0.09 us -> 1.6 us  [per_device(): got_pair = lax.ppermute(pair, 'cluster', within)]
    pallas_call x1, Pallas kernels: 4.92 us -> 4.06 us  [per_device(): pl.pallas_call(functools.partial(far_kernel, chunk), in_specs=[SMEM, SMEM...]
    all_to_all x1, waiting for transfers between devices: 13 us -> 12.1 us  [per_device(): lax.all_to_all(sent.reshape(count * 17, 1, 128), 'cluster', 0, 0, tiled=T...]
    pallas_call x1, Pallas kernels: 4.06 us -> 3.32 us  [per_device(): pl.pallas_call(functools.partial(near_kernel, chunk), in_specs=[SMEM, SME...]
    all_to_all x1, starting transfers between devices: 12.9 us -> 13.6 us  [per_device(): lax.all_to_all(sent.reshape(count * 17, 1, 128), 'cluster', 0, 0, tiled=T...]
  transfers between devices with their start and end apart: 9 -> 9, of which waited for: 5 -> 5; matrix products, arithmetic and copies ran while one was open for 1% -> 1% of each run, Pallas kernels for 7% -> 6%
where the time goes in v4:
time: 55 us; the launch traced here: 54.7 us
  starting transfers between devices  28.2 us (51%)
  waiting for transfers between devices  15.8 us (29%)
  Pallas kernels  9.53 us (17%)
  between operations  0.72 us (1%)
    all_to_all x1, starting transfers between devices, per_device(): lax.all_to_all(sent.reshape(count * 17, 1, 128), 'cluster', 0, 0, tiled=T...  13.6 us
    all_to_all x1, waiting for transfers between devices, per_device(): lax.all_to_all(sent.reshape(count * 17, 1, 128), 'cluster', 0, 0, tiled=T...  12.1 us
    ppermute x6, starting transfers between devices, over_sub(): lax.ppermute(parts[k], 'sub', shift(k))  9.9 us
    pallas_call x1, Pallas kernels, per_device(): pl.pallas_call(functools.partial(far_kernel, chunk), in_specs=[SMEM, SMEM...  4.06 us
    ppermute x6, waiting for transfers between devices, over_sub(): lax.ppermute(parts[k], 'sub', shift(k))  3.68 us
    pallas_call x1, Pallas kernels, per_device(): pl.pallas_call(functools.partial(near_kernel, chunk), in_specs=[SMEM, SME...  3.32 us
    ppermute x1, starting transfers between devices, per_device(): got_other = lax.ppermute(other, 'cluster', between)  3.1 us
    ppermute x1, starting transfers between devices, per_device(): got_pair = lax.ppermute(pair, 'cluster', within)  1.6 us
  transfers between devices with their start and end apart: 9, of which 5 were waited for; matrix products, arithmetic and copies ran while one was open for 1% of the time, Pallas kernels for 6%

profile of v4, /device:TPU:1, one launch (start us, length us, event | category | flops | bytes accessed | tf_op | source)
XLA Modules:
  0.0 54.7 jit_solution(877987646043793820)
XLA Ops:
  0.6 4.1 %far.1 = (f32[4,128,128]{2,1,0:T(8,128)S(1)}, f32[4,128,128]{2,1,0:T(8,128)S(1)}, f32[4,128,128]{2,1,0:T(8,128)S(1)}, f32[4,128,128]{2,1,0:T(8,128)S(1)}) custom-call(s32[1]{0:T(128)} %bitcast.me_ref, s32[8,16]{1,0:T(8,128)} %bitcast.24, bf16[128,128]{1,0:T(8,128)(2,1)} %bitcast.22, bf16[16,8,2,16,128]{4,3,2,1,0:T(8,128)(2,1)} %le.1, ...), custom_call_target="tpu_custom_call" | custom-call | flops 200000000 | bytes 5300000 | tf_op jit(solution)/shard_map/far/pallas_call | solution.py:215
  4.7 2.1 %collective-permute-start = (f32[4,128,128]{2,1,0:T(8,128)S(1)}, f32[4,128,128]{2,1,0:T(8,128)S(1)}, u32[]{:S(2)}, u32[]{:S(2)}) collective-permute-start(f32[4,128,128]{2,1,0:T(8,128)S(1)} %get-tuple-element.19), channel_id=1, source_target_pairs={{0,1},{1,2},{2,3},{3,0},{4,5},{5,6},{6,7},{7,4},{8,9},{9,10},{10,1... | collective-permute-start | bytes 786440 | tf_op jit(solution)/shard_map/ppermute | solution.py:231
  6.8 2.4 %collective-permute-start.1 = (f32[4,128,128]{2,1,0:T(8,128)S(1)}, f32[4,128,128]{2,1,0:T(8,128)S(1)}, u32[]{:S(2)}, u32[]{:S(2)}) collective-permute-start(f32[4,128,128]{2,1,0:T(8,128)S(1)} %get-tuple-element.20), channel_id=1, source_target_pairs={{0,2},{1,3},{2,0},{3,1},{4,6},{5,7},{6,4},{7,5},{8,10},{9,11},{10,... | collective-permute-start | bytes 786440 | tf_op jit(solution)/shard_map/ppermute | solution.py:231
  9.3 1.2 %collective-permute-start.2 = (f32[4,128,128]{2,1,0:T(8,128)S(1)}, f32[4,128,128]{2,1,0:T(8,128)S(1)}, u32[]{:S(2)}, u32[]{:S(2)}) collective-permute-start(f32[4,128,128]{2,1,0:T(8,128)S(1)} %get-tuple-element.21), channel_id=1, source_target_pairs={{0,3},{1,0},{2,1},{3,2},{4,7},{5,4},{6,5},{7,6},{8,11},{9,8},{10,9... | collective-permute-start | bytes 786440 | tf_op jit(solution)/shard_map/ppermute | solution.py:231
  10.4 3.3 %near.1 = (f32[16,2,8,128]{3,2,1,0:T(8,128)S(1)}, f32[16,2,8,128]{3,2,1,0:T(8,128)S(1)}, f32[16,2,8,128]{3,2,1,0:T(8,128)S(1)}) custom-call(s32[1]{0:T(128)} %bitcast.me_ref, s32[1]{0:T(128)} %bitcast.3.base_ref, s32[2,16]{1,0:T(2,128)} %bitcast.25, bf16[128,128]{1,0:T(8,128)(2,1)} %bitcast.23, bf16[16,2,2,128,128]{4,3,2,1,0:T(8,128)(2,1)} %de.1, ...), custom_call_target="tpu_custom_call" | custom-call | flops 200000000 | bytes 4600000 | tf_op jit(solution)/shard_map/near/pallas_call | solution.py:236
  13.8 1.6 %collective-permute-start.3 = (f32[16,2,8,128]{3,2,1,0:T(8,128)S(1)}, f32[16,2,8,128]{3,2,1,0:T(8,128)S(1)}, u32[]{:S(2)}, u32[]{:S(2)}) collective-permute-start(f32[16,2,8,128]{3,2,1,0:T(8,128)S(1)} %get-tuple-element.22), channel_id=1, source_target_pairs={{0,4},{4,0},{8,12},{12,8},{16,20},{20,16},{24,28},{28,24},{32,36},... | collective-permute-start | bytes 393224 | tf_op jit(solution)/shard_map/ppermute | solution.py:250
  15.4 3.1 %collective-permute-start.4 = (f32[16,2,8,128]{3,2,1,0:T(8,128)S(1)}, f32[16,2,8,128]{3,2,1,0:T(8,128)S(1)}, u32[]{:S(2)}, u32[]{:S(2)}) collective-permute-start(f32[16,2,8,128]{3,2,1,0:T(8,128)S(1)} %get-tuple-element.23), channel_id=1, source_target_pairs={{4,8},{12,16},{20,24},{28,32},{36,40},{44,48},{52,56},{60,64},{68,... | collective-permute-start | bytes 393224 | tf_op jit(solution)/shard_map/ppermute | solution.py:251
  18.5 0.1 copy.25
  18.5 0.1 reshape.131
  18.7 0.2 convert_reduce_fusion
  18.9 0.0 collective-permute-done.b
  18.9 1.7 %collective-permute-done.1.c = f32[4,128,128]{2,1,0:T(8,128)S(1)} collective-permute-done((f32[4,128,128]{2,1,0:T(8,128)S(1)}, f32[4,128,128]{2,1,0:T(8,128)S(1)}, u32[]{:S(2)}, u32[]{:S(2)}) %collective-permute-start.1) | collective-permute-done | bytes 262176 | tf_op jit(solution)/shard_map/ppermute | solution.py:231
  20.6 0.1 broadcast_in_dim.5.cols_ref
  20.7 1.1 %send.1.refs_0_ = f32[1088,128]{1,0:T(8,128)} custom-call(s32[8,128]{1,0:T(8,128)S(1)} %broadcast_in_dim.4.slot_ref, s32[128,128]{1,0:T(8,128)S(1)} %broadcast_in_dim.5.cols_ref, f32[4,128,128]{2,1,0:T(8,128)S(1)} %get-tuple-element.18.a.after, f32[4,128,128]{2,1,0:T(8,128)S(1)} %collective-permute-done.b, f32[4,128,128]{2,1,0:T(8,128)S(1)} %collective-permute-done.1.c, ...), custom_call_target="tpu_custom_call" | custom-call | tf_op jit(solution)/shard_map/send/pallas_call | solution.py:259
  21.8 13.6 %all-to-all-start = ((f32[1088,1,128]{2,1,0:T(1,128)}), f32[1088,1,128]{2,1,0:T(1,128)S(1)}, u32[]{:S(2)}, u32[]{:S(2)}) async-start(f32[1088,1,128]{2,1,0:T(1,128)} %bitcast.6), calls=%async_computation | async-start | bytes 1114112 | tf_op jit(solution)/shard_map/all_to_all | solution.py:285
  35.3 0.1 merge.1
  35.5 0.8 %collective-permute-start.5 = (f32[4,16,128]{2,1,0:T(8,128)S(1)}, f32[4,16,128]{2,1,0:T(8,128)S(1)}, u32[]{:S(2)}, u32[]{:S(2)}) collective-permute-start(f32[4,16,128]{2,1,0:T(8,128)S(1)} %get-tuple-element.29), channel_id=1, source_target_pairs={{0,1},{1,2},{2,3},{3,0},{4,5},{5,6},{6,7},{7,4},{8,9},{9,10},{10,1... | collective-permute-start | bytes 98312 | tf_op jit(solution)/shard_map/ppermute | solution.py:231
  36.2 2.1 %collective-permute-start.6 = (f32[4,16,128]{2,1,0:T(8,128)S(1)}, f32[4,16,128]{2,1,0:T(8,128)S(1)}, u32[]{:S(2)}, u32[]{:S(2)}) collective-permute-start(f32[4,16,128]{2,1,0:T(8,128)S(1)} %get-tuple-element.30), channel_id=1, source_target_pairs={{0,2},{1,3},{2,0},{3,1},{4,6},{5,7},{6,4},{7,5},{8,10},{9,11},{10,... | collective-permute-start | bytes 98312 | tf_op jit(solution)/shard_map/ppermute | solution.py:231
  38.3 1.3 %collective-permute-start.7 = (f32[4,16,128]{2,1,0:T(8,128)S(1)}, f32[4,16,128]{2,1,0:T(8,128)S(1)}, u32[]{:S(2)}, u32[]{:S(2)}) collective-permute-start(f32[4,16,128]{2,1,0:T(8,128)S(1)} %get-tuple-element.31), channel_id=1, source_target_pairs={{0,3},{1,0},{2,1},{3,2},{4,7},{5,4},{6,5},{7,6},{8,11},{9,8},{10,9... | collective-permute-start | bytes 98312 | tf_op jit(solution)/shard_map/ppermute | solution.py:231
  39.6 0.2 collective-permute-done.5.nb
  39.8 1.3 %collective-permute-done.6.nc = f32[4,16,128]{2,1,0:T(8,128)S(1)} collective-permute-done((f32[4,16,128]{2,1,0:T(8,128)S(1)}, f32[4,16,128]{2,1,0:T(8,128)S(1)}, u32[]{:S(2)}, u32[]{:S(2)}) %collective-permute-start.6) | collective-permute-done | bytes 32800 | tf_op jit(solution)/shard_map/ppermute | solution.py:231
  41.1 0.5 collective-permute-done.7.nd
  41.6 12.1 %all-to-all-done = f32[1088,1,128]{2,1,0:T(1,128)S(1)} async-done(((f32[1088,1,128]{2,1,0:T(1,128)}), f32[1088,1,128]{2,1,0:T(1,128)S(1)}, u32[]{:S(2)}, u32[]{:S(2)}) %all-to-all-start) | async-done | bytes 557088 | tf_op jit(solution)/shard_map/all_to_all | solution.py:285
  53.7 0.9 %total.1 = (bf16[16,2,128]{2,1,0:T(2,128)(2,1)}, bf16[16,2,128]{2,1,0:T(2,128)(2,1)}) custom-call(f32[1088,128]{1,0:T(8,128)S(1)} %bitcast.18, f32[4,16,128]{2,1,0:T(8,128)S(1)} %get-tuple-element.28.na, f32[4,16,128]{2,1,0:T(8,128)S(1)} %collective-permute-done.5.nb, f32[4,16,128]{2,1,0:T(8,128)S(1)} %collective-permute-done.6.nc, ...), custom_call_target="tpu_custom_call" | custom-call | tf_op jit(solution)/shard_map/total/pallas_call | solution.py:286
  (9 shorter events, 0.0 us)
Async XLA Ops:
  4.7 14.2 %collective-permute-start = (f32[4,128,128]{2,1,0:T(8,128)S(1)}, f32[4,128,128]{2,1,0:T(8,128)S(1)}, u32[]{:S(2)}, u32[]{:S(2)}) collective-permute-start(f32[4,128,128]{2,1,0:T(8,128)S(1)} %get-tuple-element.19), channel_id=1, source_target_pairs={{0,1},{1,2},{2,3},{3,0},{4,5},{5,6},{6,7},{7,4},{8,9},{9,10},{10,1... | collective-permute-start | bytes 786440 | tf_op jit(solution)/shard_map/ppermute | solution.py:231
  6.8 13.8 %collective-permute-start.1 = (f32[4,128,128]{2,1,0:T(8,128)S(1)}, f32[4,128,128]{2,1,0:T(8,128)S(1)}, u32[]{:S(2)}, u32[]{:S(2)}) collective-permute-start(f32[4,128,128]{2,1,0:T(8,128)S(1)} %get-tuple-element.20), channel_id=1, source_target_pairs={{0,2},{1,3},{2,0},{3,1},{4,6},{5,7},{6,4},{7,5},{8,10},{9,11},{10,... | collective-permute-start | bytes 786440 | tf_op jit(solution)/shard_map/ppermute | solution.py:231
  9.3 11.3 %collective-permute-start.2 = (f32[4,128,128]{2,1,0:T(8,128)S(1)}, f32[4,128,128]{2,1,0:T(8,128)S(1)}, u32[]{:S(2)}, u32[]{:S(2)}) collective-permute-start(f32[4,128,128]{2,1,0:T(8,128)S(1)} %get-tuple-element.21), channel_id=1, source_target_pairs={{0,3},{1,0},{2,1},{3,2},{4,7},{5,4},{6,5},{7,6},{8,11},{9,8},{10,9... | collective-permute-start | bytes 786440 | tf_op jit(solution)/shard_map/ppermute | solution.py:231
  10.4 8.0 %copy-start = (s32[16,8]{0,1:T(8,128)S(1)}, s32[16,8]{0,1:T(8,128)}, u32[]{:S(2)}) copy-start(s32[16,8]{0,1:T(8,128)} %param.16) | copy-start | bytes 1540
  13.8 8.0 %collective-permute-start.3 = (f32[16,2,8,128]{3,2,1,0:T(8,128)S(1)}, f32[16,2,8,128]{3,2,1,0:T(8,128)S(1)}, u32[]{:S(2)}, u32[]{:S(2)}) collective-permute-start(f32[16,2,8,128]{3,2,1,0:T(8,128)S(1)} %get-tuple-element.22), channel_id=1, source_target_pairs={{0,4},{4,0},{8,12},{12,8},{16,20},{20,16},{24,28},{28,24},{32,36},... | collective-permute-start | bytes 393224 | tf_op jit(solution)/shard_map/ppermute | solution.py:250
  15.4 6.4 %collective-permute-start.4 = (f32[16,2,8,128]{3,2,1,0:T(8,128)S(1)}, f32[16,2,8,128]{3,2,1,0:T(8,128)S(1)}, u32[]{:S(2)}, u32[]{:S(2)}) collective-permute-start(f32[16,2,8,128]{3,2,1,0:T(8,128)S(1)} %get-tuple-element.23), channel_id=1, source_target_pairs={{4,8},{12,16},{20,24},{28,32},{36,40},{44,48},{52,56},{60,64},{68,... | collective-permute-start | bytes 393224 | tf_op jit(solution)/shard_map/ppermute | solution.py:251
  21.8 31.9 %all-to-all-start = ((f32[1088,1,128]{2,1,0:T(1,128)}), f32[1088,1,128]{2,1,0:T(1,128)S(1)}, u32[]{:S(2)}, u32[]{:S(2)}) async-start(f32[1088,1,128]{2,1,0:T(1,128)} %bitcast.6), calls=%async_computation | async-start | bytes 1114112 | tf_op jit(solution)/shard_map/all_to_all | solution.py:285
  35.5 4.3 %collective-permute-start.5 = (f32[4,16,128]{2,1,0:T(8,128)S(1)}, f32[4,16,128]{2,1,0:T(8,128)S(1)}, u32[]{:S(2)}, u32[]{:S(2)}) collective-permute-start(f32[4,16,128]{2,1,0:T(8,128)S(1)} %get-tuple-element.29), channel_id=1, source_target_pairs={{0,1},{1,2},{2,3},{3,0},{4,5},{5,6},{6,7},{7,4},{8,9},{9,10},{10,1... | collective-permute-start | bytes 98312 | tf_op jit(solution)/shard_map/ppermute | solution.py:231
  36.2 4.9 %collective-permute-start.6 = (f32[4,16,128]{2,1,0:T(8,128)S(1)}, f32[4,16,128]{2,1,0:T(8,128)S(1)}, u32[]{:S(2)}, u32[]{:S(2)}) collective-permute-start(f32[4,16,128]{2,1,0:T(8,128)S(1)} %get-tuple-element.30), channel_id=1, source_target_pairs={{0,2},{1,3},{2,0},{3,1},{4,6},{5,7},{6,4},{7,5},{8,10},{9,11},{10,... | collective-permute-start | bytes 98312 | tf_op jit(solution)/shard_map/ppermute | solution.py:231
  38.3 3.2 %collective-permute-start.7 = (f32[4,16,128]{2,1,0:T(8,128)S(1)}, f32[4,16,128]{2,1,0:T(8,128)S(1)}, u32[]{:S(2)}, u32[]{:S(2)}) collective-permute-start(f32[4,16,128]{2,1,0:T(8,128)S(1)} %get-tuple-element.31), channel_id=1, source_target_pairs={{0,3},{1,0},{2,1},{3,2},{4,7},{5,4},{6,5},{7,6},{8,11},{9,8},{10,9... | collective-permute-start | bytes 98312 | tf_op jit(solution)/shard_map/ppermute | solution.py:231

commit v5 on v4

--- a/solution.py
+++ b/solution.py
@@ -210,7 +210,7 @@
     def in_hbm(*values):
         return [pltpu.with_memory_space_constraint(v, pltpu.HBM) for v in values]
 
-    chunk = 4
+    chunk = 8
     steps = per_dev // chunk
     far = pl.pallas_call(
         functools.partial(far_kernel, chunk),
@@ -228,8 +228,7 @@
         return [(i, (i + k) % subs) for i in range(subs)]
 
     def over_sub(parts):
-        one, three, two = (lax.ppermute(parts[k], "sub", shift(k)) for k in (1, 3, 2))
-        return [parts[0], one, two, three]
+        return [parts[0]] + [lax.ppermute(parts[k], "sub", shift(k)) for k in (1, 3, 2)]
 
     far_got = over_sub(far)
 

time: 55 us -> 54.1 us (0.984)
  starting transfers between devices: 28.2 us -> 26 us
  waiting for transfers between devices: 15.8 us -> 17.5 us
    ppermute x6, waiting for transfers between devices: 3.68 us -> 6.54 us  [over_sub(): lax.ppermute(parts[k], 'sub', shift(k))]
    ppermute x6, starting transfers between devices: 9.9 us -> 8.08 us  [over_sub(): lax.ppermute(parts[k], 'sub', shift(k))]
    all_to_all x1, waiting for transfers between devices: 12.1 us -> 10.9 us  [per_device(): lax.all_to_all(sent.reshape(count * 17, 1, 128), 'cluster', 0, 0, tiled=T...]
  transfers between devices with their start and end apart: 9 -> 9, of which waited for: 5 -> 4; matrix products, arithmetic and copies ran while one was open for 1% -> 1% of each run, Pallas kernels for 6% -> 7%
where the time goes in v5:
time: 54.1 us; the launch traced here: 53.8 us
  starting transfers between devices  26 us (48%)
  waiting for transfers between devices  17.5 us (32%)
  Pallas kernels  9.15 us (17%)
  between operations  0.73 us (1%)
    all_to_all x1, starting transfers between devices, per_device(): lax.all_to_all(sent.reshape(count * 17, 1, 128), 'cluster', 0, 0, tiled=T...  13.2 us
    all_to_all x1, waiting for transfers between devices, per_device(): lax.all_to_all(sent.reshape(count * 17, 1, 128), 'cluster', 0, 0, tiled=T...  10.9 us
    ppermute x6, starting transfers between devices, over_sub(): lax.ppermute(parts[k], 'sub', shift(k))  8.08 us
    ppermute x6, waiting for transfers between devices, over_sub(): lax.ppermute(parts[k], 'sub', shift(k))  6.54 us
    pallas_call x1, Pallas kernels, per_device(): pl.pallas_call(functools.partial(far_kernel, chunk), in_specs=[SMEM, SMEM...  3.56 us
    pallas_call x1, Pallas kernels, per_device(): pl.pallas_call(functools.partial(near_kernel, chunk), in_specs=[SMEM, SME...  3.44 us
    ppermute x1, starting transfers between devices, per_device(): got_other = lax.ppermute(other, 'cluster', between)  3.1 us
    ppermute x1, starting transfers between devices, per_device(): got_pair = lax.ppermute(pair, 'cluster', within)  1.6 us
  transfers between devices with their start and end apart: 9, of which 4 were waited for; matrix products, arithmetic and copies ran while one was open for 1% of the time, Pallas kernels for 7%

profile of v5, /device:TPU:1, one launch (start us, length us, event | category | flops | bytes accessed | tf_op | source)
XLA Modules:
  0.0 53.8 jit_solution(479299449610212552)
XLA Ops:
  0.6 3.6 %far.1 = (f32[4,128,128]{2,1,0:T(8,128)S(1)}, f32[4,128,128]{2,1,0:T(8,128)S(1)}, f32[4,128,128]{2,1,0:T(8,128)S(1)}, f32[4,128,128]{2,1,0:T(8,128)S(1)}) custom-call(s32[1]{0:T(128)} %bitcast.me_ref, s32[8,16]{1,0:T(8,128)} %bitcast.24, bf16[128,128]{1,0:T(8,128)(2,1)} %bitcast.22, bf16[16,8,2,16,128]{4,3,2,1,0:T(8,128)(2,1)} %le.1, ...), custom_call_target="tpu_custom_call" | custom-call | flops 200000000 | bytes 5300000 | tf_op jit(solution)/shard_map/far/pallas_call | solution.py:215
  4.2 2.1 %collective-permute-start = (f32[4,128,128]{2,1,0:T(8,128)S(1)}, f32[4,128,128]{2,1,0:T(8,128)S(1)}, u32[]{:S(2)}, u32[]{:S(2)}) collective-permute-start(f32[4,128,128]{2,1,0:T(8,128)S(1)} %get-tuple-element.19), channel_id=1, source_target_pairs={{0,1},{1,2},{2,3},{3,0},{4,5},{5,6},{6,7},{7,4},{8,9},{9,10},{10,1... | collective-permute-start | bytes 786440 | tf_op jit(solution)/shard_map/ppermute | solution.py:231
  6.3 1.4 %collective-permute-start.1 = (f32[4,128,128]{2,1,0:T(8,128)S(1)}, f32[4,128,128]{2,1,0:T(8,128)S(1)}, u32[]{:S(2)}, u32[]{:S(2)}) collective-permute-start(f32[4,128,128]{2,1,0:T(8,128)S(1)} %get-tuple-element.20), channel_id=1, source_target_pairs={{0,3},{1,0},{2,1},{3,2},{4,7},{5,4},{6,5},{7,6},{8,11},{9,8},{10,9... | collective-permute-start | bytes 786440 | tf_op jit(solution)/shard_map/ppermute | solution.py:231
  7.7 1.6 %collective-permute-start.2 = (f32[4,128,128]{2,1,0:T(8,128)S(1)}, f32[4,128,128]{2,1,0:T(8,128)S(1)}, u32[]{:S(2)}, u32[]{:S(2)}) collective-permute-start(f32[4,128,128]{2,1,0:T(8,128)S(1)} %get-tuple-element.21), channel_id=1, source_target_pairs={{0,2},{1,3},{2,0},{3,1},{4,6},{5,7},{6,4},{7,5},{8,10},{9,11},{10,... | collective-permute-start | bytes 786440 | tf_op jit(solution)/shard_map/ppermute | solution.py:231
  9.3 3.4 %near.1 = (f32[16,2,8,128]{3,2,1,0:T(8,128)S(1)}, f32[16,2,8,128]{3,2,1,0:T(8,128)S(1)}, f32[16,2,8,128]{3,2,1,0:T(8,128)S(1)}) custom-call(s32[1]{0:T(128)} %bitcast.me_ref, s32[1]{0:T(128)} %bitcast.3.base_ref, s32[2,16]{1,0:T(2,128)} %bitcast.25, bf16[128,128]{1,0:T(8,128)(2,1)} %bitcast.23, bf16[16,2,2,128,128]{4,3,2,1,0:T(8,128)(2,1)} %de.1, ...), custom_call_target="tpu_custom_call" | custom-call | flops 200000000 | bytes 4600000 | tf_op jit(solution)/shard_map/near/pallas_call | solution.py:235
  12.8 1.6 %collective-permute-start.3 = (f32[16,2,8,128]{3,2,1,0:T(8,128)S(1)}, f32[16,2,8,128]{3,2,1,0:T(8,128)S(1)}, u32[]{:S(2)}, u32[]{:S(2)}) collective-permute-start(f32[16,2,8,128]{3,2,1,0:T(8,128)S(1)} %get-tuple-element.22), channel_id=1, source_target_pairs={{0,4},{4,0},{8,12},{12,8},{16,20},{20,16},{24,28},{28,24},{32,36},... | collective-permute-start | bytes 393224 | tf_op jit(solution)/shard_map/ppermute | solution.py:249
  14.4 3.1 %collective-permute-start.4 = (f32[16,2,8,128]{3,2,1,0:T(8,128)S(1)}, f32[16,2,8,128]{3,2,1,0:T(8,128)S(1)}, u32[]{:S(2)}, u32[]{:S(2)}) collective-permute-start(f32[16,2,8,128]{3,2,1,0:T(8,128)S(1)} %get-tuple-element.23), channel_id=1, source_target_pairs={{4,8},{12,16},{20,24},{28,32},{36,40},{44,48},{52,56},{60,64},{68,... | collective-permute-start | bytes 393224 | tf_op jit(solution)/shard_map/ppermute | solution.py:250
  17.5 0.1 copy.25
  17.6 0.1 reshape.131
  17.7 0.2 convert_reduce_fusion
  17.9 0.0 collective-permute-done.b
  17.9 0.0 collective-permute-done.1.c
  17.9 2.2 %collective-permute-done.2.d = f32[4,128,128]{2,1,0:T(8,128)S(1)} collective-permute-done((f32[4,128,128]{2,1,0:T(8,128)S(1)}, f32[4,128,128]{2,1,0:T(8,128)S(1)}, u32[]{:S(2)}, u32[]{:S(2)}) %collective-permute-start.2) | collective-permute-done | bytes 262176 | tf_op jit(solution)/shard_map/ppermute | solution.py:231
  20.1 0.1 broadcast_in_dim.5.cols_ref
  20.2 1.1 %send.1.refs_0_ = f32[1088,128]{1,0:T(8,128)} custom-call(s32[8,128]{1,0:T(8,128)S(1)} %broadcast_in_dim.4.slot_ref, s32[128,128]{1,0:T(8,128)S(1)} %broadcast_in_dim.5.cols_ref, f32[4,128,128]{2,1,0:T(8,128)S(1)} %get-tuple-element.18.a.after, f32[4,128,128]{2,1,0:T(8,128)S(1)} %collective-permute-done.b, f32[4,128,128]{2,1,0:T(8,128)S(1)} %collective-permute-done.1.c, ...), custom_call_target="tpu_custom_call" | custom-call | tf_op jit(solution)/shard_map/send/pallas_call | solution.py:258
  21.3 13.2 %all-to-all-start = ((f32[1088,1,128]{2,1,0:T(1,128)}), f32[1088,1,128]{2,1,0:T(1,128)S(1)}, u32[]{:S(2)}, u32[]{:S(2)}) async-start(f32[1088,1,128]{2,1,0:T(1,128)} %bitcast.6), calls=%async_computation | async-start | bytes 1114112 | tf_op jit(solution)/shard_map/all_to_all | solution.py:284
  34.5 0.1 merge.1
  34.6 0.9 %collective-permute-start.5 = (f32[4,16,128]{2,1,0:T(8,128)S(1)}, f32[4,16,128]{2,1,0:T(8,128)S(1)}, u32[]{:S(2)}, u32[]{:S(2)}) collective-permute-start(f32[4,16,128]{2,1,0:T(8,128)S(1)} %get-tuple-element.29), channel_id=1, source_target_pairs={{0,1},{1,2},{2,3},{3,0},{4,5},{5,6},{6,7},{7,4},{8,9},{9,10},{10,1... | collective-permute-start | bytes 98312 | tf_op jit(solution)/shard_map/ppermute | solution.py:231
  35.5 1.8 %collective-permute-start.6 = (f32[4,16,128]{2,1,0:T(8,128)S(1)}, f32[4,16,128]{2,1,0:T(8,128)S(1)}, u32[]{:S(2)}, u32[]{:S(2)}) collective-permute-start(f32[4,16,128]{2,1,0:T(8,128)S(1)} %get-tuple-element.30), channel_id=1, source_target_pairs={{0,3},{1,0},{2,1},{3,2},{4,7},{5,4},{6,5},{7,6},{8,11},{9,8},{10,9... | collective-permute-start | bytes 98312 | tf_op jit(solution)/shard_map/ppermute | solution.py:231
  37.4 0.2 collective-permute-start.7
  37.6 1.4 %collective-permute-done.5.nb = f32[4,16,128]{2,1,0:T(8,128)S(1)} collective-permute-done((f32[4,16,128]{2,1,0:T(8,128)S(1)}, f32[4,16,128]{2,1,0:T(8,128)S(1)}, u32[]{:S(2)}, u32[]{:S(2)}) %collective-permute-start.5) | collective-permute-done | bytes 32800 | tf_op jit(solution)/shard_map/ppermute | solution.py:231
  38.9 3.0 %collective-permute-done.7.nd = f32[4,16,128]{2,1,0:T(8,128)S(1)} collective-permute-done((f32[4,16,128]{2,1,0:T(8,128)S(1)}, f32[4,16,128]{2,1,0:T(8,128)S(1)}, u32[]{:S(2)}, u32[]{:S(2)}) %collective-permute-start.7) | collective-permute-done | bytes 32800 | tf_op jit(solution)/shard_map/ppermute | solution.py:231
  41.9 10.9 %all-to-all-done = f32[1088,1,128]{2,1,0:T(1,128)S(1)} async-done(((f32[1088,1,128]{2,1,0:T(1,128)}), f32[1088,1,128]{2,1,0:T(1,128)S(1)}, u32[]{:S(2)}, u32[]{:S(2)}) %all-to-all-start) | async-done | bytes 557088 | tf_op jit(solution)/shard_map/all_to_all | solution.py:284
  52.9 0.9 %total.1 = (bf16[16,2,128]{2,1,0:T(2,128)(2,1)}, bf16[16,2,128]{2,1,0:T(2,128)(2,1)}) custom-call(f32[1088,128]{1,0:T(8,128)S(1)} %bitcast.18, f32[4,16,128]{2,1,0:T(8,128)S(1)} %get-tuple-element.28.na, f32[4,16,128]{2,1,0:T(8,128)S(1)} %collective-permute-done.5.nb, f32[4,16,128]{2,1,0:T(8,128)S(1)} %collective-permute-done.6.nc, ...), custom_call_target="tpu_custom_call" | custom-call | tf_op jit(solution)/shard_map/total/pallas_call | solution.py:285
  (9 shorter events, 0.0 us)
Async XLA Ops:
  4.2 13.7 %collective-permute-start = (f32[4,128,128]{2,1,0:T(8,128)S(1)}, f32[4,128,128]{2,1,0:T(8,128)S(1)}, u32[]{:S(2)}, u32[]{:S(2)}) collective-permute-start(f32[4,128,128]{2,1,0:T(8,128)S(1)} %get-tuple-element.19), channel_id=1, source_target_pairs={{0,1},{1,2},{2,3},{3,0},{4,5},{5,6},{6,7},{7,4},{8,9},{9,10},{10,1... | collective-permute-start | bytes 786440 | tf_op jit(solution)/shard_map/ppermute | solution.py:231
  6.3 11.6 %collective-permute-start.1 = (f32[4,128,128]{2,1,0:T(8,128)S(1)}, f32[4,128,128]{2,1,0:T(8,128)S(1)}, u32[]{:S(2)}, u32[]{:S(2)}) collective-permute-start(f32[4,128,128]{2,1,0:T(8,128)S(1)} %get-tuple-element.20), channel_id=1, source_target_pairs={{0,3},{1,0},{2,1},{3,2},{4,7},{5,4},{6,5},{7,6},{8,11},{9,8},{10,9... | collective-permute-start | bytes 786440 | tf_op jit(solution)/shard_map/ppermute | solution.py:231
  7.7 12.4 %collective-permute-start.2 = (f32[4,128,128]{2,1,0:T(8,128)S(1)}, f32[4,128,128]{2,1,0:T(8,128)S(1)}, u32[]{:S(2)}, u32[]{:S(2)}) collective-permute-start(f32[4,128,128]{2,1,0:T(8,128)S(1)} %get-tuple-element.21), channel_id=1, source_target_pairs={{0,2},{1,3},{2,0},{3,1},{4,6},{5,7},{6,4},{7,5},{8,10},{9,11},{10,... | collective-permute-start | bytes 786440 | tf_op jit(solution)/shard_map/ppermute | solution.py:231
  9.3 8.2 %copy-start = (s32[16,8]{0,1:T(8,128)S(1)}, s32[16,8]{0,1:T(8,128)}, u32[]{:S(2)}) copy-start(s32[16,8]{0,1:T(8,128)} %param.16) | copy-start | bytes 1540
  12.8 8.5 %collective-permute-start.3 = (f32[16,2,8,128]{3,2,1,0:T(8,128)S(1)}, f32[16,2,8,128]{3,2,1,0:T(8,128)S(1)}, u32[]{:S(2)}, u32[]{:S(2)}) collective-permute-start(f32[16,2,8,128]{3,2,1,0:T(8,128)S(1)} %get-tuple-element.22), channel_id=1, source_target_pairs={{0,4},{4,0},{8,12},{12,8},{16,20},{20,16},{24,28},{28,24},{32,36},... | collective-permute-start | bytes 393224 | tf_op jit(solution)/shard_map/ppermute | solution.py:249
  14.4 6.9 %collective-permute-start.4 = (f32[16,2,8,128]{3,2,1,0:T(8,128)S(1)}, f32[16,2,8,128]{3,2,1,0:T(8,128)S(1)}, u32[]{:S(2)}, u32[]{:S(2)}) collective-permute-start(f32[16,2,8,128]{3,2,1,0:T(8,128)S(1)} %get-tuple-element.23), channel_id=1, source_target_pairs={{4,8},{12,16},{20,24},{28,32},{36,40},{44,48},{52,56},{60,64},{68,... | collective-permute-start | bytes 393224 | tf_op jit(solution)/shard_map/ppermute | solution.py:250
  21.3 31.6 %all-to-all-start = ((f32[1088,1,128]{2,1,0:T(1,128)}), f32[1088,1,128]{2,1,0:T(1,128)S(1)}, u32[]{:S(2)}, u32[]{:S(2)}) async-start(f32[1088,1,128]{2,1,0:T(1,128)} %bitcast.6), calls=%async_computation | async-start | bytes 1114112 | tf_op jit(solution)/shard_map/all_to_all | solution.py:284
  34.6 4.3 %collective-permute-start.5 = (f32[4,16,128]{2,1,0:T(8,128)S(1)}, f32[4,16,128]{2,1,0:T(8,128)S(1)}, u32[]{:S(2)}, u32[]{:S(2)}) collective-permute-start(f32[4,16,128]{2,1,0:T(8,128)S(1)} %get-tuple-element.29), channel_id=1, source_target_pairs={{0,1},{1,2},{2,3},{3,0},{4,5},{5,6},{6,7},{7,4},{8,9},{9,10},{10,1... | collective-permute-start | bytes 98312 | tf_op jit(solution)/shard_map/ppermute | solution.py:231
  35.5 3.4 %collective-permute-start.6 = (f32[4,16,128]{2,1,0:T(8,128)S(1)}, f32[4,16,128]{2,1,0:T(8,128)S(1)}, u32[]{:S(2)}, u32[]{:S(2)}) collective-permute-start(f32[4,16,128]{2,1,0:T(8,128)S(1)} %get-tuple-element.30), channel_id=1, source_target_pairs={{0,3},{1,0},{2,1},{3,2},{4,7},{5,4},{6,5},{7,6},{8,11},{9,8},{10,9... | collective-permute-start | bytes 98312 | tf_op jit(solution)/shard_map/ppermute | solution.py:231
  37.4 4.6 %collective-permute-start.7 = (f32[4,16,128]{2,1,0:T(8,128)S(1)}, f32[4,16,128]{2,1,0:T(8,128)S(1)}, u32[]{:S(2)}, u32[]{:S(2)}) collective-permute-start(f32[4,16,128]{2,1,0:T(8,128)S(1)} %get-tuple-element.31), channel_id=1, source_target_pairs={{0,2},{1,3},{2,0},{3,1},{4,6},{5,7},{6,4},{7,5},{8,10},{9,11},{10,... | collective-permute-start | bytes 98312 | tf_op jit(solution)/shard_map/ppermute | solution.py:231

commit v6 on v5

--- a/solution.py
+++ b/solution.py
@@ -177,6 +177,11 @@
     dual[...] = jnp.stack([sums[2], sums[3]], axis=1).astype(BF16)
 
 
+def turn(index):
+    z, y, core = index // 8, (index // 2) % 4, index % 2
+    return z * 8 + (y + (z % 2) * (3 - 2 * y)) * 2 + (core + (y % 2) * (1 - 2 * core))
+
+
 SMEM = pl.BlockSpec(memory_space=pltpu.SMEM)
 VMEM = pl.BlockSpec(memory_space=pltpu.VMEM)
 ANY = pl.BlockSpec(memory_space=pl.ANY)
@@ -253,7 +258,7 @@
     owner = cols // per_dev
     earlier = (owner[:, None] == owner[None, :]) & (jnp.arange(128)[None, :] < jnp.arange(128)[:, None])
     order = jnp.sum(earlier.astype(jnp.int32), axis=1)
-    slot = jnp.broadcast_to((owner * 4 + order)[None, :], (8, 128))
+    slot = jnp.broadcast_to((turn(owner) * 4 + order)[None, :], (8, 128))
     place = jnp.broadcast_to((order * 16 + cols % per_dev)[:, None], (128, 128))
     sent = pl.pallas_call(
         send_kernel,
@@ -281,7 +286,8 @@
         name="merge",
     )(*(v.reshape(per_dev * 16, 128) for v in (mid, got_pair, got_other)))
     near_got = over_sub(near)
-    got = lax.all_to_all(sent.reshape(count * 17, 1, 128), "cluster", 0, 0, tiled=True)
+    path = sorted(range(count), key=turn)
+    got = lax.all_to_all(sent.reshape(count * 17, 1, 128), "cluster", 0, 0, axis_index_groups=[path], tiled=True)
     efie, dual = pl.pallas_call(
         sum_kernel,
         in_specs=[VMEM] * 5,

time: 54.1 us -> 53.3 us (0.985)
  waiting for transfers between devices: 17.5 us -> 16.6 us
    all_to_all x1, waiting for transfers between devices: 10.9 us -> 10.1 us  [per_device(): lax.all_to_all(sent.reshape(count * 17, 1, 128), 'cluster', 0, 0, axis_in...]
where the time goes in v6:
time: 53.3 us; the launch traced here: 53 us
  starting transfers between devices  26 us (49%)
  waiting for transfers between devices  16.6 us (31%)
  Pallas kernels  9.16 us (17%)
  between operations  0.72 us (1%)
    all_to_all x1, starting transfers between devices, per_device(): lax.all_to_all(sent.reshape(count * 17, 1, 128), 'cluster', 0, 0, axis_in...  13.2 us
    all_to_all x1, waiting for transfers between devices, per_device(): lax.all_to_all(sent.reshape(count * 17, 1, 128), 'cluster', 0, 0, axis_in...  10.1 us
    ppermute x6, starting transfers between devices, over_sub(): lax.ppermute(parts[k], 'sub', shift(k))  8.08 us
    ppermute x6, waiting for transfers between devices, over_sub(): lax.ppermute(parts[k], 'sub', shift(k))  6.52 us
    pallas_call x1, Pallas kernels, per_device(): pl.pallas_call(functools.partial(far_kernel, chunk), in_specs=[SMEM, SMEM...  3.56 us
    pallas_call x1, Pallas kernels, per_device(): pl.pallas_call(functools.partial(near_kernel, chunk), in_specs=[SMEM, SME...  3.45 us
    ppermute x1, starting transfers between devices, per_device(): got_other = lax.ppermute(other, 'cluster', between)  3.1 us
    ppermute x1, starting transfers between devices, per_device(): got_pair = lax.ppermute(pair, 'cluster', within)  1.6 us
  transfers between devices with their start and end apart: 9, of which 4 were waited for; matrix products, arithmetic and copies ran while one was open for 1% of the time, Pallas kernels for 7%

profile of v6, /device:TPU:1, one launch (start us, length us, event | category | flops | bytes accessed | tf_op | source)
XLA Modules:
  0.0 53.0 jit_solution(17933154311143666798)
XLA Ops:
  0.6 3.6 %far.1 = (f32[4,128,128]{2,1,0:T(8,128)S(1)}, f32[4,128,128]{2,1,0:T(8,128)S(1)}, f32[4,128,128]{2,1,0:T(8,128)S(1)}, f32[4,128,128]{2,1,0:T(8,128)S(1)}) custom-call(s32[1]{0:T(128)} %bitcast.me_ref, s32[8,16]{1,0:T(8,128)} %bitcast.24, bf16[128,128]{1,0:T(8,128)(2,1)} %bitcast.22, bf16[16,8,2,16,128]{4,3,2,1,0:T(8,128)(2,1)} %le.1, ...), custom_call_target="tpu_custom_call" | custom-call | flops 200000000 | bytes 5300000 | tf_op jit(solution)/shard_map/far/pallas_call | solution.py:220
  4.2 2.1 %collective-permute-start = (f32[4,128,128]{2,1,0:T(8,128)S(1)}, f32[4,128,128]{2,1,0:T(8,128)S(1)}, u32[]{:S(2)}, u32[]{:S(2)}) collective-permute-start(f32[4,128,128]{2,1,0:T(8,128)S(1)} %get-tuple-element.19), channel_id=1, source_target_pairs={{0,1},{1,2},{2,3},{3,0},{4,5},{5,6},{6,7},{7,4},{8,9},{9,10},{10,1... | collective-permute-start | bytes 786440 | tf_op jit(solution)/shard_map/ppermute | solution.py:236
  6.3 1.4 %collective-permute-start.1 = (f32[4,128,128]{2,1,0:T(8,128)S(1)}, f32[4,128,128]{2,1,0:T(8,128)S(1)}, u32[]{:S(2)}, u32[]{:S(2)}) collective-permute-start(f32[4,128,128]{2,1,0:T(8,128)S(1)} %get-tuple-element.20), channel_id=1, source_target_pairs={{0,3},{1,0},{2,1},{3,2},{4,7},{5,4},{6,5},{7,6},{8,11},{9,8},{10,9... | collective-permute-start | bytes 786440 | tf_op jit(solution)/shard_map/ppermute | solution.py:236
  7.7 1.6 %collective-permute-start.2 = (f32[4,128,128]{2,1,0:T(8,128)S(1)}, f32[4,128,128]{2,1,0:T(8,128)S(1)}, u32[]{:S(2)}, u32[]{:S(2)}) collective-permute-start(f32[4,128,128]{2,1,0:T(8,128)S(1)} %get-tuple-element.21), channel_id=1, source_target_pairs={{0,2},{1,3},{2,0},{3,1},{4,6},{5,7},{6,4},{7,5},{8,10},{9,11},{10,... | collective-permute-start | bytes 786440 | tf_op jit(solution)/shard_map/ppermute | solution.py:236
  9.3 3.4 %near.1 = (f32[16,2,8,128]{3,2,1,0:T(8,128)S(1)}, f32[16,2,8,128]{3,2,1,0:T(8,128)S(1)}, f32[16,2,8,128]{3,2,1,0:T(8,128)S(1)}) custom-call(s32[1]{0:T(128)} %bitcast.me_ref, s32[1]{0:T(128)} %bitcast.3.base_ref, s32[2,16]{1,0:T(2,128)} %bitcast.25, bf16[128,128]{1,0:T(8,128)(2,1)} %bitcast.23, bf16[16,2,2,128,128]{4,3,2,1,0:T(8,128)(2,1)} %de.1, ...), custom_call_target="tpu_custom_call" | custom-call | flops 200000000 | bytes 4600000 | tf_op jit(solution)/shard_map/near/pallas_call | solution.py:240
  12.8 1.6 %collective-permute-start.3 = (f32[16,2,8,128]{3,2,1,0:T(8,128)S(1)}, f32[16,2,8,128]{3,2,1,0:T(8,128)S(1)}, u32[]{:S(2)}, u32[]{:S(2)}) collective-permute-start(f32[16,2,8,128]{3,2,1,0:T(8,128)S(1)} %get-tuple-element.22), channel_id=1, source_target_pairs={{0,4},{4,0},{8,12},{12,8},{16,20},{20,16},{24,28},{28,24},{32,36},... | collective-permute-start | bytes 393224 | tf_op jit(solution)/shard_map/ppermute | solution.py:254
  14.4 3.1 %collective-permute-start.4 = (f32[16,2,8,128]{3,2,1,0:T(8,128)S(1)}, f32[16,2,8,128]{3,2,1,0:T(8,128)S(1)}, u32[]{:S(2)}, u32[]{:S(2)}) collective-permute-start(f32[16,2,8,128]{3,2,1,0:T(8,128)S(1)} %get-tuple-element.23), channel_id=1, source_target_pairs={{4,8},{12,16},{20,24},{28,32},{36,40},{44,48},{52,56},{60,64},{68,... | collective-permute-start | bytes 393224 | tf_op jit(solution)/shard_map/ppermute | solution.py:255
  17.5 0.1 copy.25
  17.6 0.1 reshape.212
  17.7 0.2 convert_reduce_fusion
  17.9 0.0 collective-permute-done.b
  17.9 2.2 %collective-permute-done.2.d = f32[4,128,128]{2,1,0:T(8,128)S(1)} collective-permute-done((f32[4,128,128]{2,1,0:T(8,128)S(1)}, f32[4,128,128]{2,1,0:T(8,128)S(1)}, u32[]{:S(2)}, u32[]{:S(2)}) %collective-permute-start.2) | collective-permute-done | bytes 262176 | tf_op jit(solution)/shard_map/ppermute | solution.py:236
  20.1 0.1 broadcast_in_dim.5.cols_ref
  20.2 1.1 %send.1.refs_0_ = f32[1088,128]{1,0:T(8,128)} custom-call(s32[8,128]{1,0:T(8,128)S(1)} %broadcast_in_dim.4.slot_ref, s32[128,128]{1,0:T(8,128)S(1)} %broadcast_in_dim.5.cols_ref, f32[4,128,128]{2,1,0:T(8,128)S(1)} %get-tuple-element.18.a.after, f32[4,128,128]{2,1,0:T(8,128)S(1)} %collective-permute-done.b, f32[4,128,128]{2,1,0:T(8,128)S(1)} %collective-permute-done.1.c, ...), custom_call_target="tpu_custom_call" | custom-call | tf_op jit(solution)/shard_map/send/pallas_call | solution.py:263
  21.3 0.0 collective-permute-done.3.refs_1_
  21.3 13.2 %all-to-all-start = ((f32[1088,1,128]{2,1,0:T(1,128)}), f32[1088,1,128]{2,1,0:T(1,128)S(1)}, u32[]{:S(2)}, u32[]{:S(2)}) async-start(f32[1088,1,128]{2,1,0:T(1,128)} %bitcast.6), calls=%async_computation | async-start | bytes 1114112 | tf_op jit(solution)/shard_map/all_to_all | solution.py:290
  34.5 0.1 merge.1
  34.6 0.9 %collective-permute-start.5 = (f32[4,16,128]{2,1,0:T(8,128)S(1)}, f32[4,16,128]{2,1,0:T(8,128)S(1)}, u32[]{:S(2)}, u32[]{:S(2)}) collective-permute-start(f32[4,16,128]{2,1,0:T(8,128)S(1)} %get-tuple-element.29), channel_id=1, source_target_pairs={{0,1},{1,2},{2,3},{3,0},{4,5},{5,6},{6,7},{7,4},{8,9},{9,10},{10,1... | collective-permute-start | bytes 98312 | tf_op jit(solution)/shard_map/ppermute | solution.py:236
  35.5 1.8 %collective-permute-start.6 = (f32[4,16,128]{2,1,0:T(8,128)S(1)}, f32[4,16,128]{2,1,0:T(8,128)S(1)}, u32[]{:S(2)}, u32[]{:S(2)}) collective-permute-start(f32[4,16,128]{2,1,0:T(8,128)S(1)} %get-tuple-element.30), channel_id=1, source_target_pairs={{0,3},{1,0},{2,1},{3,2},{4,7},{5,4},{6,5},{7,6},{8,11},{9,8},{10,9... | collective-permute-start | bytes 98312 | tf_op jit(solution)/shard_map/ppermute | solution.py:236
  37.4 0.2 collective-permute-start.7
  37.6 1.4 %collective-permute-done.5.nb = f32[4,16,128]{2,1,0:T(8,128)S(1)} collective-permute-done((f32[4,16,128]{2,1,0:T(8,128)S(1)}, f32[4,16,128]{2,1,0:T(8,128)S(1)}, u32[]{:S(2)}, u32[]{:S(2)}) %collective-permute-start.5) | collective-permute-done | bytes 32800 | tf_op jit(solution)/shard_map/ppermute | solution.py:236
  38.9 3.0 %collective-permute-done.7.nd = f32[4,16,128]{2,1,0:T(8,128)S(1)} collective-permute-done((f32[4,16,128]{2,1,0:T(8,128)S(1)}, f32[4,16,128]{2,1,0:T(8,128)S(1)}, u32[]{:S(2)}, u32[]{:S(2)}) %collective-permute-start.7) | collective-permute-done | bytes 32800 | tf_op jit(solution)/shard_map/ppermute | solution.py:236
  41.9 10.1 %all-to-all-done = f32[1088,1,128]{2,1,0:T(1,128)S(1)} async-done(((f32[1088,1,128]{2,1,0:T(1,128)}), f32[1088,1,128]{2,1,0:T(1,128)S(1)}, u32[]{:S(2)}, u32[]{:S(2)}) %all-to-all-start) | async-done | bytes 557088 | tf_op jit(solution)/shard_map/all_to_all | solution.py:290
  52.0 0.9 %total.1 = (bf16[16,2,128]{2,1,0:T(2,128)(2,1)}, bf16[16,2,128]{2,1,0:T(2,128)(2,1)}) custom-call(f32[1088,128]{1,0:T(8,128)S(1)} %bitcast.18, f32[4,16,128]{2,1,0:T(8,128)S(1)} %get-tuple-element.28.na, f32[4,16,128]{2,1,0:T(8,128)S(1)} %collective-permute-done.5.nb, f32[4,16,128]{2,1,0:T(8,128)S(1)} %collective-permute-done.6.nc, ...), custom_call_target="tpu_custom_call" | custom-call | tf_op jit(solution)/shard_map/total/pallas_call | solution.py:291
  (9 shorter events, 0.1 us)
Async XLA Ops:
  4.2 13.7 %collective-permute-start = (f32[4,128,128]{2,1,0:T(8,128)S(1)}, f32[4,128,128]{2,1,0:T(8,128)S(1)}, u32[]{:S(2)}, u32[]{:S(2)}) collective-permute-start(f32[4,128,128]{2,1,0:T(8,128)S(1)} %get-tuple-element.19), channel_id=1, source_target_pairs={{0,1},{1,2},{2,3},{3,0},{4,5},{5,6},{6,7},{7,4},{8,9},{9,10},{10,1... | collective-permute-start | bytes 786440 | tf_op jit(solution)/shard_map/ppermute | solution.py:236
  6.3 11.6 %collective-permute-start.1 = (f32[4,128,128]{2,1,0:T(8,128)S(1)}, f32[4,128,128]{2,1,0:T(8,128)S(1)}, u32[]{:S(2)}, u32[]{:S(2)}) collective-permute-start(f32[4,128,128]{2,1,0:T(8,128)S(1)} %get-tuple-element.20), channel_id=1, source_target_pairs={{0,3},{1,0},{2,1},{3,2},{4,7},{5,4},{6,5},{7,6},{8,11},{9,8},{10,9... | collective-permute-start | bytes 786440 | tf_op jit(solution)/shard_map/ppermute | solution.py:236
  7.7 12.4 %collective-permute-start.2 = (f32[4,128,128]{2,1,0:T(8,128)S(1)}, f32[4,128,128]{2,1,0:T(8,128)S(1)}, u32[]{:S(2)}, u32[]{:S(2)}) collective-permute-start(f32[4,128,128]{2,1,0:T(8,128)S(1)} %get-tuple-element.21), channel_id=1, source_target_pairs={{0,2},{1,3},{2,0},{3,1},{4,6},{5,7},{6,4},{7,5},{8,10},{9,11},{10,... | collective-permute-start | bytes 786440 | tf_op jit(solution)/shard_map/ppermute | solution.py:236
  9.3 8.2 %copy-start = (s32[16,8]{0,1:T(8,128)S(1)}, s32[16,8]{0,1:T(8,128)}, u32[]{:S(2)}) copy-start(s32[16,8]{0,1:T(8,128)} %param.16) | copy-start | bytes 1540
  12.8 8.5 %collective-permute-start.3 = (f32[16,2,8,128]{3,2,1,0:T(8,128)S(1)}, f32[16,2,8,128]{3,2,1,0:T(8,128)S(1)}, u32[]{:S(2)}, u32[]{:S(2)}) collective-permute-start(f32[16,2,8,128]{3,2,1,0:T(8,128)S(1)} %get-tuple-element.22), channel_id=1, source_target_pairs={{0,4},{4,0},{8,12},{12,8},{16,20},{20,16},{24,28},{28,24},{32,36},... | collective-permute-start | bytes 393224 | tf_op jit(solution)/shard_map/ppermute | solution.py:254
  14.4 6.9 %collective-permute-start.4 = (f32[16,2,8,128]{3,2,1,0:T(8,128)S(1)}, f32[16,2,8,128]{3,2,1,0:T(8,128)S(1)}, u32[]{:S(2)}, u32[]{:S(2)}) collective-permute-start(f32[16,2,8,128]{3,2,1,0:T(8,128)S(1)} %get-tuple-element.23), channel_id=1, source_target_pairs={{4,8},{12,16},{20,24},{28,32},{36,40},{44,48},{52,56},{60,64},{68,... | collective-permute-start | bytes 393224 | tf_op jit(solution)/shard_map/ppermute | solution.py:255
  21.3 30.7 %all-to-all-start = ((f32[1088,1,128]{2,1,0:T(1,128)}), f32[1088,1,128]{2,1,0:T(1,128)S(1)}, u32[]{:S(2)}, u32[]{:S(2)}) async-start(f32[1088,1,128]{2,1,0:T(1,128)} %bitcast.6), calls=%async_computation | async-start | bytes 1114112 | tf_op jit(solution)/shard_map/all_to_all | solution.py:290
  34.6 4.3 %collective-permute-start.5 = (f32[4,16,128]{2,1,0:T(8,128)S(1)}, f32[4,16,128]{2,1,0:T(8,128)S(1)}, u32[]{:S(2)}, u32[]{:S(2)}) collective-permute-start(f32[4,16,128]{2,1,0:T(8,128)S(1)} %get-tuple-element.29), channel_id=1, source_target_pairs={{0,1},{1,2},{2,3},{3,0},{4,5},{5,6},{6,7},{7,4},{8,9},{9,10},{10,1... | collective-permute-start | bytes 98312 | tf_op jit(solution)/shard_map/ppermute | solution.py:236
  35.5 3.4 %collective-permute-start.6 = (f32[4,16,128]{2,1,0:T(8,128)S(1)}, f32[4,16,128]{2,1,0:T(8,128)S(1)}, u32[]{:S(2)}, u32[]{:S(2)}) collective-permute-start(f32[4,16,128]{2,1,0:T(8,128)S(1)} %get-tuple-element.30), channel_id=1, source_target_pairs={{0,3},{1,0},{2,1},{3,2},{4,7},{5,4},{6,5},{7,6},{8,11},{9,8},{10,9... | collective-permute-start | bytes 98312 | tf_op jit(solution)/shard_map/ppermute | solution.py:236
  37.4 4.6 %collective-permute-start.7 = (f32[4,16,128]{2,1,0:T(8,128)S(1)}, f32[4,16,128]{2,1,0:T(8,128)S(1)}, u32[]{:S(2)}, u32[]{:S(2)}) collective-permute-start(f32[4,16,128]{2,1,0:T(8,128)S(1)} %get-tuple-element.31), channel_id=1, source_target_pairs={{0,2},{1,3},{2,0},{3,1},{4,6},{5,7},{6,4},{7,5},{8,10},{9,11},{10,... | collective-permute-start | bytes 98312 | tf_op jit(solution)/shard_map/ppermute | solution.py:236

commit v7 on v6

--- a/solution.py
+++ b/solution.py
@@ -179,7 +179,7 @@
 
 def turn(index):
     z, y, core = index // 8, (index // 2) % 4, index % 2
-    return z * 8 + (y + (z % 2) * (3 - 2 * y)) * 2 + (core + (y % 2) * (1 - 2 * core))
+    return 63 - z * 8 - (y + (z % 2) * (3 - 2 * y)) * 2 - (core + (y % 2) * (1 - 2 * core))
 
 
 SMEM = pl.BlockSpec(memory_space=pltpu.SMEM)
@@ -251,8 +251,8 @@
     count = lax.axis_size("cluster")
     within = [(i, i ^ 1) for i in range(count)]
     between = [(i, i + 1) for i in range(1, count - 1, 2)] + [(i + 1, i) for i in range(1, count - 1, 2)]
+    got_other = lax.ppermute(other, "cluster", between)
     got_pair = lax.ppermute(pair, "cluster", within)
-    got_other = lax.ppermute(other, "cluster", between)
 
     cols = far_cols.reshape(-1)
     owner = cols // per_dev
@@ -268,7 +268,7 @@
         compiler_params=small,
         name="send",
     )(slot, place, *far_got)
-    sent, got_pair, got_other = pl.pallas_call(
+    sent, got_other, got_pair = pl.pallas_call(
         lambda *refs: None,
         in_specs=[ANY] * 3,
         out_specs=[ANY] * 3,
@@ -276,7 +276,7 @@
         input_output_aliases={0: 0, 1: 1, 2: 2},
         compiler_params=small,
         name="join",
-    )(sent, got_pair, got_other)
+    )(sent, got_other, got_pair)
     near = pl.pallas_call(
         merge_kernel,
         in_specs=[VMEM] * 3,

time: 53.3 us -> 51.8 us (0.972)
  waiting for transfers between devices: 16.6 us -> 15 us
    all_to_all x1, waiting for transfers between devices: 10.1 us -> 8.47 us  [per_device(): lax.all_to_all(sent.reshape(count * 17, 1, 128), 'cluster', 0, 0, axis_in...]
    ppermute x1, starting transfers between devices: 1.6 us -> 0.09 us  [per_device(): got_pair = lax.ppermute(pair, 'cluster', within)]
    ppermute x1, starting transfers between devices: 3.1 us -> 4.6 us  [per_device(): got_other = lax.ppermute(other, 'cluster', between)]
where the time goes in v7:
time: 51.8 us; the launch traced here: 51.5 us
  starting transfers between devices  26.2 us (51%)
  waiting for transfers between devices  15 us (29%)
  Pallas kernels  9.15 us (18%)
  between operations  0.73 us (1%)
    all_to_all x1, starting transfers between devices, per_device(): lax.all_to_all(sent.reshape(count * 17, 1, 128), 'cluster', 0, 0, axis_in...  13.4 us
    all_to_all x1, waiting for transfers between devices, per_device(): lax.all_to_all(sent.reshape(count * 17, 1, 128), 'cluster', 0, 0, axis_in...  8.47 us
    ppermute x6, starting transfers between devices, over_sub(): lax.ppermute(parts[k], 'sub', shift(k))  8.08 us
    ppermute x6, waiting for transfers between devices, over_sub(): lax.ppermute(parts[k], 'sub', shift(k))  6.52 us
    ppermute x1, starting transfers between devices, per_device(): got_other = lax.ppermute(other, 'cluster', between)  4.6 us
    pallas_call x1, Pallas kernels, per_device(): pl.pallas_call(functools.partial(far_kernel, chunk), in_specs=[SMEM, SMEM...  3.56 us
    pallas_call x1, Pallas kernels, per_device(): pl.pallas_call(functools.partial(near_kernel, chunk), in_specs=[SMEM, SME...  3.45 us
    pallas_call x1, Pallas kernels, per_device(): pl.pallas_call(send_kernel, in_specs=[VMEM] * 6, out_specs=VMEM, out_shap...  1.09 us
  transfers between devices with their start and end apart: 9, of which 4 were waited for; matrix products, arithmetic and copies ran while one was open for 1% of the time, Pallas kernels for 7%

profile of v7, /device:TPU:1, one launch (start us, length us, event | category | flops | bytes accessed | tf_op | source)
XLA Modules:
  0.0 51.5 jit_solution(6823115941719753948)
XLA Ops:
  0.6 3.6 %far.1 = (f32[4,128,128]{2,1,0:T(8,128)S(1)}, f32[4,128,128]{2,1,0:T(8,128)S(1)}, f32[4,128,128]{2,1,0:T(8,128)S(1)}, f32[4,128,128]{2,1,0:T(8,128)S(1)}) custom-call(s32[1]{0:T(128)} %bitcast.me_ref, s32[8,16]{1,0:T(8,128)} %bitcast.24, bf16[128,128]{1,0:T(8,128)(2,1)} %bitcast.22, bf16[16,8,2,16,128]{4,3,2,1,0:T(8,128)(2,1)} %le.1, ...), custom_call_target="tpu_custom_call" | custom-call | flops 200000000 | bytes 5300000 | tf_op jit(solution)/shard_map/far/pallas_call | solution.py:220
  4.2 2.1 %collective-permute-start = (f32[4,128,128]{2,1,0:T(8,128)S(1)}, f32[4,128,128]{2,1,0:T(8,128)S(1)}, u32[]{:S(2)}, u32[]{:S(2)}) collective-permute-start(f32[4,128,128]{2,1,0:T(8,128)S(1)} %get-tuple-element.19), channel_id=1, source_target_pairs={{0,1},{1,2},{2,3},{3,0},{4,5},{5,6},{6,7},{7,4},{8,9},{9,10},{10,1... | collective-permute-start | bytes 786440 | tf_op jit(solution)/shard_map/ppermute | solution.py:236
  6.3 1.4 %collective-permute-start.1 = (f32[4,128,128]{2,1,0:T(8,128)S(1)}, f32[4,128,128]{2,1,0:T(8,128)S(1)}, u32[]{:S(2)}, u32[]{:S(2)}) collective-permute-start(f32[4,128,128]{2,1,0:T(8,128)S(1)} %get-tuple-element.20), channel_id=1, source_target_pairs={{0,3},{1,0},{2,1},{3,2},{4,7},{5,4},{6,5},{7,6},{8,11},{9,8},{10,9... | collective-permute-start | bytes 786440 | tf_op jit(solution)/shard_map/ppermute | solution.py:236
  7.7 1.6 %collective-permute-start.2 = (f32[4,128,128]{2,1,0:T(8,128)S(1)}, f32[4,128,128]{2,1,0:T(8,128)S(1)}, u32[]{:S(2)}, u32[]{:S(2)}) collective-permute-start(f32[4,128,128]{2,1,0:T(8,128)S(1)} %get-tuple-element.21), channel_id=1, source_target_pairs={{0,2},{1,3},{2,0},{3,1},{4,6},{5,7},{6,4},{7,5},{8,10},{9,11},{10,... | collective-permute-start | bytes 786440 | tf_op jit(solution)/shard_map/ppermute | solution.py:236
  9.3 3.4 %near.1 = (f32[16,2,8,128]{3,2,1,0:T(8,128)S(1)}, f32[16,2,8,128]{3,2,1,0:T(8,128)S(1)}, f32[16,2,8,128]{3,2,1,0:T(8,128)S(1)}) custom-call(s32[1]{0:T(128)} %bitcast.me_ref, s32[1]{0:T(128)} %bitcast.3.base_ref, s32[2,16]{1,0:T(2,128)} %bitcast.25, bf16[128,128]{1,0:T(8,128)(2,1)} %bitcast.23, bf16[16,2,2,128,128]{4,3,2,1,0:T(8,128)(2,1)} %de.1, ...), custom_call_target="tpu_custom_call" | custom-call | flops 200000000 | bytes 4600000 | tf_op jit(solution)/shard_map/near/pallas_call | solution.py:240
  12.8 4.6 %collective-permute-start.3 = (f32[16,2,8,128]{3,2,1,0:T(8,128)S(1)}, f32[16,2,8,128]{3,2,1,0:T(8,128)S(1)}, u32[]{:S(2)}, u32[]{:S(2)}) collective-permute-start(f32[16,2,8,128]{3,2,1,0:T(8,128)S(1)} %get-tuple-element.22), channel_id=1, source_target_pairs={{4,8},{12,16},{20,24},{28,32},{36,40},{44,48},{52,56},{60,64},{68,... | collective-permute-start | bytes 393224 | tf_op jit(solution)/shard_map/ppermute | solution.py:254
  17.4 0.1 collective-permute-start.4
  17.5 0.1 copy.25
  17.6 0.1 reshape.213
  17.7 0.2 convert_reduce_fusion
  17.9 0.0 collective-permute-done.b
  17.9 2.2 %collective-permute-done.2.d = f32[4,128,128]{2,1,0:T(8,128)S(1)} collective-permute-done((f32[4,128,128]{2,1,0:T(8,128)S(1)}, f32[4,128,128]{2,1,0:T(8,128)S(1)}, u32[]{:S(2)}, u32[]{:S(2)}) %collective-permute-start.2) | collective-permute-done | bytes 262176 | tf_op jit(solution)/shard_map/ppermute | solution.py:236
  20.1 0.1 broadcast_in_dim.5.cols_ref
  20.2 1.1 %send.1.refs_0_ = f32[1088,128]{1,0:T(8,128)} custom-call(s32[8,128]{1,0:T(8,128)S(1)} %broadcast_in_dim.4.slot_ref, s32[128,128]{1,0:T(8,128)S(1)} %broadcast_in_dim.5.cols_ref, f32[4,128,128]{2,1,0:T(8,128)S(1)} %get-tuple-element.18.a.after, f32[4,128,128]{2,1,0:T(8,128)S(1)} %collective-permute-done.b, f32[4,128,128]{2,1,0:T(8,128)S(1)} %collective-permute-done.1.c, ...), custom_call_target="tpu_custom_call" | custom-call | tf_op jit(solution)/shard_map/send/pallas_call | solution.py:263
  21.3 0.0 collective-permute-done.3.refs_1_
  21.3 13.4 %all-to-all-start = ((f32[1088,1,128]{2,1,0:T(1,128)}), f32[1088,1,128]{2,1,0:T(1,128)S(1)}, u32[]{:S(2)}, u32[]{:S(2)}) async-start(f32[1088,1,128]{2,1,0:T(1,128)} %bitcast.6), calls=%async_computation | async-start | bytes 1114112 | tf_op jit(solution)/shard_map/all_to_all | solution.py:290
  34.7 0.1 merge.1
  34.8 0.9 %collective-permute-start.5 = (f32[4,16,128]{2,1,0:T(8,128)S(1)}, f32[4,16,128]{2,1,0:T(8,128)S(1)}, u32[]{:S(2)}, u32[]{:S(2)}) collective-permute-start(f32[4,16,128]{2,1,0:T(8,128)S(1)} %get-tuple-element.29), channel_id=1, source_target_pairs={{0,1},{1,2},{2,3},{3,0},{4,5},{5,6},{6,7},{7,4},{8,9},{9,10},{10,1... | collective-permute-start | bytes 98312 | tf_op jit(solution)/shard_map/ppermute | solution.py:236
  35.7 1.8 %collective-permute-start.6 = (f32[4,16,128]{2,1,0:T(8,128)S(1)}, f32[4,16,128]{2,1,0:T(8,128)S(1)}, u32[]{:S(2)}, u32[]{:S(2)}) collective-permute-start(f32[4,16,128]{2,1,0:T(8,128)S(1)} %get-tuple-element.30), channel_id=1, source_target_pairs={{0,3},{1,0},{2,1},{3,2},{4,7},{5,4},{6,5},{7,6},{8,11},{9,8},{10,9... | collective-permute-start | bytes 98312 | tf_op jit(solution)/shard_map/ppermute | solution.py:236
  37.5 0.2 collective-permute-start.7
  37.8 1.4 %collective-permute-done.5.nb = f32[4,16,128]{2,1,0:T(8,128)S(1)} collective-permute-done((f32[4,16,128]{2,1,0:T(8,128)S(1)}, f32[4,16,128]{2,1,0:T(8,128)S(1)}, u32[]{:S(2)}, u32[]{:S(2)}) %collective-permute-start.5) | collective-permute-done | bytes 32800 | tf_op jit(solution)/shard_map/ppermute | solution.py:236
  39.1 3.0 %collective-permute-done.7.nd = f32[4,16,128]{2,1,0:T(8,128)S(1)} collective-permute-done((f32[4,16,128]{2,1,0:T(8,128)S(1)}, f32[4,16,128]{2,1,0:T(8,128)S(1)}, u32[]{:S(2)}, u32[]{:S(2)}) %collective-permute-start.7) | collective-permute-done | bytes 32800 | tf_op jit(solution)/shard_map/ppermute | solution.py:236
  42.1 8.5 %all-to-all-done = f32[1088,1,128]{2,1,0:T(1,128)S(1)} async-done(((f32[1088,1,128]{2,1,0:T(1,128)}), f32[1088,1,128]{2,1,0:T(1,128)S(1)}, u32[]{:S(2)}, u32[]{:S(2)}) %all-to-all-start) | async-done | bytes 557088 | tf_op jit(solution)/shard_map/all_to_all | solution.py:290
  50.6 0.9 %total.1 = (bf16[16,2,128]{2,1,0:T(2,128)(2,1)}, bf16[16,2,128]{2,1,0:T(2,128)(2,1)}) custom-call(f32[1088,128]{1,0:T(8,128)S(1)} %bitcast.18, f32[4,16,128]{2,1,0:T(8,128)S(1)} %get-tuple-element.28.na, f32[4,16,128]{2,1,0:T(8,128)S(1)} %collective-permute-done.5.nb, f32[4,16,128]{2,1,0:T(8,128)S(1)} %collective-permute-done.6.nc, ...), custom_call_target="tpu_custom_call" | custom-call | tf_op jit(solution)/shard_map/total/pallas_call | solution.py:291
  (9 shorter events, 0.1 us)
Async XLA Ops:
  4.2 13.7 %collective-permute-start = (f32[4,128,128]{2,1,0:T(8,128)S(1)}, f32[4,128,128]{2,1,0:T(8,128)S(1)}, u32[]{:S(2)}, u32[]{:S(2)}) collective-permute-start(f32[4,128,128]{2,1,0:T(8,128)S(1)} %get-tuple-element.19), channel_id=1, source_target_pairs={{0,1},{1,2},{2,3},{3,0},{4,5},{5,6},{6,7},{7,4},{8,9},{9,10},{10,1... | collective-permute-start | bytes 786440 | tf_op jit(solution)/shard_map/ppermute | solution.py:236
  6.3 11.6 %collective-permute-start.1 = (f32[4,128,128]{2,1,0:T(8,128)S(1)}, f32[4,128,128]{2,1,0:T(8,128)S(1)}, u32[]{:S(2)}, u32[]{:S(2)}) collective-permute-start(f32[4,128,128]{2,1,0:T(8,128)S(1)} %get-tuple-element.20), channel_id=1, source_target_pairs={{0,3},{1,0},{2,1},{3,2},{4,7},{5,4},{6,5},{7,6},{8,11},{9,8},{10,9... | collective-permute-start | bytes 786440 | tf_op jit(solution)/shard_map/ppermute | solution.py:236
  7.7 12.4 %collective-permute-start.2 = (f32[4,128,128]{2,1,0:T(8,128)S(1)}, f32[4,128,128]{2,1,0:T(8,128)S(1)}, u32[]{:S(2)}, u32[]{:S(2)}) collective-permute-start(f32[4,128,128]{2,1,0:T(8,128)S(1)} %get-tuple-element.21), channel_id=1, source_target_pairs={{0,2},{1,3},{2,0},{3,1},{4,6},{5,7},{6,4},{7,5},{8,10},{9,11},{10,... | collective-permute-start | bytes 786440 | tf_op jit(solution)/shard_map/ppermute | solution.py:236
  9.3 8.2 %copy-start = (s32[16,8]{0,1:T(8,128)S(1)}, s32[16,8]{0,1:T(8,128)}, u32[]{:S(2)}) copy-start(s32[16,8]{0,1:T(8,128)} %param.16) | copy-start | bytes 1540
  12.8 8.5 %collective-permute-start.3 = (f32[16,2,8,128]{3,2,1,0:T(8,128)S(1)}, f32[16,2,8,128]{3,2,1,0:T(8,128)S(1)}, u32[]{:S(2)}, u32[]{:S(2)}) collective-permute-start(f32[16,2,8,128]{3,2,1,0:T(8,128)S(1)} %get-tuple-element.22), channel_id=1, source_target_pairs={{4,8},{12,16},{20,24},{28,32},{36,40},{44,48},{52,56},{60,64},{68,... | collective-permute-start | bytes 393224 | tf_op jit(solution)/shard_map/ppermute | solution.py:254
  17.4 3.9 %collective-permute-start.4 = (f32[16,2,8,128]{3,2,1,0:T(8,128)S(1)}, f32[16,2,8,128]{3,2,1,0:T(8,128)S(1)}, u32[]{:S(2)}, u32[]{:S(2)}) collective-permute-start(f32[16,2,8,128]{3,2,1,0:T(8,128)S(1)} %get-tuple-element.23), channel_id=1, source_target_pairs={{0,4},{4,0},{8,12},{12,8},{16,20},{20,16},{24,28},{28,24},{32,36},... | collective-permute-start | bytes 393224 | tf_op jit(solution)/shard_map/ppermute | solution.py:255
  21.3 29.3 %all-to-all-start = ((f32[1088,1,128]{2,1,0:T(1,128)}), f32[1088,1,128]{2,1,0:T(1,128)S(1)}, u32[]{:S(2)}, u32[]{:S(2)}) async-start(f32[1088,1,128]{2,1,0:T(1,128)} %bitcast.6), calls=%async_computation | async-start | bytes 1114112 | tf_op jit(solution)/shard_map/all_to_all | solution.py:290
  34.8 4.3 %collective-permute-start.5 = (f32[4,16,128]{2,1,0:T(8,128)S(1)}, f32[4,16,128]{2,1,0:T(8,128)S(1)}, u32[]{:S(2)}, u32[]{:S(2)}) collective-permute-start(f32[4,16,128]{2,1,0:T(8,128)S(1)} %get-tuple-element.29), channel_id=1, source_target_pairs={{0,1},{1,2},{2,3},{3,0},{4,5},{5,6},{6,7},{7,4},{8,9},{9,10},{10,1... | collective-permute-start | bytes 98312 | tf_op jit(solution)/shard_map/ppermute | solution.py:236
  35.7 3.4 %collective-permute-start.6 = (f32[4,16,128]{2,1,0:T(8,128)S(1)}, f32[4,16,128]{2,1,0:T(8,128)S(1)}, u32[]{:S(2)}, u32[]{:S(2)}) collective-permute-start(f32[4,16,128]{2,1,0:T(8,128)S(1)} %get-tuple-element.30), channel_id=1, source_target_pairs={{0,3},{1,0},{2,1},{3,2},{4,7},{5,4},{6,5},{7,6},{8,11},{9,8},{10,9... | collective-permute-start | bytes 98312 | tf_op jit(solution)/shard_map/ppermute | solution.py:236
  37.5 4.6 %collective-permute-start.7 = (f32[4,16,128]{2,1,0:T(8,128)S(1)}, f32[4,16,128]{2,1,0:T(8,128)S(1)}, u32[]{:S(2)}, u32[]{:S(2)}) collective-permute-start(f32[4,16,128]{2,1,0:T(8,128)S(1)} %get-tuple-element.31), channel_id=1, source_target_pairs={{0,2},{1,3},{2,0},{3,1},{4,6},{5,7},{6,4},{7,5},{8,10},{9,11},{10,... | collective-permute-start | bytes 98312 | tf_op jit(solution)/shard_map/ppermute | solution.py:236

commit v8 on v7

--- a/solution.py
+++ b/solution.py
@@ -167,12 +167,12 @@
     marks = got[pl.ds(16, 64, stride=17), :].T
     pick = jnp.concatenate([marks[k * 16 : k * 16 + 16, :] for k in range(4)], axis=1).astype(BF16)
     pick = jnp.concatenate([pick, pick], axis=1)
-    sums = []
+    parts = []
     for j in range(4):
         value = jnp.concatenate([got[pl.ds(k * 4 + j, 64, stride=17), :] for k in range(4)], axis=0)
-        high, low = halves(value)
-        far = dot(pick, jnp.concatenate([high, low], axis=0))
-        sums.append(far + na[j] + nb[j] + nc[j] + nd[j])
+        parts.append(jnp.concatenate(halves(value), axis=0))
+    far = dot(pick, jnp.concatenate(parts, axis=1))
+    sums = [far[:, j * 128 : j * 128 + 128] + na[j] + nb[j] + nc[j] + nd[j] for j in range(4)]
     efie[...] = jnp.stack([sums[0], sums[1]], axis=1).astype(BF16)
     dual[...] = jnp.stack([sums[2], sums[3]], axis=1).astype(BF16)
 

time: 51.8 us -> 51.8 us (level)
  no operation moved by 1% of the time
where the time goes in v8:
time: 51.8 us; the launch traced here: 51.5 us
  starting transfers between devices  26.2 us (51%)
  waiting for transfers between devices  15 us (29%)
  Pallas kernels  9.15 us (18%)
  between operations  0.73 us (1%)
    all_to_all x1, starting transfers between devices, per_device(): lax.all_to_all(sent.reshape(count * 17, 1, 128), 'cluster', 0, 0, axis_in...  13.4 us
    all_to_all x1, waiting for transfers between devices, per_device(): lax.all_to_all(sent.reshape(count * 17, 1, 128), 'cluster', 0, 0, axis_in...  8.47 us
    ppermute x6, starting transfers between devices, over_sub(): lax.ppermute(parts[k], 'sub', shift(k))  8.08 us
    ppermute x6, waiting for transfers between devices, over_sub(): lax.ppermute(parts[k], 'sub', shift(k))  6.52 us
    ppermute x1, starting transfers between devices, per_device(): got_other = lax.ppermute(other, 'cluster', between)  4.61 us
    pallas_call x1, Pallas kernels, per_device(): pl.pallas_call(functools.partial(far_kernel, chunk), in_specs=[SMEM, SMEM...  3.56 us
    pallas_call x1, Pallas kernels, per_device(): pl.pallas_call(functools.partial(near_kernel, chunk), in_specs=[SMEM, SME...  3.44 us
    pallas_call x1, Pallas kernels, per_device(): pl.pallas_call(send_kernel, in_specs=[VMEM] * 6, out_specs=VMEM, out_shap...  1.09 us
  transfers between devices with their start and end apart: 9, of which 4 were waited for; matrix products, arithmetic and copies ran while one was open for 1% of the time, Pallas kernels for 7%

profile of v8, /device:TPU:1, one launch (start us, length us, event | category | flops | bytes accessed | tf_op | source)
XLA Modules:
  0.0 51.5 jit_solution(7493642904493239582)
XLA Ops:
  0.6 3.6 %far.1 = (f32[4,128,128]{2,1,0:T(8,128)S(1)}, f32[4,128,128]{2,1,0:T(8,128)S(1)}, f32[4,128,128]{2,1,0:T(8,128)S(1)}, f32[4,128,128]{2,1,0:T(8,128)S(1)}) custom-call(s32[1]{0:T(128)} %bitcast.me_ref, s32[8,16]{1,0:T(8,128)} %bitcast.24, bf16[128,128]{1,0:T(8,128)(2,1)} %bitcast.22, bf16[16,8,2,16,128]{4,3,2,1,0:T(8,128)(2,1)} %le.1, ...), custom_call_target="tpu_custom_call" | custom-call | flops 200000000 | bytes 5300000 | tf_op jit(solution)/shard_map/far/pallas_call | solution.py:220
  4.2 2.1 %collective-permute-start = (f32[4,128,128]{2,1,0:T(8,128)S(1)}, f32[4,128,128]{2,1,0:T(8,128)S(1)}, u32[]{:S(2)}, u32[]{:S(2)}) collective-permute-start(f32[4,128,128]{2,1,0:T(8,128)S(1)} %get-tuple-element.19), channel_id=1, source_target_pairs={{0,1},{1,2},{2,3},{3,0},{4,5},{5,6},{6,7},{7,4},{8,9},{9,10},{10,1... | collective-permute-start | bytes 786440 | tf_op jit(solution)/shard_map/ppermute | solution.py:236
  6.3 1.4 %collective-permute-start.1 = (f32[4,128,128]{2,1,0:T(8,128)S(1)}, f32[4,128,128]{2,1,0:T(8,128)S(1)}, u32[]{:S(2)}, u32[]{:S(2)}) collective-permute-start(f32[4,128,128]{2,1,0:T(8,128)S(1)} %get-tuple-element.20), channel_id=1, source_target_pairs={{0,3},{1,0},{2,1},{3,2},{4,7},{5,4},{6,5},{7,6},{8,11},{9,8},{10,9... | collective-permute-start | bytes 786440 | tf_op jit(solution)/shard_map/ppermute | solution.py:236
  7.7 1.6 %collective-permute-start.2 = (f32[4,128,128]{2,1,0:T(8,128)S(1)}, f32[4,128,128]{2,1,0:T(8,128)S(1)}, u32[]{:S(2)}, u32[]{:S(2)}) collective-permute-start(f32[4,128,128]{2,1,0:T(8,128)S(1)} %get-tuple-element.21), channel_id=1, source_target_pairs={{0,2},{1,3},{2,0},{3,1},{4,6},{5,7},{6,4},{7,5},{8,10},{9,11},{10,... | collective-permute-start | bytes 786440 | tf_op jit(solution)/shard_map/ppermute | solution.py:236
  9.3 3.4 %near.1 = (f32[16,2,8,128]{3,2,1,0:T(8,128)S(1)}, f32[16,2,8,128]{3,2,1,0:T(8,128)S(1)}, f32[16,2,8,128]{3,2,1,0:T(8,128)S(1)}) custom-call(s32[1]{0:T(128)} %bitcast.me_ref, s32[1]{0:T(128)} %bitcast.3.base_ref, s32[2,16]{1,0:T(2,128)} %bitcast.25, bf16[128,128]{1,0:T(8,128)(2,1)} %bitcast.23, bf16[16,2,2,128,128]{4,3,2,1,0:T(8,128)(2,1)} %de.1, ...), custom_call_target="tpu_custom_call" | custom-call | flops 200000000 | bytes 4600000 | tf_op jit(solution)/shard_map/near/pallas_call | solution.py:240
  12.8 4.6 %collective-permute-start.3 = (f32[16,2,8,128]{3,2,1,0:T(8,128)S(1)}, f32[16,2,8,128]{3,2,1,0:T(8,128)S(1)}, u32[]{:S(2)}, u32[]{:S(2)}) collective-permute-start(f32[16,2,8,128]{3,2,1,0:T(8,128)S(1)} %get-tuple-element.22), channel_id=1, source_target_pairs={{4,8},{12,16},{20,24},{28,32},{36,40},{44,48},{52,56},{60,64},{68,... | collective-permute-start | bytes 393224 | tf_op jit(solution)/shard_map/ppermute | solution.py:254
  17.4 0.1 collective-permute-start.4
  17.5 0.1 copy.25
  17.6 0.1 reshape.213
  17.7 0.2 convert_reduce_fusion
  17.9 0.0 collective-permute-done.1.c
  17.9 2.2 %collective-permute-done.2.d = f32[4,128,128]{2,1,0:T(8,128)S(1)} collective-permute-done((f32[4,128,128]{2,1,0:T(8,128)S(1)}, f32[4,128,128]{2,1,0:T(8,128)S(1)}, u32[]{:S(2)}, u32[]{:S(2)}) %collective-permute-start.2) | collective-permute-done | bytes 262176 | tf_op jit(solution)/shard_map/ppermute | solution.py:236
  20.1 0.1 broadcast_in_dim.5.cols_ref
  20.2 1.1 %send.1.refs_0_ = f32[1088,128]{1,0:T(8,128)} custom-call(s32[8,128]{1,0:T(8,128)S(1)} %broadcast_in_dim.4.slot_ref, s32[128,128]{1,0:T(8,128)S(1)} %broadcast_in_dim.5.cols_ref, f32[4,128,128]{2,1,0:T(8,128)S(1)} %get-tuple-element.18.a.after, f32[4,128,128]{2,1,0:T(8,128)S(1)} %collective-permute-done.b, f32[4,128,128]{2,1,0:T(8,128)S(1)} %collective-permute-done.1.c, ...), custom_call_target="tpu_custom_call" | custom-call | tf_op jit(solution)/shard_map/send/pallas_call | solution.py:263
  21.3 0.0 collective-permute-done.3.refs_1_
  21.3 13.4 %all-to-all-start = ((f32[1088,1,128]{2,1,0:T(1,128)}), f32[1088,1,128]{2,1,0:T(1,128)S(1)}, u32[]{:S(2)}, u32[]{:S(2)}) async-start(f32[1088,1,128]{2,1,0:T(1,128)} %bitcast.6), calls=%async_computation | async-start | bytes 1114112 | tf_op jit(solution)/shard_map/all_to_all | solution.py:290
  34.7 0.1 merge.1
  34.8 0.9 %collective-permute-start.5 = (f32[4,16,128]{2,1,0:T(8,128)S(1)}, f32[4,16,128]{2,1,0:T(8,128)S(1)}, u32[]{:S(2)}, u32[]{:S(2)}) collective-permute-start(f32[4,16,128]{2,1,0:T(8,128)S(1)} %get-tuple-element.29), channel_id=1, source_target_pairs={{0,1},{1,2},{2,3},{3,0},{4,5},{5,6},{6,7},{7,4},{8,9},{9,10},{10,1... | collective-permute-start | bytes 98312 | tf_op jit(solution)/shard_map/ppermute | solution.py:236
  35.7 1.8 %collective-permute-start.6 = (f32[4,16,128]{2,1,0:T(8,128)S(1)}, f32[4,16,128]{2,1,0:T(8,128)S(1)}, u32[]{:S(2)}, u32[]{:S(2)}) collective-permute-start(f32[4,16,128]{2,1,0:T(8,128)S(1)} %get-tuple-element.30), channel_id=1, source_target_pairs={{0,3},{1,0},{2,1},{3,2},{4,7},{5,4},{6,5},{7,6},{8,11},{9,8},{10,9... | collective-permute-start | bytes 98312 | tf_op jit(solution)/shard_map/ppermute | solution.py:236
  37.5 0.2 collective-permute-start.7
  37.8 1.4 %collective-permute-done.5.nb = f32[4,16,128]{2,1,0:T(8,128)S(1)} collective-permute-done((f32[4,16,128]{2,1,0:T(8,128)S(1)}, f32[4,16,128]{2,1,0:T(8,128)S(1)}, u32[]{:S(2)}, u32[]{:S(2)}) %collective-permute-start.5) | collective-permute-done | bytes 32800 | tf_op jit(solution)/shard_map/ppermute | solution.py:236
  39.1 3.0 %collective-permute-done.7.nd = f32[4,16,128]{2,1,0:T(8,128)S(1)} collective-permute-done((f32[4,16,128]{2,1,0:T(8,128)S(1)}, f32[4,16,128]{2,1,0:T(8,128)S(1)}, u32[]{:S(2)}, u32[]{:S(2)}) %collective-permute-start.7) | collective-permute-done | bytes 32800 | tf_op jit(solution)/shard_map/ppermute | solution.py:236
  42.1 8.5 %all-to-all-done = f32[1088,1,128]{2,1,0:T(1,128)S(1)} async-done(((f32[1088,1,128]{2,1,0:T(1,128)}), f32[1088,1,128]{2,1,0:T(1,128)S(1)}, u32[]{:S(2)}, u32[]{:S(2)}) %all-to-all-start) | async-done | bytes 557088 | tf_op jit(solution)/shard_map/all_to_all | solution.py:290
  50.6 0.9 %total.1 = (bf16[16,2,128]{2,1,0:T(2,128)(2,1)}, bf16[16,2,128]{2,1,0:T(2,128)(2,1)}) custom-call(f32[1088,128]{1,0:T(8,128)S(1)} %bitcast.18, f32[4,16,128]{2,1,0:T(8,128)S(1)} %get-tuple-element.28.na, f32[4,16,128]{2,1,0:T(8,128)S(1)} %collective-permute-done.5.nb, f32[4,16,128]{2,1,0:T(8,128)S(1)} %collective-permute-done.6.nc, ...), custom_call_target="tpu_custom_call" | custom-call | tf_op jit(solution)/shard_map/total/pallas_call | solution.py:291
  (9 shorter events, 0.1 us)
Async XLA Ops:
  4.2 13.7 %collective-permute-start = (f32[4,128,128]{2,1,0:T(8,128)S(1)}, f32[4,128,128]{2,1,0:T(8,128)S(1)}, u32[]{:S(2)}, u32[]{:S(2)}) collective-permute-start(f32[4,128,128]{2,1,0:T(8,128)S(1)} %get-tuple-element.19), channel_id=1, source_target_pairs={{0,1},{1,2},{2,3},{3,0},{4,5},{5,6},{6,7},{7,4},{8,9},{9,10},{10,1... | collective-permute-start | bytes 786440 | tf_op jit(solution)/shard_map/ppermute | solution.py:236
  6.3 11.6 %collective-permute-start.1 = (f32[4,128,128]{2,1,0:T(8,128)S(1)}, f32[4,128,128]{2,1,0:T(8,128)S(1)}, u32[]{:S(2)}, u32[]{:S(2)}) collective-permute-start(f32[4,128,128]{2,1,0:T(8,128)S(1)} %get-tuple-element.20), channel_id=1, source_target_pairs={{0,3},{1,0},{2,1},{3,2},{4,7},{5,4},{6,5},{7,6},{8,11},{9,8},{10,9... | collective-permute-start | bytes 786440 | tf_op jit(solution)/shard_map/ppermute | solution.py:236
  7.7 12.4 %collective-permute-start.2 = (f32[4,128,128]{2,1,0:T(8,128)S(1)}, f32[4,128,128]{2,1,0:T(8,128)S(1)}, u32[]{:S(2)}, u32[]{:S(2)}) collective-permute-start(f32[4,128,128]{2,1,0:T(8,128)S(1)} %get-tuple-element.21), channel_id=1, source_target_pairs={{0,2},{1,3},{2,0},{3,1},{4,6},{5,7},{6,4},{7,5},{8,10},{9,11},{10,... | collective-permute-start | bytes 786440 | tf_op jit(solution)/shard_map/ppermute | solution.py:236
  9.3 8.2 %copy-start = (s32[16,8]{0,1:T(8,128)S(1)}, s32[16,8]{0,1:T(8,128)}, u32[]{:S(2)}) copy-start(s32[16,8]{0,1:T(8,128)} %param.16) | copy-start | bytes 1540
  12.8 8.5 %collective-permute-start.3 = (f32[16,2,8,128]{3,2,1,0:T(8,128)S(1)}, f32[16,2,8,128]{3,2,1,0:T(8,128)S(1)}, u32[]{:S(2)}, u32[]{:S(2)}) collective-permute-start(f32[16,2,8,128]{3,2,1,0:T(8,128)S(1)} %get-tuple-element.22), channel_id=1, source_target_pairs={{4,8},{12,16},{20,24},{28,32},{36,40},{44,48},{52,56},{60,64},{68,... | collective-permute-start | bytes 393224 | tf_op jit(solution)/shard_map/ppermute | solution.py:254
  17.4 3.9 %collective-permute-start.4 = (f32[16,2,8,128]{3,2,1,0:T(8,128)S(1)}, f32[16,2,8,128]{3,2,1,0:T(8,128)S(1)}, u32[]{:S(2)}, u32[]{:S(2)}) collective-permute-start(f32[16,2,8,128]{3,2,1,0:T(8,128)S(1)} %get-tuple-element.23), channel_id=1, source_target_pairs={{0,4},{4,0},{8,12},{12,8},{16,20},{20,16},{24,28},{28,24},{32,36},... | collective-permute-start | bytes 393224 | tf_op jit(solution)/shard_map/ppermute | solution.py:255
  21.3 29.3 %all-to-all-start = ((f32[1088,1,128]{2,1,0:T(1,128)}), f32[1088,1,128]{2,1,0:T(1,128)S(1)}, u32[]{:S(2)}, u32[]{:S(2)}) async-start(f32[1088,1,128]{2,1,0:T(1,128)} %bitcast.6), calls=%async_computation | async-start | bytes 1114112 | tf_op jit(solution)/shard_map/all_to_all | solution.py:290
  34.8 4.3 %collective-permute-start.5 = (f32[4,16,128]{2,1,0:T(8,128)S(1)}, f32[4,16,128]{2,1,0:T(8,128)S(1)}, u32[]{:S(2)}, u32[]{:S(2)}) collective-permute-start(f32[4,16,128]{2,1,0:T(8,128)S(1)} %get-tuple-element.29), channel_id=1, source_target_pairs={{0,1},{1,2},{2,3},{3,0},{4,5},{5,6},{6,7},{7,4},{8,9},{9,10},{10,1... | collective-permute-start | bytes 98312 | tf_op jit(solution)/shard_map/ppermute | solution.py:236
  35.7 3.4 %collective-permute-start.6 = (f32[4,16,128]{2,1,0:T(8,128)S(1)}, f32[4,16,128]{2,1,0:T(8,128)S(1)}, u32[]{:S(2)}, u32[]{:S(2)}) collective-permute-start(f32[4,16,128]{2,1,0:T(8,128)S(1)} %get-tuple-element.30), channel_id=1, source_target_pairs={{0,3},{1,0},{2,1},{3,2},{4,7},{5,4},{6,5},{7,6},{8,11},{9,8},{10,9... | collective-permute-start | bytes 98312 | tf_op jit(solution)/shard_map/ppermute | solution.py:236
  37.5 4.6 %collective-permute-start.7 = (f32[4,16,128]{2,1,0:T(8,128)S(1)}, f32[4,16,128]{2,1,0:T(8,128)S(1)}, u32[]{:S(2)}, u32[]{:S(2)}) collective-permute-start(f32[4,16,128]{2,1,0:T(8,128)S(1)} %get-tuple-element.31), channel_id=1, source_target_pairs={{0,2},{1,3},{2,0},{3,1},{4,6},{5,7},{6,4},{7,5},{8,10},{9,11},{10,... | collective-permute-start | bytes 98312 | tf_op jit(solution)/shard_map/ppermute | solution.py:236
